TPU v7x, 32 devices: a whole 2x2x4 slice. The times are simulated.
32 devices in a mesh: dp: 8 (over y, x, core), tensor: 4 (over z).
Axes of the slice: x: 2, y: 2, z: 4, core: 2. Of those that a mesh axis runs over, the one named last changes fastest.
Arguments:
- tokens: bfloat16 [4096, 2048], P(('dp', 'tensor')), may hold values from -6 to 6
- seq_lengths: int32 [24], replicated, may hold values from 64 to 384, as said below
- seq_group: int32 [24], replicated, may hold values from 0 to 7, as said below
- attn_gain: bfloat16 [2048], P('dp'), may hold values from 0.099609375 to 1.8984375
- w_query: bfloat16 [2048, 2048], P('dp', 'tensor'), may hold values from -0.125 to 0.125
- w_key: bfloat16 [2048, 512], P('dp', 'tensor'), may hold values from -0.125 to 0.125
- w_value: bfloat16 [2048, 512], P('dp', 'tensor'), may hold values from -0.125 to 0.125
- w_out: bfloat16 [2048, 2048], P('tensor', 'dp'), may hold values from -1 to 1
- mlp_gain: bfloat16 [2048], P('dp'), may hold values from 0.099609375 to 1.8984375
- w_gate: bfloat16 [2048, 8192], P('dp', 'tensor'), may hold values from -0.125 to 0.125
- w_up: bfloat16 [2048, 8192], P('dp', 'tensor'), may hold values from -0.125 to 0.125
- w_down: bfloat16 [8192, 2048], P('tensor', 'dp'), may hold values from -0.125 to 0.125
- cotangent: bfloat16 [4096, 2048], P(('dp', 'tensor')), may hold values from -6 to 6
Outputs:
- block_out: bfloat16 [4096, 2048], P(('dp', 'tensor'))
- grad_tokens: bfloat16 [4096, 2048], P(('dp', 'tensor'))
- grad_attn_gain: float32 [2048], P('dp')
- grad_w_query: float32 [2048, 2048], P('dp', 'tensor')
- grad_w_key: float32 [2048, 512], P('dp', 'tensor')
- grad_w_value: float32 [2048, 512], P('dp', 'tensor')
- grad_w_out: float32 [2048, 2048], P('tensor', 'dp')
- grad_mlp_gain: float32 [2048], P('dp')
- grad_w_gate: float32 [2048, 8192], P('dp', 'tensor')
- grad_w_up: float32 [2048, 8192], P('dp', 'tensor')
- grad_w_down: float32 [8192, 2048], P('tensor', 'dp')
Inputs may be any that keep to these rules, and one draw needn't show every extreme that they name: `seq_group`: each data group gets exactly 3 sequences. `seq_lengths`: the sequences of one data group fill at most its 512 rows, in at least one group exactly; in every group one sequence starts within the group's first 128 rows and ends within its last 128 rows.
All inputs are finite; a program needn't handle non-finite values.
Results may differ from a plain program's by a relative error of at most 0.02.
Values may be sent and summed in bfloat16 or wider, within the bound.
No kernel may reach another device: no remote copies, remote signals or barrier semaphores. Data moves between devices by JAX's collectives and lax.ppermute only.
A program may use at most 128 MiB of HBM per device.

v0:
```python
import math

import jax
import jax.numpy as jnp
from jax import lax
from jax.sharding import PartitionSpec as P

HEAD_DIM = 64


EPSILON = 1e-05
ROPE_BASE = 500000.0


def rope_tables(position, width):
    half_width = width // 2
    steps_f = jnp.arange(half_width, dtype=jnp.float32)
    inverse = 1.0 / ROPE_BASE ** (steps_f * 2.0 / width)
    angles = position.astype(jnp.float32)[:, None] * inverse[None, :]
    return (jnp.cos(angles)[:, None, :], jnp.sin(angles)[:, None, :])


def rotate(values, cosine_table, sine_table):
    half_width = values.shape[-1] // 2
    first_half = values[..., :half_width]
    second_half = values[..., half_width:]
    return jnp.concatenate(
        [
            first_half * cosine_table - second_half * sine_table,
            second_half * cosine_table + first_half * sine_table,
        ],
        axis=-1,
    )


def rotate_back(values, cosine_table, sine_table):
    half_width = values.shape[-1] // 2
    first_half = values[..., :half_width]
    second_half = values[..., half_width:]
    return jnp.concatenate(
        [
            first_half * cosine_table + second_half * sine_table,
            second_half * cosine_table - first_half * sine_table,
        ],
        axis=-1,
    )


def layout(seq_lengths, seq_group, group_id, row_count):
    owned_mask = (seq_group == group_id).astype(jnp.int32)
    owned_len = seq_lengths * owned_mask
    seq_ends = jnp.cumsum(owned_len)
    row_index = jnp.arange(row_count, dtype=jnp.int32)
    finished = (seq_ends[None, :] <= row_index[:, None]).astype(jnp.int32)
    segment = jnp.sum(finished * owned_mask[None, :], axis=1)
    offsets = jnp.sum(finished * owned_len[None, :], axis=1)
    return (segment, row_index - offsets)


def inner(left, right):
    return lax.dot_general(
        left, right, (((0,), (0,)), ((), ())), preferred_element_type=jnp.float32
    )


def outer(left, right):
    return lax.dot_general(
        left, right, (((1,), (1,)), ((), ())), preferred_element_type=jnp.float32
    )


def norm_parts(values):
    factor = lax.rsqrt(jnp.mean(values * values, axis=-1, keepdims=True) + EPSILON)
    return (values * factor, factor)


def norm_back(grad_rows, gain, normed, factor):
    scaled = grad_rows * gain
    return factor * (scaled - normed * jnp.mean(scaled * normed, axis=-1, keepdims=True))


def block_scores(queries, keys_all, segment, block_start, block_rows, scale):
    query_block = lax.dynamic_slice_in_dim(queries, block_start, block_rows, 0)
    row_ids = block_start + jnp.arange(block_rows, dtype=jnp.int32)
    key_ids = jnp.arange(segment.shape[0], dtype=jnp.int32)
    seg_block = lax.dynamic_slice_in_dim(segment, block_start, block_rows, 0)
    allowed = (seg_block[:, None] == segment[None, :]) & (key_ids[None, :] <= row_ids[:, None])
    scores = (
        jnp.einsum("qcgd,kcd->cgqk", query_block, keys_all, preferred_element_type=jnp.float32)
        * scale
    )
    return (jnp.where(allowed, scores, -1e30), query_block)


def per_device(
    tokens,
    seq_lengths,
    seq_group,
    attn_gain,
    w_query,
    w_key,
    w_value,
    w_out,
    mlp_gain,
    w_gate,
    w_up,
    w_down,
    cotangent,
):
    query_w, key_w, value_w, out_w, attn_g = (
        lax.all_gather(w_query, "dp", axis=0, tiled=True),
        lax.all_gather(w_key, "dp", axis=0, tiled=True),
        lax.all_gather(w_value, "dp", axis=0, tiled=True),
        lax.all_gather(w_out, "dp", axis=1, tiled=True),
        lax.all_gather(attn_gain, "dp", axis=0, tiled=True),
    )
    tokens_f = tokens.astype(jnp.float32)
    normed_one, factor_one = norm_parts(tokens_f)
    gain_one = attn_g.astype(jnp.float32)
    attn_input = lax.all_gather(
        (normed_one * gain_one).astype(jnp.bfloat16), "tensor", axis=0, tiled=True
    )
    row_count = attn_input.shape[0]
    heads_here = query_w.shape[1] // HEAD_DIM
    kv_here = key_w.shape[1] // HEAD_DIM
    head_group = heads_here // kv_here
    scale = 1.0 / math.sqrt(HEAD_DIM)
    segment, position = layout(seq_lengths, seq_group, lax.axis_index("dp"), row_count)
    cosine_table, sine_table = rope_tables(position, HEAD_DIM)
    query_raw = jnp.dot(attn_input, query_w, preferred_element_type=jnp.float32).reshape(
        row_count, heads_here, HEAD_DIM
    )
    queries = (
        rotate(query_raw, cosine_table, sine_table)
        .astype(jnp.bfloat16)
        .reshape(row_count, kv_here, head_group, HEAD_DIM)
    )
    key_raw = jnp.dot(attn_input, key_w, preferred_element_type=jnp.float32).reshape(
        row_count, kv_here, HEAD_DIM
    )
    keys_all = rotate(key_raw, cosine_table, sine_table).astype(jnp.bfloat16)
    values_all = (
        jnp.dot(attn_input, value_w, preferred_element_type=jnp.float32)
        .astype(jnp.bfloat16)
        .reshape(row_count, kv_here, HEAD_DIM)
    )
    block_rows = min(512, row_count)
    block_total = row_count // block_rows

    def forward_block(block_id):
        block_start = block_id * block_rows
        scores = block_scores(queries, keys_all, segment, block_start, block_rows, scale)[0]
        row_max = jnp.max(scores, axis=-1, keepdims=True)
        exponent = jnp.exp(scores - row_max)
        row_sum = jnp.sum(exponent, axis=-1, keepdims=True)
        weights_low = (exponent / row_sum).astype(jnp.bfloat16)
        mixed = jnp.einsum(
            "cgqk,kcd->qcgd", weights_low, values_all, preferred_element_type=jnp.float32
        )
        return (
            mixed.reshape(block_rows, heads_here * HEAD_DIM).astype(jnp.bfloat16),
            (row_max + jnp.log(row_sum))[..., 0],
        )

    attended, log_mass = lax.map(forward_block, jnp.arange(block_total, dtype=jnp.int32))
    attended = attended.reshape(row_count, heads_here * HEAD_DIM)
    residual = tokens_f + lax.psum_scatter(
        jnp.dot(attended, out_w, preferred_element_type=jnp.float32),
        "tensor",
        scatter_dimension=0,
        tiled=True,
    )
    gate_w, up_w, down_w, mlp_g = (
        lax.all_gather(w_gate, "dp", axis=0, tiled=True),
        lax.all_gather(w_up, "dp", axis=0, tiled=True),
        lax.all_gather(w_down, "dp", axis=1, tiled=True),
        lax.all_gather(mlp_gain, "dp", axis=0, tiled=True),
    )
    normed_two, factor_two = norm_parts(residual)
    gain_two = mlp_g.astype(jnp.float32)
    mlp_input = lax.all_gather(
        (normed_two * gain_two).astype(jnp.bfloat16), "tensor", axis=0, tiled=True
    )
    gate = jnp.dot(mlp_input, gate_w, preferred_element_type=jnp.float32)
    up_proj = jnp.dot(mlp_input, up_w, preferred_element_type=jnp.float32)
    sigmoid_gate = jax.nn.sigmoid(gate)
    hidden = (gate * sigmoid_gate * up_proj).astype(jnp.bfloat16)
    block_out = (
        residual
        + lax.psum_scatter(
            jnp.dot(hidden, down_w, preferred_element_type=jnp.float32).astype(jnp.bfloat16),
            "tensor",
            scatter_dimension=0,
            tiled=True,
        ).astype(jnp.float32)
    ).astype(jnp.bfloat16)
    query_w, key_w, value_w, out_w, gate_w, up_w, down_w = (
        lax.all_gather(w_query, "dp", axis=0, tiled=True),
        lax.all_gather(w_key, "dp", axis=0, tiled=True),
        lax.all_gather(w_value, "dp", axis=0, tiled=True),
        lax.all_gather(w_out, "dp", axis=1, tiled=True),
        lax.all_gather(w_gate, "dp", axis=0, tiled=True),
        lax.all_gather(w_up, "dp", axis=0, tiled=True),
        lax.all_gather(w_down, "dp", axis=1, tiled=True),
    )
    incoming = lax.all_gather(cotangent, "tensor", axis=0, tiled=True)
    grad_down = inner(hidden, incoming)
    grad_hidden = outer(incoming, down_w)
    silu_slope = sigmoid_gate * (1.0 + gate * (1.0 - sigmoid_gate))
    grad_gate = (grad_hidden * up_proj * silu_slope).astype(jnp.bfloat16)
    grad_up = (grad_hidden * gate * sigmoid_gate).astype(jnp.bfloat16)
    grad_gate_w = inner(mlp_input, grad_gate)
    grad_up_w = inner(mlp_input, grad_up)
    grad_two = lax.psum_scatter(
        outer(grad_gate, gate_w) + outer(grad_up, up_w), "tensor", scatter_dimension=0, tiled=True
    )
    gain_two_part = jnp.sum(grad_two * normed_two, axis=0)
    grad_residual = cotangent.astype(jnp.float32) + norm_back(
        grad_two, gain_two, normed_two, factor_two
    )
    grad_attn_rows = lax.all_gather(
        grad_residual.astype(jnp.bfloat16), "tensor", axis=0, tiled=True
    )
    grad_out_w = inner(attended, grad_attn_rows)
    grad_attended = (
        outer(grad_attn_rows, out_w)
        .astype(jnp.bfloat16)
        .reshape(row_count, kv_here, head_group, HEAD_DIM)
    )

    def backward_block(carry, operands):
        key_acc, value_acc = carry
        block_id, lse_block = operands
        block_start = block_id * block_rows
        scores, query_block = block_scores(
            queries, keys_all, segment, block_start, block_rows, scale
        )
        probs = jnp.exp(scores - lse_block[..., None])
        weights_low = probs.astype(jnp.bfloat16)
        grad_block = lax.dynamic_slice_in_dim(grad_attended, block_start, block_rows, 0)
        grad_probs = jnp.einsum(
            "qcgd,kcd->cgqk", grad_block, values_all, preferred_element_type=jnp.float32
        )
        delta = jnp.sum(probs * grad_probs, axis=-1, keepdims=True)
        grad_scores = (probs * (grad_probs - delta)).astype(jnp.bfloat16)
        grad_query = (
            jnp.einsum("cgqk,kcd->qcgd", grad_scores, keys_all, preferred_element_type=jnp.float32)
            * scale
        )
        key_acc = (
            key_acc
            + jnp.einsum(
                "cgqk,qcgd->kcd", grad_scores, query_block, preferred_element_type=jnp.float32
            )
            * scale
        )
        value_acc = value_acc + jnp.einsum(
            "cgqk,qcgd->kcd", weights_low, grad_block, preferred_element_type=jnp.float32
        )
        return ((key_acc, value_acc), grad_query)

    zero_kv = jnp.zeros((row_count, kv_here, HEAD_DIM), jnp.float32)
    (grad_keys, grad_values), grad_queries = lax.scan(
        backward_block, (zero_kv, zero_kv), (jnp.arange(block_total, dtype=jnp.int32), log_mass)
    )
    grad_queries = (
        rotate_back(grad_queries.reshape(row_count, heads_here, HEAD_DIM), cosine_table, sine_table)
        .astype(jnp.bfloat16)
        .reshape(row_count, heads_here * HEAD_DIM)
    )
    grad_keys = (
        rotate_back(grad_keys, cosine_table, sine_table)
        .astype(jnp.bfloat16)
        .reshape(row_count, kv_here * HEAD_DIM)
    )
    grad_values = grad_values.astype(jnp.bfloat16).reshape(row_count, kv_here * HEAD_DIM)
    grad_query_w = inner(attn_input, grad_queries)
    grad_key_w = inner(attn_input, grad_keys)
    grad_value_w = inner(attn_input, grad_values)
    grad_one = lax.psum_scatter(
        (
            outer(grad_queries, query_w) + outer(grad_keys, key_w) + outer(grad_values, value_w)
        ).astype(jnp.bfloat16),
        "tensor",
        scatter_dimension=0,
        tiled=True,
    ).astype(jnp.float32)
    gain_one_part = jnp.sum(grad_one * normed_one, axis=0)
    grad_tokens = (grad_residual + norm_back(grad_one, gain_one, normed_one, factor_one)).astype(
        jnp.bfloat16
    )
    gain_sums = lax.psum((gain_one_part, gain_two_part), "tensor")
    results = (
        lax.psum_scatter(
            gain_sums[0].astype(jnp.bfloat16), "dp", scatter_dimension=0, tiled=True
        ).astype(jnp.float32),
        lax.psum_scatter(
            grad_query_w.astype(jnp.bfloat16), "dp", scatter_dimension=0, tiled=True
        ).astype(jnp.float32),
        lax.psum_scatter(
            grad_key_w.astype(jnp.bfloat16), "dp", scatter_dimension=0, tiled=True
        ).astype(jnp.float32),
        lax.psum_scatter(
            grad_value_w.astype(jnp.bfloat16), "dp", scatter_dimension=0, tiled=True
        ).astype(jnp.float32),
        lax.psum_scatter(
            grad_out_w.astype(jnp.bfloat16), "dp", scatter_dimension=1, tiled=True
        ).astype(jnp.float32),
        lax.psum_scatter(
            gain_sums[1].astype(jnp.bfloat16), "dp", scatter_dimension=0, tiled=True
        ).astype(jnp.float32),
        lax.psum_scatter(
            grad_gate_w.astype(jnp.bfloat16), "dp", scatter_dimension=0, tiled=True
        ).astype(jnp.float32),
        lax.psum_scatter(
            grad_up_w.astype(jnp.bfloat16), "dp", scatter_dimension=0, tiled=True
        ).astype(jnp.float32),
        lax.psum_scatter(
            grad_down.astype(jnp.bfloat16), "dp", scatter_dimension=1, tiled=True
        ).astype(jnp.float32),
    )
    return (
        block_out,
        grad_tokens,
        results[0],
        results[1],
        results[2],
        results[3],
        results[4],
        results[5],
        results[6],
        results[7],
        results[8],
    )


def solution(mesh):
    return jax.shard_map(
        per_device,
        mesh=mesh,
        in_specs=(
            P(("dp", "tensor"), None),
            P(),
            P(),
            P("dp"),
            P("dp", "tensor"),
            P("dp", "tensor"),
            P("dp", "tensor"),
            P("tensor", "dp"),
            P("dp"),
            P("dp", "tensor"),
            P("dp", "tensor"),
            P("tensor", "dp"),
            P(("dp", "tensor"), None),
        ),
        out_specs=(
            P(("dp", "tensor"), None),
            P(("dp", "tensor"), None),
            P("dp"),
            P("dp", "tensor"),
            P("dp", "tensor"),
            P("dp", "tensor"),
            P("tensor", "dp"),
            P("dp"),
            P("dp", "tensor"),
            P("dp", "tensor"),
            P("tensor", "dp"),
        ),
        check_vma=False,
    )
```

profile of v0, /device:TPU:0, one launch (start us, length us, event | category | flops | bytes accessed | tf_op | source)
XLA Modules:
  0.0 1131.3 jit_solution(18338162891160590768)
XLA Ops:
  7.9 10.3 all-gather
  45.0 22.9 %all-gather.12.cloned.1.call-done = bf16[512,2048]{1,0:T(8,128)(2,1)} async-done(((bf16[128,2048]{1,0:T(8,128)(2,1)}), bf16[512,2048]{1,0:T(8,128)(2,1)}) %all-gather.12.cloned.1.call-update) | async-done | bytes 2097168 | tf_op jit(solution)/shard_map/all_gather | solution.py:120
  74.3 22.2 %all-gather.14.cloned.1.call-done = bf16[2048,512]{1,0:T(8,128)(2,1)} async-done(((bf16[256,512]{1,0:T(8,128)(2,1)}), bf16[2048,512]{1,0:T(8,128)(2,1)}) %all-gather.14.cloned.1.call-update) | async-done | bytes 2097168 | tf_op jit(solution)/shard_map/all_gather | solution.py:111
  106.1 20.5 %all-gather.16.cloned.1.call-done = bf16[512,2048]{1,0:T(8,128)(2,1)} async-done(((bf16[512,256]{1,0:T(8,128)(2,1)}), bf16[512,2048]{1,0:T(8,128)(2,1)}) %all-gather.16.cloned.1.call-update) | async-done | bytes 2097168 | tf_op jit(solution)/shard_map/all_gather | solution.py:114
  141.1 67.4 %reduce-scatter.12.cloned.1.call-done = f32[128,2048]{1,0:T(8,128)} async-done(((f32[512,2048]{1,0:T(8,128)}), f32[128,2048]{1,0:T(8,128)}) %reduce-scatter.12.cloned.1.call-update) | async-done | bytes 1048592 | tf_op jit(solution)/shard_map/reduce_scatter | solution.py:167
  213.7 51.6 %all-gather.20.cloned.1.call-done = bf16[2048,2048]{1,0:T(8,128)(2,1)} async-done(((bf16[256,2048]{1,0:T(8,128)(2,1)}), bf16[2048,2048]{1,0:T(8,128)(2,1)}) %all-gather.20.cloned.1.call-update) | async-done | bytes 8388624 | tf_op jit(solution)/shard_map/all_gather | solution.py:174
  265.3 48.0 %all-gather.18.cloned.1.call-done = bf16[512,2048]{1,0:T(8,128)(2,1)} async-done(((bf16[128,2048]{1,0:T(8,128)(2,1)}), bf16[512,2048]{1,0:T(8,128)(2,1)}) %all-gather.18.cloned.1.call-update) | async-done | bytes 2097168 | tf_op jit(solution)/shard_map/all_gather | solution.py:181
  313.4 10.6 fusion.39
  323.9 44.6 %all-gather.22.cloned.1.call-done = bf16[2048,2048]{1,0:T(8,128)(2,1)} async-done(((bf16[256,2048]{1,0:T(8,128)(2,1)}), bf16[2048,2048]{1,0:T(8,128)(2,1)}) %all-gather.22.cloned.1.call-update) | async-done | bytes 8388624 | tf_op jit(solution)/shard_map/all_gather | solution.py:175
  368.5 10.5 fusion.40
  379.0 37.1 %all-gather.26.cloned.1.call-done = bf16[512,2048]{1,0:T(8,128)(2,1)} async-done(((bf16[128,2048]{1,0:T(8,128)(2,1)}), bf16[512,2048]{1,0:T(8,128)(2,1)}) %all-gather.26.cloned.1.call-update) | async-done | bytes 2097168 | tf_op jit(solution)/shard_map/all_gather | solution.py:206
  416.2 56.7 %all-gather.24.cloned.1.call-done = bf16[2048,2048]{1,0:T(8,128)(2,1)} async-done(((bf16[2048,256]{1,0:T(8,128)(2,1)}), bf16[2048,2048]{1,0:T(8,128)(2,1)}) %all-gather.24.cloned.1.call-update) | async-done | bytes 8388624 | tf_op jit(solution)/shard_map/all_gather | solution.py:176
  472.9 11.8 %multiply_convert_fusion = (bf16[512,2048]{1,0:T(8,128)(2,1)S(1)}, bf16[512,2048]{1,0:T(8,128)(2,1)S(1)}, bf16[512,2048]{1,0:T(8,128)(2,1)}) fusion(f32[512,2048]{1,0:T(8,128)} %fusion.39, f32[512,2048]{1,0:T(8,128)} %fusion.40, bf16[512,2048]{1,0:T(8,128)(2,1)} %all-gather.26.cloned.1.call-done, bf16[2048,2048]{1,0:T(8,128)(2,1)} %all-gather.24.cloned.1.call-done), kind=kOutput, calls=%fused_computation.17 | convolution fusion | flops 4311744512 | bytes 25165824 | tf_op jit(solution)/shard_map/dot_general | solution.py:67
  499.6 76.9 %reduce-scatter.16.cloned.1.call-done = f32[128,2048]{1,0:T(8,128)} async-done(((f32[512,2048]{1,0:T(8,128)}), f32[128,2048]{1,0:T(8,128)}) %reduce-scatter.16.cloned.1.call-update) | async-done | bytes 1048592 | tf_op jit(solution)/shard_map/reduce_scatter | solution.py:214
  582.5 45.8 %all-gather.28.cloned.1.call-done = bf16[512,2048]{1,0:T(8,128)(2,1)} async-done(((bf16[128,2048]{1,0:T(8,128)(2,1)}), bf16[512,2048]{1,0:T(8,128)(2,1)}) %all-gather.28.cloned.1.call-update) | async-done | bytes 2097168 | tf_op jit(solution)/shard_map/all_gather | solution.py:221
  717.5 73.1 %reduce-scatter.28.cloned.1.call-done = bf16[256,2048]{1,0:T(8,128)(2,1)} async-done(((bf16[2048,2048]{1,0:T(8,128)(2,1)}), bf16[256,2048]{1,0:T(8,128)(2,1)}) %reduce-scatter.28.cloned.1.call-update) | async-done | bytes 1048592 | tf_op jit(solution)/shard_map/reduce_scatter | solution.py:312
  793.5 72.2 %reduce-scatter.30.cloned.1.call-done = bf16[256,2048]{1,0:T(8,128)(2,1)} async-done(((bf16[2048,2048]{1,0:T(8,128)(2,1)}), bf16[256,2048]{1,0:T(8,128)(2,1)}) %reduce-scatter.30.cloned.1.call-update) | async-done | bytes 1048592 | tf_op jit(solution)/shard_map/reduce_scatter | solution.py:315
  868.4 71.8 %reduce-scatter.32.cloned.1.call-done = bf16[2048,256]{1,0:T(8,128)(2,1)} async-done(((bf16[2048,2048]{1,0:T(8,128)(2,1)}), bf16[2048,256]{1,0:T(8,128)(2,1)}) %reduce-scatter.32.cloned.1.call-update) | async-done | bytes 1048592 | tf_op jit(solution)/shard_map/reduce_scatter | solution.py:318
  942.9 42.0 %reduce-scatter.20.cloned.1.call-done = bf16[256,512]{1,0:T(8,128)(2,1)} async-done(((bf16[2048,512]{1,0:T(8,128)(2,1)}), bf16[256,512]{1,0:T(8,128)(2,1)}) %reduce-scatter.20.cloned.1.call-update) | async-done | bytes 262160 | tf_op jit(solution)/shard_map/reduce_scatter | solution.py:297
  986.8 42.6 %reduce-scatter.26.cloned.1.call-done = bf16[512,256]{1,0:T(8,128)(2,1)} async-done(((bf16[512,2048]{1,0:T(8,128)(2,1)}), bf16[512,256]{1,0:T(8,128)(2,1)}) %reduce-scatter.26.cloned.1.call-update) | async-done | bytes 262160 | tf_op jit(solution)/shard_map/reduce_scatter | solution.py:306
  1031.2 44.5 %reduce-scatter.18.cloned.1.call-done = bf16[128,2048]{1,0:T(8,128)(2,1)} async-done(((bf16[512,2048]{1,0:T(8,128)(2,1)}), bf16[128,2048]{1,0:T(8,128)(2,1)}) %reduce-scatter.18.cloned.1.call-update) | async-done | bytes 524304 | tf_op jit(solution)/shard_map/reduce_scatter | solution.py:280
  1077.1 17.4 %all-reduce.2 = (bf16[2048]{0:T(1024)(128)(2,1)S(1)}, bf16[2048]{0:T(1024)(128)(2,1)S(1)}) all-reduce(f32[2048]{0:T(1024)S(1)} %get-tuple-element.54, f32[2048]{0:T(1024)S(1)} %copy-done.28), channel_id=1, replica_groups=mesh['dp'=8,'tensor'=4] {'tensor'}, use_global_device_ids=true, to_apply=%region_15.16 | all-reduce | flops 4096 | bytes 24576 | tf_op jit(solution)/shard_map/psum | solution.py:292
  1094.5 12.2 %all-reduce.3 = (bf16[2048]{0:T(1024)(128)(2,1)S(1)}, bf16[2048]{0:T(1024)(128)(2,1)S(1)}) all-reduce(bf16[2048]{0:T(1024)(128)(2,1)S(1)} %get-tuple-element.68, bf16[2048]{0:T(1024)(128)(2,1)S(1)} %get-tuple-element.69), channel_id=6, replica_groups=mesh['dp'=8,'tensor'=4] {'dp'}, use_global_device_ids=true, to_apply=%region_16.17.clone | all-reduce | flops 4096 | bytes 16384
  1107.4 13.9 %reduce-scatter.14.cloned.1.call-done = bf16[128,2048]{1,0:T(8,128)(2,1)} async-done(((bf16[512,2048]{1,0:T(8,128)(2,1)}), bf16[128,2048]{1,0:T(8,128)(2,1)}) %reduce-scatter.14.cloned.1.call-update) | async-done | bytes 524304 | tf_op jit(solution)/shard_map/reduce_scatter | solution.py:190
  (198 shorter events, 188.6 us)
Async XLA Ops:
  7.2 60.8 %all-gather.12.cloned.1.call-start = ((), (), s32[]{:S(2)}) async-start(), calls=%async_computation.11 | async-start | bytes 2621440 | tf_op jit(solution)/shard_map/all_gather | solution.py:120
  21.5 74.9 %all-gather.14.cloned.1.call-start = ((), (), s32[]{:S(2)}) async-start(), calls=%async_computation.12 | async-start | bytes 2359296 | tf_op jit(solution)/shard_map/all_gather | solution.py:111
  22.3 104.3 %all-gather.16.cloned.1.call-start = ((), (), s32[]{:S(2)}) async-start(), calls=%async_computation.13 | async-start | bytes 2359296 | tf_op jit(solution)/shard_map/all_gather | solution.py:114
  23.0 185.5 %reduce-scatter.12.cloned.1.call-start = ((), (), s32[]{:S(2)}) async-start(), calls=%async_computation.14 | async-start | bytes 5242880 | tf_op jit(solution)/shard_map/reduce_scatter | solution.py:167
  131.6 133.7 %all-gather.20.cloned.1.call-start = ((), (), s32[]{:S(2)}) async-start(), calls=%async_computation.16 | async-start | bytes 9437184 | tf_op jit(solution)/shard_map/all_gather | solution.py:174
  132.2 181.2 %all-gather.18.cloned.1.call-start = ((), (), s32[]{:S(2)}) async-start(), calls=%async_computation.15 | async-start | bytes 2621440 | tf_op jit(solution)/shard_map/all_gather | solution.py:181
  141.1 437.5 %copy-start.22 = (f32[8,1,256]{2,1,0:T(1,128)}, f32[8,1,256]{2,1,0:T(1,128)S(1)}, u32[]{:S(2)}) copy-start(f32[8,1,256]{2,1,0:T(1,128)S(1)} %convert_element_type.209) | copy-start | bytes 24580
  210.1 368.5 %copy-start.29 = (f32[128]{0:T(128)}, f32[128]{0:T(128)S(1)}, u32[]{:S(2)}) copy-start(f32[128]{0:T(128)S(1)} %add_rsqrt_fusion) | copy-start | bytes 1540
  211.1 157.5 %all-gather.22.cloned.1.call-start = ((), (), s32[]{:S(2)}) async-start(), calls=%async_computation.17 | async-start | bytes 9437184 | tf_op jit(solution)/shard_map/all_gather | solution.py:175
  211.8 204.3 %all-gather.26.cloned.1.call-start = ((), (), s32[]{:S(2)}) async-start(), calls=%async_computation.20 | async-start | bytes 2621440 | tf_op jit(solution)/shard_map/all_gather | solution.py:206
  212.6 260.3 %all-gather.24.cloned.1.call-start = ((), (), s32[]{:S(2)}) async-start(), calls=%async_computation.18 | async-start | bytes 9437184 | tf_op jit(solution)/shard_map/all_gather | solution.py:176
  213.3 363.1 %reduce-scatter.16.cloned.1.call-start = ((), (), s32[]{:S(2)}) async-start(), calls=%async_computation.21 | async-start | bytes 5242880 | tf_op jit(solution)/shard_map/reduce_scatter | solution.py:214
  499.5 128.7 %all-gather.28.cloned.1.call-start = ((), (), s32[]{:S(2)}) async-start(), calls=%async_computation.22 | async-start | bytes 2621440 | tf_op jit(solution)/shard_map/all_gather | solution.py:221
  581.7 129.3 %reduce-scatter.22.cloned.1.call-start = ((), (), s32[]{:S(2)}) async-start(), calls=%async_computation.25 | async-start | bytes 589824 | tf_op jit(solution)/shard_map/reduce_scatter | solution.py:300
  645.4 70.6 %reduce-scatter.24.cloned.1.call-start = ((), (), s32[]{:S(2)}) async-start(), calls=%async_computation.26 | async-start | bytes 589824 | tf_op jit(solution)/shard_map/reduce_scatter | solution.py:303
  652.1 138.5 %reduce-scatter.28.cloned.1.call-start = ((), (), s32[]{:S(2)}) async-start(), calls=%async_computation.28 | async-start | bytes 9437184 | tf_op jit(solution)/shard_map/reduce_scatter | solution.py:312
  662.2 203.4 %reduce-scatter.30.cloned.1.call-start = ((), (), s32[]{:S(2)}) async-start(), calls=%async_computation.29 | async-start | bytes 9437184 | tf_op jit(solution)/shard_map/reduce_scatter | solution.py:315
  672.6 267.6 %reduce-scatter.32.cloned.1.call-start = ((), (), s32[]{:S(2)}) async-start(), calls=%async_computation.30 | async-start | bytes 9437184 | tf_op jit(solution)/shard_map/reduce_scatter | solution.py:318
  682.8 302.2 %reduce-scatter.20.cloned.1.call-start = ((), (), s32[]{:S(2)}) async-start(), calls=%async_computation.24 | async-start | bytes 2359296 | tf_op jit(solution)/shard_map/reduce_scatter | solution.py:297
  689.7 339.7 %reduce-scatter.26.cloned.1.call-start = ((), (), s32[]{:S(2)}) async-start(), calls=%async_computation.27 | async-start | bytes 2359296 | tf_op jit(solution)/shard_map/reduce_scatter | solution.py:306
  694.4 381.2 %reduce-scatter.18.cloned.1.call-start = ((), (), s32[]{:S(2)}) async-start(), calls=%async_computation.23 | async-start | bytes 2621440 | tf_op jit(solution)/shard_map/reduce_scatter | solution.py:280
  699.7 421.6 %reduce-scatter.14.cloned.1.call-start = ((), (), s32[]{:S(2)}) async-start(), calls=%async_computation.19 | async-start | bytes 2621440 | tf_op jit(solution)/shard_map/reduce_scatter | solution.py:190
  793.4 327.9 %copy-start.4 = (f32[128,2048]{1,0:T(8,128)S(1)}, f32[128,2048]{1,0:T(8,128)}, u32[]{:S(2)}) copy-start(f32[128,2048]{1,0:T(8,128)} %reduce-scatter.16.cloned.1.call-done) | copy-start | bytes 3145732
  793.4 327.9 %copy-start.5 = (bf16[128,2048]{1,0:T(8,128)(2,1)S(1)}, bf16[128,2048]{1,0:T(8,128)(2,1)}, u32[]{:S(2)}) copy-start(bf16[128,2048]{1,0:T(8,128)(2,1)} %param.25) | copy-start | bytes 1572868
  (38 other events, 2397.0 us)
Sparse Core Ops, SparseCore 0:
  21.7 46.2 all-gather.11
  69.8 26.5 all-gather.13
  98.3 28.2 all-gather.15
  131.7 76.7 reduce-scatter.11
  210.4 54.8 all-gather.19
  267.4 45.9 all-gather.17
  315.4 53.0 all-gather.21
  370.2 45.9 all-gather.25
  418.2 54.6 all-gather.23
  499.6 76.7 reduce-scatter.15
  581.8 46.4 all-gather.27
  645.6 32.8 reduce-scatter.21
  681.8 34.1 reduce-scatter.23
  719.3 71.2 reduce-scatter.27
  794.3 71.2 reduce-scatter.29
  868.9 71.2 reduce-scatter.31
  943.7 41.2 reduce-scatter.19
  988.1 41.2 reduce-scatter.25
  1031.8 43.8 reduce-scatter.17
  1077.8 43.4 reduce-scatter.13
where the time goes:
time: 1140 us; the launch traced here: 1130 us
  waiting for transfers between devices  862 us (76%)
  matrix products  137 us (12%)
  blocking collectives  67.8 us (6%)
  other arithmetic  38.6 us (3%)
  between operations  16 us (1%)
    reduce_scatter x1, waiting for transfers between devices, per_device(): lax.psum_scatter(outer(grad_gate, gate_w) + outer(grad_up, up_w), 'tensor...  76.9 us
    reduce_scatter x1, waiting for transfers between devices, per_device(): lax.psum_scatter(grad_gate_w.astype(jnp.bfloat16), 'dp', scatter_dimensio...  73.1 us
    reduce_scatter x1, waiting for transfers between devices, per_device(): lax.psum_scatter(grad_up_w.astype(jnp.bfloat16), 'dp', scatter_dimension=...  72.2 us
    reduce_scatter x1, waiting for transfers between devices, per_device(): lax.psum_scatter(grad_down.astype(jnp.bfloat16), 'dp', scatter_dimension=...  71.8 us
    reduce_scatter x1, waiting for transfers between devices, per_device(): lax.psum_scatter(jnp.dot(attended, out_w, preferred_element_type=jnp.floa...  67.4 us
    all_gather x1, waiting for transfers between devices, per_device(): lax.all_gather(w_down, 'dp', axis=1, tiled=True)  56.7 us
    all_gather x1, waiting for transfers between devices, per_device(): lax.all_gather(w_gate, 'dp', axis=0, tiled=True)  51.6 us
    all_gather x1, waiting for transfers between devices, per_device(): lax.all_gather((normed_two * gain_two).astype(jnp.bfloat16), 'tensor', ax...  48 us
  transfers between devices with their start and end apart: 20, of which 19 were waited for; matrix products, arithmetic and copies ran while one was open for 11% of the time, Pallas kernels for 0%

commit v1 on v0

v1 whole, which is shorter than its diff:
```python
import functools
import math

import jax
import jax.numpy as jnp
from jax import lax
from jax.sharding import PartitionSpec as P

HEAD_DIM = 64
EPSILON = 1e-05
ROPE_BASE = 500000.0
F32 = jnp.float32
BF16 = jnp.bfloat16


def rope_tables(position, width):
    half_width = width // 2
    steps_f = jnp.arange(half_width, dtype=F32)
    inverse = 1.0 / ROPE_BASE ** (steps_f * 2.0 / width)
    angles = position.astype(F32)[:, None] * inverse[None, :]
    return (jnp.cos(angles)[:, None, :], jnp.sin(angles)[:, None, :])


def rotate(values, cosine_table, sine_table):
    half_width = values.shape[-1] // 2
    first_half = values[..., :half_width]
    second_half = values[..., half_width:]
    return jnp.concatenate(
        [
            first_half * cosine_table - second_half * sine_table,
            second_half * cosine_table + first_half * sine_table,
        ],
        axis=-1,
    )


def layout(seq_lengths, seq_group, group_id, place):
    owned_mask = (seq_group == group_id).astype(jnp.int32)
    owned_len = seq_lengths * owned_mask
    seq_ends = jnp.cumsum(owned_len)
    finished = (seq_ends[None, :] <= place[:, None]).astype(jnp.int32)
    segment = jnp.sum(finished * owned_mask[None, :], axis=1)
    offsets = jnp.sum(finished * owned_len[None, :], axis=1)
    return (segment, place - offsets)


def mm(left, right):
    return jnp.dot(left, right, preferred_element_type=F32)


def inner(left, right):
    return lax.dot_general(left, right, (((0,), (0,)), ((), ())), preferred_element_type=F32)


def outer(left, right):
    return lax.dot_general(left, right, (((1,), (1,)), ((), ())), preferred_element_type=F32)


def norm_parts(values):
    factor = lax.rsqrt(jnp.mean(values * values, axis=-1, keepdims=True) + EPSILON)
    return (values * factor, factor)


def norm_back(grad_rows, gain, normed, factor):
    scaled = grad_rows * gain
    return factor * (scaled - normed * jnp.mean(scaled * normed, axis=-1, keepdims=True))


def after(value, *deps):
    return lax.optimization_barrier((value,) + deps)[0]


def add16(*terms):
    return functools.reduce(lambda a, b: a + b, [t.astype(F32) for t in terms]).astype(BF16)


class Line:
    def __init__(self, size):
        self.size = size
        self.index = lax.axis_index("tensor")

    def gather(self, v):
        size = self.size
        left, right = {}, {}
        to_right = to_left = v
        for s in range(1, size):
            to_right = lax.ppermute(to_right, "tensor", [(i, i + 1) for i in range(s - 1, size - 1)])
            to_left = lax.ppermute(to_left, "tensor", [(i, i - 1) for i in range(1, size - s + 1)])
            left[s], right[s] = to_right, to_left
        blocks = [v] + [jnp.where(self.index >= r, left[r], right[size - r]) for r in range(1, size)]
        return jnp.concatenate(blocks, axis=0)

    def scatter(self, parts):
        size = self.size
        from_left = from_right = None
        for s in range(1, size):
            to_right = parts[s] if from_left is None else add16(parts[s], from_left)
            to_left = parts[size - s] if from_right is None else add16(parts[size - s], from_right)
            from_left = lax.ppermute(to_right, "tensor", [(i, i + 1) for i in range(0, s)])
            from_right = lax.ppermute(to_left, "tensor", [(i, i - 1) for i in range(size - s, size)])
        return parts[0].astype(F32) + from_left.astype(F32) + from_right.astype(F32)

    def total(self, v):
        out = v
        for r in range(1, self.size):
            out = out + lax.ppermute(v, "tensor", [(i, (i + r) % self.size) for i in range(self.size)])
        return out


class Cube:
    def __init__(self, size):
        self.size = size
        self.me = lax.axis_index("dp")
        self.bits = [1 << b for b in range(1, size.bit_length() - 1)]
        self.keys = [2 * q for q in range(size // 2)] + [2 * q + 1 for q in range(size // 2)]

    def swap(self, v, m):
        return lax.ppermute(v, "dp", [(i, i ^ m) for i in range(self.size)])

    def gather(self, v, order):
        pieces = {0: v}
        for m in order + [1]:
            pieces.update({k ^ m: self.swap(p, m) for k, p in list(pieces.items())})
        return [pieces[k] for k in self.keys]

    def reduce(self, own, other, axis, order):
        received = self.swap(other, 1)
        width = own.shape[axis] // (self.size // 2)
        pieces = {}
        for q in range(self.size // 2):
            cut = [lax.slice_in_dim(a, q * width, (q + 1) * width, axis=axis) for a in (own, received)]
            pieces[2 * q] = add16(*cut)
        for m in order:
            gone = [k for k in pieces if k & m]
            arrived = {k ^ m: self.swap(pieces.pop(k), m) for k in gone}
            for k, p in arrived.items():
                pieces[k] = (pieces[k].astype(F32) + p.astype(F32)) if m == order[-1] else add16(pieces[k], p)
        return pieces[0]

    def reduce_small(self, v):
        out = v[0]
        for pos, k in enumerate(self.keys):
            if k:
                out = out + self.swap(v[pos], k)
        return out

    def columns_in(self, v):
        width = v.shape[1] // self.size
        return jnp.concatenate(
            [lax.dynamic_slice_in_dim(v, (self.me ^ k) * width, width, 1) for k in self.keys], axis=1
        )

    def columns_out(self, v):
        width = v.shape[1] // self.size
        high = self.size.bit_length() - 2
        blocks = []
        for b in range(self.size):
            k = self.me ^ b
            pos = (k >> 1) | ((k & 1) << high)
            blocks.append(lax.dynamic_slice_in_dim(v, pos * width, width, 1))
        return jnp.concatenate(blocks, axis=1)


def attention_masked(queries, keys_all, segment, place):
    scale = 1.0 / math.sqrt(HEAD_DIM)
    allowed = (segment[:, None] == segment[None, :]) & (place[None, :] <= place[:, None])
    scores = jnp.einsum("qcgd,kcd->cgqk", queries, keys_all, preferred_element_type=F32) * scale
    return jnp.where(allowed, scores, -1e30)


def per_device(
    dp_size,
    tensor_size,
    tokens,
    seq_lengths,
    seq_group,
    attn_gain,
    w_query,
    w_key,
    w_value,
    w_out,
    mlp_gain,
    w_gate,
    w_up,
    w_down,
    cotangent,
):
    cube = Cube(dp_size)
    line = Line(tensor_size)
    order_a, order_b = cube.bits, cube.bits[::-1]
    scale = 1.0 / math.sqrt(HEAD_DIM)
    width_q, width_k = w_query.shape[1], w_key.shape[1]
    own_rows = tokens.shape[0]
    row_count = own_rows * tensor_size
    features = tokens.shape[1]
    half = features // 2

    gains = cube.gather(jnp.stack([attn_gain, mlp_gain]), order_a)
    w_qkv = jnp.concatenate([w_query, w_key, w_value], axis=1)
    cut = w_qkv.shape[0] // 2
    qkv_a = cube.gather(w_qkv[:cut], order_a)
    qkv_b = cube.gather(w_qkv[cut:], order_b)
    tokens_rel = cube.columns_in(tokens)
    rows_all = line.gather(tokens_rel)
    w_out_0, mark = lax.optimization_barrier((w_out, qkv_a[cube.size // 2 - 1]))
    cut = w_out.shape[0] // 2
    out_a = cube.gather(w_out_0[:cut], order_a)
    out_b = cube.gather(w_out_0[cut:], order_b)
    gate_0 = after(w_gate, out_a[cube.size // 2 - 1])
    up_0 = after(w_up, out_a[cube.size // 2 - 1])
    gate_p = cube.gather(gate_0, order_a)
    up_p = cube.gather(up_0, order_b)
    down_0 = after(w_down, gate_p[cube.size // 2 - 1], up_p[cube.size // 2 - 1])
    cut = w_down.shape[0] // 2
    down_a = cube.gather(down_0[:cut], order_a)
    down_b = cube.gather(down_0[cut:], order_b)
    cot_0 = after(cotangent, rows_all)
    cot_rel = cube.columns_in(cot_0)
    incoming = line.gather(cot_rel)

    gain_one = jnp.concatenate([g[0] for g in gains]).astype(F32)
    gain_two = jnp.concatenate([g[1] for g in gains]).astype(F32)
    qkv_w = jnp.concatenate([p for ab in zip(qkv_a, qkv_b) for p in ab], axis=0)
    out_w = jnp.concatenate([jnp.concatenate(out_a, axis=1), jnp.concatenate(out_b, axis=1)], axis=0)
    gate_w = jnp.concatenate(gate_p, axis=0)
    up_w = jnp.concatenate(up_p, axis=0)
    down_w = jnp.concatenate([jnp.concatenate(down_a, axis=1), jnp.concatenate(down_b, axis=1)], axis=0)

    normed_all, _ = norm_parts(rows_all.astype(F32))
    attn_input = (normed_all * gain_one).astype(BF16)
    tokens_f = tokens_rel.astype(F32)
    normed_one, factor_one = norm_parts(tokens_f)
    heads_here = width_q // HEAD_DIM
    kv_here = width_k // HEAD_DIM
    head_group = heads_here // kv_here
    row = jnp.arange(row_count, dtype=jnp.int32)
    owner = lax.rem(line.index - row // own_rows + tensor_size, tensor_size)
    place = owner * own_rows + row % own_rows
    segment, position = layout(seq_lengths, seq_group, cube.me, place)
    cosine_table, sine_table = rope_tables(position, HEAD_DIM)
    qkv = mm(attn_input, qkv_w)
    queries = (
        rotate(qkv[:, :width_q].reshape(row_count, heads_here, HEAD_DIM), cosine_table, sine_table)
        .astype(BF16)
        .reshape(row_count, kv_here, head_group, HEAD_DIM)
    )
    keys_all = rotate(
        qkv[:, width_q : width_q + width_k].reshape(row_count, kv_here, HEAD_DIM), cosine_table, sine_table
    ).astype(BF16)
    values_all = qkv[:, width_q + width_k :].astype(BF16).reshape(row_count, kv_here, HEAD_DIM)
    scores = attention_masked(queries, keys_all, segment, place)
    row_max = jnp.max(scores, axis=-1, keepdims=True)
    exponent = jnp.exp(scores - row_max)
    row_sum = jnp.sum(exponent, axis=-1, keepdims=True)
    weights_low = (exponent / row_sum).astype(BF16)
    mixed = jnp.einsum("cgqk,kcd->qcgd", weights_low, values_all, preferred_element_type=F32)
    attended = mixed.reshape(row_count, heads_here * HEAD_DIM).astype(BF16)
    log_mass = row_max + jnp.log(row_sum)

    def split_rows(v):
        return [lax.slice_in_dim(v, r * own_rows, (r + 1) * own_rows, axis=0) for r in range(tensor_size)]

    residual = tokens_f + line.scatter(split_rows(mm(attended, out_w).astype(BF16)))
    normed_two, factor_two = norm_parts(residual)
    mlp_input = line.gather((normed_two * gain_two).astype(BF16))

    gate = mm(mlp_input, gate_w)
    up_proj = mm(mlp_input, up_w)
    sigmoid_gate = jax.nn.sigmoid(gate)
    hidden = (gate * sigmoid_gate * up_proj).astype(BF16)
    grad_hidden = outer(incoming, down_w)
    silu_slope = sigmoid_gate * (1.0 + gate * (1.0 - sigmoid_gate))
    grad_gate = (grad_hidden * up_proj * silu_slope).astype(BF16)
    grad_up = (grad_hidden * gate * sigmoid_gate).astype(BF16)
    grad_two_parts = (outer(grad_gate, gate_w) + outer(grad_up, up_w)).astype(BF16)
    grad_two = line.scatter(split_rows(grad_two_parts))

    down_grad = cube.reduce(
        inner(hidden, incoming[:, :half]).astype(BF16),
        inner(hidden, incoming[:, half:]).astype(BF16),
        1,
        order_a,
    )
    gate_grad = cube.reduce(
        inner(mlp_input[:, :half], grad_gate).astype(BF16),
        inner(mlp_input[:, half:], grad_gate).astype(BF16),
        0,
        order_b,
    )
    up_grad = cube.reduce(
        inner(mlp_input[:, :half], grad_up).astype(BF16),
        inner(mlp_input[:, half:], grad_up).astype(BF16),
        0,
        order_a,
    )
    block_part = line.scatter(split_rows(mm(hidden, down_w).astype(BF16)))
    block_out = cube.columns_out((residual + block_part).astype(BF16))

    gain_two_part = jnp.sum(grad_two * normed_two, axis=0)
    grad_residual = cot_rel.astype(F32) + norm_back(grad_two, gain_two, normed_two, factor_two)
    grad_attn_rows = line.gather(grad_residual.astype(BF16))

    grad_attended = outer(grad_attn_rows, out_w).astype(BF16)
    grad_block = grad_attended.reshape(row_count, kv_here, head_group, HEAD_DIM)
    scores = attention_masked(queries, keys_all, segment, place)
    probs = jnp.exp(scores - log_mass)
    weights_low = probs.astype(BF16)
    grad_probs = jnp.einsum("qcgd,kcd->cgqk", grad_block, values_all, preferred_element_type=F32)
    delta = jnp.sum(probs * grad_probs, axis=-1, keepdims=True)
    grad_scores = (probs * (grad_probs - delta)).astype(BF16)
    grad_queries = jnp.einsum("cgqk,kcd->qcgd", grad_scores, keys_all, preferred_element_type=F32) * scale
    grad_keys = jnp.einsum("cgqk,qcgd->kcd", grad_scores, queries, preferred_element_type=F32) * scale
    grad_values = jnp.einsum("cgqk,qcgd->kcd", weights_low, grad_block, preferred_element_type=F32)
    grad_queries = (
        rotate(grad_queries.reshape(row_count, heads_here, HEAD_DIM), cosine_table, -sine_table)
        .astype(BF16)
        .reshape(row_count, width_q)
    )
    grad_keys = rotate(grad_keys, cosine_table, -sine_table).astype(BF16).reshape(row_count, width_k)
    grad_qkv = jnp.concatenate(
        [grad_queries, grad_keys, grad_values.astype(BF16).reshape(row_count, width_k)], axis=1
    )
    grad_one_parts = outer(grad_qkv, qkv_w)
    gain_one_part = jnp.sum(grad_one_parts * normed_all, axis=0)
    grad_one = line.scatter(split_rows(grad_one_parts.astype(BF16)))
    qkv_grad = cube.reduce(
        inner(attn_input[:, :half], grad_qkv).astype(BF16),
        inner(attn_input[:, half:], grad_qkv).astype(BF16),
        0,
        order_b,
    )
    out_grad = cube.reduce(
        inner(attended, grad_attn_rows[:, :half]).astype(BF16),
        inner(attended, grad_attn_rows[:, half:]).astype(BF16),
        1,
        order_a,
    )
    gain_two_sum = cube.reduce_small(line.total(gain_two_part).reshape(dp_size, 1, -1))
    gain_one_sum = cube.reduce_small(line.total(gain_one_part).reshape(dp_size, 1, -1))
    grad_tokens = cube.columns_out(
        (grad_residual + norm_back(grad_one, gain_one, normed_one, factor_one)).astype(BF16)
    )
    return (
        block_out,
        grad_tokens,
        gain_one_sum[0],
        qkv_grad[:, :width_q],
        qkv_grad[:, width_q : width_q + width_k],
        qkv_grad[:, width_q + width_k :],
        out_grad,
        gain_two_sum[0],
        gate_grad,
        up_grad,
        down_grad,
    )


def solution(mesh):
    return jax.shard_map(
        functools.partial(per_device, mesh.shape["dp"], mesh.shape["tensor"]),
        mesh=mesh,
        in_specs=(
            P(("dp", "tensor"), None),
            P(),
            P(),
            P("dp"),
            P("dp", "tensor"),
            P("dp", "tensor"),
            P("dp", "tensor"),
            P("tensor", "dp"),
            P("dp"),
            P("dp", "tensor"),
            P("dp", "tensor"),
            P("tensor", "dp"),
            P(("dp", "tensor"), None),
        ),
        out_specs=(
            P(("dp", "tensor"), None),
            P(("dp", "tensor"), None),
            P("dp"),
            P("dp", "tensor"),
            P("dp", "tensor"),
            P("dp", "tensor"),
            P("tensor", "dp"),
            P("dp"),
            P("dp", "tensor"),
            P("dp", "tensor"),
            P("tensor", "dp"),
        ),
        check_vma=False,
    )
```

time: 1140 us -> 752 us (0.66)
  waiting for transfers between devices: 862 us -> 339 us
  starting transfers between devices: 1.62 us -> 180 us
  blocking collectives: 67.8 us -> 0 us
  local copies, waits for them, and re-layouts: 8.47 us -> 72.4 us
  matrix products: 137 us -> 111 us
  between operations: 16 us -> 3.18 us
    reduce_scatter x11 -> x0, waiting for transfers between devices: 508 us -> none  [the longest x1 76.9 us: per_device(): lax.psum_scatter(outer(grad_gate, gate_w) + outer(grad_up, up_w), 'tensor...]
    all_gather x9 -> x0, waiting for transfers between devices: 350 us -> none  [the longest x1 56.7 us: per_device(): lax.all_gather(w_down, 'dp', axis=1, tiled=True)]
    ppermute x0 -> x151, waiting for transfers between devices: none -> 339 us  [the longest x97 211 us: swap(): return lax.ppermute(v, 'dp', [(i, i ^ m) for i in range(self.size)])]
    ppermute x0 -> x151, starting transfers between devices: none -> 180 us  [the longest x12 58.7 us: scatter(): lax.ppermute(to_right, 'tensor', [(i, i + 1) for i in range(0, s)])]
    unnamed x87 -> x173, local copies, waits for them, and re-layouts: 8.38 us -> 58 us
    all_gather x4 -> x0, blocking collectives: 38.2 us -> none  [the longest x1 10.3 us: per_device(): lax.all_gather(attn_gain, 'dp', axis=0, tiled=True)]
    psum x1 -> x0, blocking collectives: 17.4 us -> none  [per_device(): gain_sums = lax.psum((gain_one_part, gain_two_part), 'tensor')]
    dot_general x13 -> x11, matrix products: 62.4 us -> 46.2 us  [the longest x5 36.6 us: mm(): return jnp.dot(left, right, preferred_element_type=F32)]
  transfers between devices with their start and end apart: 20 -> 151, of which waited for: 19 -> 60; matrix products, arithmetic and copies ran while one was open for 11% -> 20% of each run, Pallas kernels for 0% -> 0%
where the time goes in v1:
time: 752 us; the launch traced here: 740 us
  waiting for transfers between devices  339 us (45%)
  starting transfers between devices  180 us (24%)
  matrix products  111 us (15%)
  local copies, waits for them, and re-layouts  72.4 us (10%)
  other arithmetic  35.1 us (5%)
    ppermute x97, waiting for transfers between devices, swap(): return lax.ppermute(v, 'dp', [(i, i ^ m) for i in range(self.size)])  211 us
    ppermute x12, starting transfers between devices, scatter(): lax.ppermute(to_right, 'tensor', [(i, i + 1) for i in range(0, s)])  58.7 us
    unnamed x173, local copies, waits for them, and re-layouts  58 us
    ppermute x97, starting transfers between devices, swap(): return lax.ppermute(v, 'dp', [(i, i ^ m) for i in range(self.size)])  54.6 us
    ppermute x12, waiting for transfers between devices, gather(): lax.ppermute(to_left, 'tensor', [(i, i - 1) for i in range(1, size - s +...  53.2 us
    ppermute x12, waiting for transfers between devices, scatter(): lax.ppermute(to_right, 'tensor', [(i, i + 1) for i in range(0, s)])  46.2 us
    dot_general x5, matrix products, mm(): return jnp.dot(left, right, preferred_element_type=F32)  36.6 us
    dot_general x5, matrix products, outer(): lax.dot_general(left, right, (((1,), (1,)), ((), ())), preferred_element_...  33.3 us
  transfers between devices with their start and end apart: 151, of which 60 were waited for; matrix products, arithmetic and copies ran while one was open for 20% of the time, Pallas kernels for 0%

profile of v1, /device:TPU:0, one launch (start us, length us, event | category | flops | bytes accessed | tf_op | source)
XLA Modules:
  0.0 739.9 jit_solution(10177759898793990158)
XLA Ops:
  110.4 13.1 %collective-permute-done.3 = bf16[128,2048]{1,0:T(8,128)(2,1)S(1)} collective-permute-done((bf16[128,2048]{1,0:T(8,128)(2,1)S(1)}, bf16[128,2048]{1,0:T(8,128)(2,1)S(1)}, u32[]{:S(2)}, u32[]{:S(2)}) %collective-permute-start.3) | collective-permute-done | bytes 524320 | tf_op jit(solution)/shard_map/ppermute | solution.py:88
  177.8 8.4 %collective-permute-done.55 = bf16[256,2048]{1,0:T(8,128)(2,1)S(1)} collective-permute-done((bf16[256,2048]{1,0:T(8,128)(2,1)}, bf16[256,2048]{1,0:T(8,128)(2,1)S(1)}, u32[]{:S(2)}, u32[]{:S(2)}) %collective-permute-start.55) | collective-permute-done | bytes 1048608 | tf_op jit(solution)/shard_map/ppermute | solution.py:118
  189.9 12.6 %collective-permute-done.62 = bf16[256,2048]{1,0:T(8,128)(2,1)S(1)} collective-permute-done((bf16[256,2048]{1,0:T(8,128)(2,1)S(1)}, bf16[256,2048]{1,0:T(8,128)(2,1)S(1)}, u32[]{:S(2)}, u32[]{:S(2)}) %collective-permute-start.62) | collective-permute-done | bytes 1048608 | tf_op jit(solution)/shard_map/ppermute | solution.py:118
  202.5 11.5 %collective-permute-start.43 = (bf16[128,2048]{1,0:T(8,128)(2,1)S(1)}, bf16[128,2048]{1,0:T(8,128)(2,1)S(1)}, u32[]{:S(2)}, u32[]{:S(2)}) collective-permute-start(bf16[128,2048]{1,0:T(8,128)(2,1)S(1)} %get-tuple-element.78), channel_id=1, source_target_pairs={{0,1},{1,2},{2,3},{4,5},{5,6},{6,7},{8,9},{9,10},{10,11},{12,13},{... | collective-permute-start | bytes 1572872 | tf_op jit(solution)/shard_map/ppermute | solution.py:99
  232.8 7.4 collective-permute-done.90
  246.1 8.9 %collective-permute-done.75 = bf16[1024,256]{1,0:T(8,128)(2,1)S(1)} collective-permute-done((bf16[1024,256]{1,0:T(8,128)(2,1)S(1)}, bf16[1024,256]{1,0:T(8,128)(2,1)S(1)}, u32[]{:S(2)}, u32[]{:S(2)}) %collective-permute-start.75) | collective-permute-done | bytes 524320 | tf_op jit(solution)/shard_map/ppermute | solution.py:118
  258.3 7.6 %collective-permute-done.69 = bf16[1024,256]{1,0:T(8,128)(2,1)S(1)} collective-permute-done((bf16[1024,256]{1,0:T(8,128)(2,1)S(1)}, bf16[1024,256]{1,0:T(8,128)(2,1)S(1)}, u32[]{:S(2)}, u32[]{:S(2)}) %collective-permute-start.69) | collective-permute-done | bytes 524320 | tf_op jit(solution)/shard_map/ppermute | solution.py:118
  288.3 8.7 %collective-permute-done.49 = bf16[128,2048]{1,0:T(8,128)(2,1)} collective-permute-done((bf16[128,2048]{1,0:T(8,128)(2,1)S(1)}, bf16[128,2048]{1,0:T(8,128)(2,1)}, u32[]{:S(2)}, u32[]{:S(2)}) %collective-permute-start.49) | collective-permute-done | bytes 524320 | tf_op jit(solution)/shard_map/ppermute | solution.py:88
  301.9 10.2 %fusion.5 = f32[512,2048]{1,0:T(8,128)} fusion(bf16[1024,2048]{1,0:T(8,128)(2,1)} %constant_dynamic-update-slice_fusion.68, bf16[1024,2048]{1,0:T(8,128)(2,1)} %constant_dynamic-update-slice_fusion.60, bf16[128,2048]{1,0:T(8,128)(2,1)S(1)} %broadcast_select_fusion.1, bf16[128,2048]{1,0:T(8,128)(2,1)S(1)} %broadcast_select_fusion.5, ...), kind=kOutput, calls=%fused_computation.12 | convolution fusion | flops 4320133120 | bytes 14680064 | tf_op jit(solution)/shard_map/dot_general | solution.py:56
  312.4 11.8 %fusion.77 = f32[512,2048]{1,0:T(8,128)} fusion(bf16[2048,2048]{1,0:T(8,128)(2,1)} %constant_dynamic-update-slice_fusion.52, bf16[128,2048]{1,0:T(8,128)(2,1)S(1)} %broadcast_select_fusion.2, bf16[128,2048]{1,0:T(8,128)(2,1)S(1)} %broadcast_select_fusion.6, bf16[128,2048]{1,0:T(8,128)(2,1)S(1)} %broadcast_select_fusion.10, ...), kind=kOutput, calls=%fused_computation.332 | convolution fusion | flops 4303355904 | bytes 14680064 | tf_op jit(solution)/shard_map/dot_general | solution.py:48
  324.2 13.7 %multiply_convert_fusion.1 = (bf16[512,2048]{1,0:T(8,128)(2,1)S(1)}, bf16[512,2048]{1,0:T(8,128)(2,1)}, bf16[512,2048]{1,0:T(8,128)(2,1)S(1)}) fusion(f32[512,2048]{1,0:T(8,128)} %fusion.5, f32[512,2048]{1,0:T(8,128)} %fusion.77, bf16[2048,2048]{1,0:T(8,128)(2,1)} %constant_dynamic-update-slice_fusion.44, bf16[128,2048]{1,0:T(8,128)(2,1)S(1)} %broadcast_select_fusion.2, ...), kind=kOutput, calls=%fused_computation.25 | convolution fusion | flops 4320133120 | bytes 25165824 | tf_op jit(solution)/shard_map/dot_general | solution.py:48
  346.9 9.7 %fusion.92 = f32[512,2048]{1,0:T(8,128)} fusion(bf16[512,2048]{1,0:T(8,128)(2,1)S(1)} %get-tuple-element.53, bf16[2048,2048]{1,0:T(8,128)(2,1)} %constant_dynamic-update-slice_fusion.52), kind=kOutput, calls=%fused_computation.347 | convolution fusion | flops 4294967296 | bytes 14680064 | tf_op jit(solution)/shard_map/dot_general | solution.py:56
  356.6 8.0 %fusion.16 = bf16[512,2048]{1,0:T(8,128)(2,1)S(1)} fusion(bf16[512,2048]{1,0:T(8,128)(2,1)S(1)} %copy-done.37, bf16[1024,2048]{1,0:T(8,128)(2,1)} %constant_dynamic-update-slice_fusion.68, bf16[1024,2048]{1,0:T(8,128)(2,1)} %constant_dynamic-update-slice_fusion.60), kind=kOutput, calls=%fused_computation.35 | convolution fusion | flops 4312793088 | bytes 12582912 | tf_op jit(solution)/shard_map/dot_general | solution.py:48
  364.6 9.7 %add_convert_fusion = bf16[512,2048]{1,0:T(8,128)(2,1)S(1)} fusion(f32[512,2048]{1,0:T(8,128)} %fusion.92, bf16[512,2048]{1,0:T(8,128)(2,1)} %copy-done.36, bf16[2048,2048]{1,0:T(8,128)(2,1)} %constant_dynamic-update-slice_fusion.44), kind=kOutput, calls=%fused_computation.23 | convolution fusion | flops 4297064448 | bytes 16777216 | tf_op jit(solution)/shard_map/dot_general | solution.py:56
  437.1 8.1 %collective-permute-done.83 = bf16[128,2048]{1,0:T(8,128)(2,1)S(1)} collective-permute-done((bf16[128,2048]{1,0:T(8,128)(2,1)S(1)}, bf16[128,2048]{1,0:T(8,128)(2,1)S(1)}, u32[]{:S(2)}, u32[]{:S(2)}) %collective-permute-start.83) | collective-permute-done | bytes 524320 | tf_op jit(solution)/shard_map/ppermute | solution.py:99
  452.0 8.2 %collective-permute-start.131 = (f32[2048]{0:T(1024)S(1)}, f32[2048]{0:T(1024)S(1)}, u32[]{:S(2)}, u32[]{:S(2)}) collective-permute-start(f32[2048]{0:T(1024)S(1)} %get-tuple-element.21), channel_id=1, source_target_pairs={{0,3},{1,0},{2,1},{3,2},{4,7},{5,4},{6,5},{7,6},{8,11},{9,8},{10,9... | collective-permute-start | bytes 24584 | tf_op jit(solution)/shard_map/ppermute | solution.py:106
  479.4 12.6 %collective-permute-done.102 = bf16[128,2048]{1,0:T(8,128)(2,1)S(1)} collective-permute-done((bf16[128,2048]{1,0:T(8,128)(2,1)S(1)}, bf16[128,2048]{1,0:T(8,128)(2,1)S(1)}, u32[]{:S(2)}, u32[]{:S(2)}) %collective-permute-start.102) | collective-permute-done | bytes 524320 | tf_op jit(solution)/shard_map/ppermute | solution.py:88
  562.7 10.5 %collective-permute-done.127 = bf16[512,256]{1,0:T(8,128)(2,1)S(1)} collective-permute-done((bf16[512,256]{1,0:T(8,128)(2,1)S(1)}, bf16[512,256]{1,0:T(8,128)(2,1)S(1)}, u32[]{:S(2)}, u32[]{:S(2)}) %collective-permute-start.127) | collective-permute-done | bytes 262176 | tf_op jit(solution)/shard_map/ppermute | solution.py:118
  577.4 7.4 %collective-permute-start.107 = (bf16[128,2048]{1,0:T(8,128)(2,1)S(1)}, bf16[128,2048]{1,0:T(8,128)(2,1)S(1)}, u32[]{:S(2)}, u32[]{:S(2)}) collective-permute-start(bf16[128,2048]{1,0:T(8,128)(2,1)S(1)} %get-tuple-element.60), channel_id=1, source_target_pairs={{0,1},{1,2},{2,3},{4,5},{5,6},{6,7},{8,9},{9,10},{10,11},{12,13},{... | collective-permute-start | bytes 1572872 | tf_op jit(solution)/shard_map/ppermute | solution.py:99
  602.6 7.4 collective-permute-done.123
  610.9 10.9 %collective-permute-done.145 = bf16[256,2048]{1,0:T(8,128)(2,1)S(1)} collective-permute-done((bf16[256,2048]{1,0:T(8,128)(2,1)S(1)}, bf16[256,2048]{1,0:T(8,128)(2,1)S(1)}, u32[]{:S(2)}, u32[]{:S(2)}) %collective-permute-start.145) | collective-permute-done | bytes 1048608 | tf_op jit(solution)/shard_map/ppermute | solution.py:118
  625.0 40.0 %collective-permute-done.149 = bf16[2048,256]{1,0:T(8,128)(2,1)S(1)} collective-permute-done((bf16[2048,256]{1,0:T(8,128)(2,1)S(1)}, bf16[2048,256]{1,0:T(8,128)(2,1)S(1)}, u32[]{:S(2)}, u32[]{:S(2)}) %collective-permute-start.149) | collective-permute-done | bytes 1048608 | tf_op jit(solution)/shard_map/ppermute | solution.py:118
  679.1 14.2 %collective-permute-done.146 = bf16[256,2048]{1,0:T(8,128)(2,1)S(1)} collective-permute-done((bf16[256,2048]{1,0:T(8,128)(2,1)S(1)}, bf16[256,2048]{1,0:T(8,128)(2,1)S(1)}, u32[]{:S(2)}, u32[]{:S(2)}) %collective-permute-start.146) | collective-permute-done | bytes 1048608 | tf_op jit(solution)/shard_map/ppermute | solution.py:118
  696.5 38.9 %collective-permute-done.150 = bf16[2048,256]{1,0:T(8,128)(2,1)S(1)} collective-permute-done((bf16[2048,256]{1,0:T(8,128)(2,1)S(1)}, bf16[2048,256]{1,0:T(8,128)(2,1)S(1)}, u32[]{:S(2)}, u32[]{:S(2)}) %collective-permute-start.150) | collective-permute-done | bytes 1048608 | tf_op jit(solution)/shard_map/ppermute | solution.py:118
  (597 shorter events, 437.4 us)
Async XLA Ops:
  13.4 78.4 %collective-permute-start.1 = (bf16[128,2048]{1,0:T(8,128)(2,1)S(1)}, bf16[128,2048]{1,0:T(8,128)(2,1)S(1)}, u32[]{:S(2)}, u32[]{:S(2)}) collective-permute-start(bf16[128,2048]{1,0:T(8,128)(2,1)S(1)} %constant_dynamic-update-slice_fusion), channel_id=1, source_target_pairs={{1,0},{2,1},{3,2},{5,4},{6,5},{7,6},{9,8},{10,9},{11,10},{13,12},{... | collective-permute-start | bytes 1572872 | tf_op jit(solution)/shard_map/ppermute | solution.py:88
  14.7 77.4 %collective-permute-start = (bf16[128,2048]{1,0:T(8,128)(2,1)S(1)}, bf16[128,2048]{1,0:T(8,128)(2,1)S(1)}, u32[]{:S(2)}, u32[]{:S(2)}) collective-permute-start(bf16[128,2048]{1,0:T(8,128)(2,1)S(1)} %constant_dynamic-update-slice_fusion), channel_id=1, source_target_pairs={{0,1},{1,2},{2,3},{4,5},{5,6},{6,7},{8,9},{9,10},{10,11},{12,13},{... | collective-permute-start | bytes 1572872 | tf_op jit(solution)/shard_map/ppermute | solution.py:87
  30.1 33.7 %collective-permute-start.20 = (bf16[128,768]{1,0:T(8,128)(2,1)S(1)}, bf16[128,768]{1,0:T(8,128)(2,1)S(1)}, u32[]{:S(2)}, u32[]{:S(2)}) collective-permute-start(bf16[128,768]{1,0:T(8,128)(2,1)S(1)} %get-tuple-element.100), channel_id=1, source_target_pairs={{0,4},{4,0},{8,12},{12,8},{16,20},{20,16},{24,28},{28,24},{1,5},{5... | collective-permute-start | bytes 589832 | tf_op jit(solution)/shard_map/ppermute | solution.py:118
  96.7 57.5 %collective-permute-start.54 = (bf16[256,2048]{1,0:T(8,128)(2,1)}, bf16[256,2048]{1,0:T(8,128)(2,1)}, u32[]{:S(2)}, u32[]{:S(2)}) collective-permute-start(bf16[256,2048]{1,0:T(8,128)(2,1)} %param.22), channel_id=1, source_target_pairs={{0,16},{4,20},{8,24},{12,28},{16,0},{20,4},{24,8},{28,12},{1,17},{... | collective-permute-start | bytes 3145736 | tf_op jit(solution)/shard_map/ppermute | solution.py:118
  98.7 39.5 %collective-permute-start.53 = (bf16[256,2048]{1,0:T(8,128)(2,1)}, bf16[256,2048]{1,0:T(8,128)(2,1)}, u32[]{:S(2)}, u32[]{:S(2)}) collective-permute-start(bf16[256,2048]{1,0:T(8,128)(2,1)} %param.22), channel_id=1, source_target_pairs={{0,8},{4,12},{8,0},{12,4},{16,24},{20,28},{24,16},{28,20},{1,9},{5... | collective-permute-start | bytes 3145736 | tf_op jit(solution)/shard_map/ppermute | solution.py:118
  99.5 60.5 %collective-permute-start.60 = (bf16[256,2048]{1,0:T(8,128)(2,1)}, bf16[256,2048]{1,0:T(8,128)(2,1)}, u32[]{:S(2)}, u32[]{:S(2)}) collective-permute-start(bf16[256,2048]{1,0:T(8,128)(2,1)} %param.23), channel_id=1, source_target_pairs={{0,8},{4,12},{8,0},{12,4},{16,24},{20,28},{24,16},{28,20},{1,9},{5... | collective-permute-start | bytes 3145736 | tf_op jit(solution)/shard_map/ppermute | solution.py:118
  177.0 38.2 %collective-permute-start.58 = (bf16[256,2048]{1,0:T(8,128)(2,1)}, bf16[256,2048]{1,0:T(8,128)(2,1)S(1)}, u32[]{:S(2)}, u32[]{:S(2)}) collective-permute-start(bf16[256,2048]{1,0:T(8,128)(2,1)} %collective-permute-done.54), channel_id=1, source_target_pairs={{0,4},{4,0},{8,12},{12,8},{16,20},{20,16},{24,28},{28,24},{1,5},{5... | collective-permute-start | bytes 3145736 | tf_op jit(solution)/shard_map/ppermute | solution.py:118
  186.1 31.4 %collective-permute-start.63 = (bf16[256,2048]{1,0:T(8,128)(2,1)}, bf16[256,2048]{1,0:T(8,128)(2,1)S(1)}, u32[]{:S(2)}, u32[]{:S(2)}) collective-permute-start(bf16[256,2048]{1,0:T(8,128)(2,1)} %param.23), channel_id=1, source_target_pairs={{0,4},{4,0},{8,12},{12,8},{16,20},{20,16},{24,28},{28,24},{1,5},{5... | collective-permute-start | bytes 3145736 | tf_op jit(solution)/shard_map/ppermute | solution.py:118
  187.2 33.1 %collective-permute-start.64 = (bf16[256,2048]{1,0:T(8,128)(2,1)}, bf16[256,2048]{1,0:T(8,128)(2,1)S(1)}, u32[]{:S(2)}, u32[]{:S(2)}) collective-permute-start(bf16[256,2048]{1,0:T(8,128)(2,1)} %collective-permute-done.60), channel_id=1, source_target_pairs={{0,4},{4,0},{8,12},{12,8},{16,20},{20,16},{24,28},{28,24},{1,5},{5... | collective-permute-start | bytes 3145736 | tf_op jit(solution)/shard_map/ppermute | solution.py:118
  188.8 34.5 %collective-permute-start.65 = (bf16[256,2048]{1,0:T(8,128)(2,1)S(1)}, bf16[256,2048]{1,0:T(8,128)(2,1)S(1)}, u32[]{:S(2)}, u32[]{:S(2)}) collective-permute-start(bf16[256,2048]{1,0:T(8,128)(2,1)S(1)} %collective-permute-done.61), channel_id=1, source_target_pairs={{0,4},{4,0},{8,12},{12,8},{16,20},{20,16},{24,28},{28,24},{1,5},{5... | collective-permute-start | bytes 3145736 | tf_op jit(solution)/shard_map/ppermute | solution.py:118
  473.8 82.2 %collective-permute-start.143 = (bf16[1024,2048]{1,0:T(8,128)(2,1)}, bf16[1024,2048]{1,0:T(8,128)(2,1)}, u32[]{:S(2)}, u32[]{:S(2)}) collective-permute-start(bf16[1024,2048]{1,0:T(8,128)(2,1)} %convolution_convert_fusion.2), channel_id=1, source_target_pairs={{0,4},{4,0},{8,12},{12,8},{16,20},{20,16},{24,28},{28,24},{1,5},{5... | collective-permute-start | bytes 12582920 | tf_op jit(solution)/shard_map/ppermute | solution.py:118
  473.9 85.2 %collective-permute-start.147 = (bf16[2048,1024]{1,0:T(8,128)(2,1)}, bf16[2048,1024]{1,0:T(8,128)(2,1)S(1)}, u32[]{:S(2)}, u32[]{:S(2)}) collective-permute-start(bf16[2048,1024]{1,0:T(8,128)(2,1)} %convolution_convert_fusion), channel_id=1, source_target_pairs={{0,4},{4,0},{8,12},{12,8},{16,20},{20,16},{24,28},{28,24},{1,5},{5... | collective-permute-start | bytes 12582920 | tf_op jit(solution)/shard_map/ppermute | solution.py:118
  478.5 34.5 %collective-permute-start.138 = (f32[1,256]{1,0:T(1,128)S(1)}, f32[1,256]{1,0:T(1,128)S(1)}, u32[]{:S(2)}, u32[]{:S(2)}) collective-permute-start(f32[1,256]{1,0:T(1,128)S(1)} %bitcast.138), channel_id=1, source_target_pairs={{0,28},{4,24},{8,20},{12,16},{16,12},{20,8},{24,4},{28,0},{1,29},{... | collective-permute-start | bytes 3080 | tf_op jit(solution)/shard_map/ppermute | solution.py:118
  522.6 38.6 %collective-permute-start.139 = (bf16[1024,2048]{1,0:T(8,128)(2,1)}, bf16[1024,2048]{1,0:T(8,128)(2,1)S(1)}, u32[]{:S(2)}, u32[]{:S(2)}) collective-permute-start(bf16[1024,2048]{1,0:T(8,128)(2,1)} %convolution_convert_fusion.4), channel_id=1, source_target_pairs={{0,4},{4,0},{8,12},{12,8},{16,20},{20,16},{24,28},{28,24},{1,5},{5... | collective-permute-start | bytes 12582920 | tf_op jit(solution)/shard_map/ppermute | solution.py:118
  550.8 36.5 %collective-permute-start.121 = (bf16[1024,768]{1,0:T(8,128)(2,1)}, bf16[1024,768]{1,0:T(8,128)(2,1)S(1)}, u32[]{:S(2)}, u32[]{:S(2)}) collective-permute-start(bf16[1024,768]{1,0:T(8,128)(2,1)} %convolution_convert_fusion.7), channel_id=1, source_target_pairs={{0,4},{4,0},{8,12},{12,8},{16,20},{20,16},{24,28},{28,24},{1,5},{5... | collective-permute-start | bytes 4718600 | tf_op jit(solution)/shard_map/ppermute | solution.py:118
  573.2 104.7 %collective-permute-start.144 = (bf16[256,2048]{1,0:T(8,128)(2,1)S(1)}, bf16[256,2048]{1,0:T(8,128)(2,1)S(1)}, u32[]{:S(2)}, u32[]{:S(2)}) collective-permute-start(bf16[256,2048]{1,0:T(8,128)(2,1)S(1)} %get-tuple-element.47), channel_id=1, source_target_pairs={{0,8},{4,12},{8,0},{12,4},{16,24},{20,28},{24,16},{28,20},{1,9},{5... | collective-permute-start | bytes 3145736 | tf_op jit(solution)/shard_map/ppermute | solution.py:118
  574.7 47.0 %collective-permute-start.145 = (bf16[256,2048]{1,0:T(8,128)(2,1)S(1)}, bf16[256,2048]{1,0:T(8,128)(2,1)S(1)}, u32[]{:S(2)}, u32[]{:S(2)}) collective-permute-start(bf16[256,2048]{1,0:T(8,128)(2,1)S(1)} %get-tuple-element.48), channel_id=1, source_target_pairs={{0,8},{4,12},{8,0},{12,4},{16,24},{20,28},{24,16},{28,20},{1,9},{5... | collective-permute-start | bytes 3145736 | tf_op jit(solution)/shard_map/ppermute | solution.py:118
  587.3 109.2 %collective-permute-start.148 = (bf16[2048,256]{1,0:T(8,128)(2,1)S(1)}, bf16[2048,256]{1,0:T(8,128)(2,1)S(1)}, u32[]{:S(2)}, u32[]{:S(2)}) collective-permute-start(bf16[2048,256]{1,0:T(8,128)(2,1)S(1)} %get-tuple-element.45), channel_id=1, source_target_pairs={{0,8},{4,12},{8,0},{12,4},{16,24},{20,28},{24,16},{28,20},{1,9},{5... | collective-permute-start | bytes 3145736 | tf_op jit(solution)/shard_map/ppermute | solution.py:118
  594.6 70.4 %collective-permute-start.149 = (bf16[2048,256]{1,0:T(8,128)(2,1)S(1)}, bf16[2048,256]{1,0:T(8,128)(2,1)S(1)}, u32[]{:S(2)}, u32[]{:S(2)}) collective-permute-start(bf16[2048,256]{1,0:T(8,128)(2,1)S(1)} %get-tuple-element.46), channel_id=1, source_target_pairs={{0,8},{4,12},{8,0},{12,4},{16,24},{20,28},{24,16},{28,20},{1,9},{5... | collective-permute-start | bytes 3145736 | tf_op jit(solution)/shard_map/ppermute | solution.py:118
  610.0 57.1 %collective-permute-start.141 = (bf16[256,2048]{1,0:T(8,128)(2,1)S(1)}, bf16[256,2048]{1,0:T(8,128)(2,1)S(1)}, u32[]{:S(2)}, u32[]{:S(2)}) collective-permute-start(bf16[256,2048]{1,0:T(8,128)(2,1)S(1)} %get-tuple-element.50), channel_id=1, source_target_pairs={{0,16},{4,20},{8,24},{12,28},{16,0},{20,4},{24,8},{28,12},{1,17},{... | collective-permute-start | bytes 3145736 | tf_op jit(solution)/shard_map/ppermute | solution.py:118
  621.7 47.5 %collective-permute-start.122 = (bf16[256,768]{1,0:T(8,128)(2,1)S(1)}, bf16[256,768]{1,0:T(8,128)(2,1)S(1)}, u32[]{:S(2)}, u32[]{:S(2)}) collective-permute-start(bf16[256,768]{1,0:T(8,128)(2,1)S(1)} %get-tuple-element.56), channel_id=1, source_target_pairs={{0,16},{4,20},{8,24},{12,28},{16,0},{20,4},{24,8},{28,12},{1,17},{... | collective-permute-start | bytes 1179656 | tf_op jit(solution)/shard_map/ppermute | solution.py:118
  669.3 68.3 %collective-permute-start.140 = (bf16[256,2048]{1,0:T(8,128)(2,1)S(1)}, bf16[256,2048]{1,0:T(8,128)(2,1)S(1)}, u32[]{:S(2)}, u32[]{:S(2)}) collective-permute-start(bf16[256,2048]{1,0:T(8,128)(2,1)S(1)} %get-tuple-element.49), channel_id=1, source_target_pairs={{0,16},{4,20},{8,24},{12,28},{16,0},{20,4},{24,8},{28,12},{1,17},{... | collective-permute-start | bytes 3145736 | tf_op jit(solution)/shard_map/ppermute | solution.py:118
  674.6 60.9 %collective-permute-start.150 = (bf16[2048,256]{1,0:T(8,128)(2,1)S(1)}, bf16[2048,256]{1,0:T(8,128)(2,1)S(1)}, u32[]{:S(2)}, u32[]{:S(2)}) collective-permute-start(bf16[2048,256]{1,0:T(8,128)(2,1)S(1)} %add_convert_fusion.1), channel_id=1, source_target_pairs={{0,16},{4,20},{8,24},{12,28},{16,0},{20,4},{24,8},{28,12},{1,17},{... | collective-permute-start | bytes 3145736 | tf_op jit(solution)/shard_map/ppermute | solution.py:118
  677.9 59.6 %collective-permute-start.142 = (bf16[256,2048]{1,0:T(8,128)(2,1)S(1)}, bf16[256,2048]{1,0:T(8,128)(2,1)S(1)}, u32[]{:S(2)}, u32[]{:S(2)}) collective-permute-start(bf16[256,2048]{1,0:T(8,128)(2,1)S(1)} %add_convert_fusion.13), channel_id=1, source_target_pairs={{0,8},{4,12},{8,0},{12,4},{16,24},{20,28},{24,16},{28,20},{1,9},{5... | collective-permute-start | bytes 3145736 | tf_op jit(solution)/shard_map/ppermute | solution.py:118
  (166 other events, 2285.0 us)

commit v2 on v1

v2 whole, which is shorter than its diff:
```python
import functools
import math

import jax
import jax.numpy as jnp
from jax import lax
from jax.experimental import pallas as pl
from jax.experimental.pallas import tpu as pltpu
from jax.sharding import PartitionSpec as P

HEAD_DIM = 64
EPSILON = 1e-05
ROPE_BASE = 500000.0
F32 = jnp.float32
BF16 = jnp.bfloat16


def rope_tables(position, width):
    half_width = width // 2
    steps_f = jnp.arange(half_width, dtype=F32)
    inverse = 1.0 / ROPE_BASE ** (steps_f * 2.0 / width)
    angles = position.astype(F32)[:, None] * inverse[None, :]
    return (jnp.cos(angles)[:, None, :], jnp.sin(angles)[:, None, :])


def rotate(values, cosine_table, sine_table):
    half_width = values.shape[-1] // 2
    first_half = values[..., :half_width]
    second_half = values[..., half_width:]
    return jnp.concatenate(
        [
            first_half * cosine_table - second_half * sine_table,
            second_half * cosine_table + first_half * sine_table,
        ],
        axis=-1,
    )


def layout(seq_lengths, seq_group, group_id, place):
    owned_mask = (seq_group == group_id).astype(jnp.int32)
    owned_len = seq_lengths * owned_mask
    seq_ends = jnp.cumsum(owned_len)
    finished = (seq_ends[None, :] <= place[:, None]).astype(jnp.int32)
    segment = jnp.sum(finished * owned_mask[None, :], axis=1)
    offsets = jnp.sum(finished * owned_len[None, :], axis=1)
    return (segment, place - offsets)


def mm(left, right):
    return jnp.dot(left, right, preferred_element_type=F32)


def inner(left, right):
    return lax.dot_general(left, right, (((0,), (0,)), ((), ())), preferred_element_type=F32)


def outer(left, right):
    return lax.dot_general(left, right, (((1,), (1,)), ((), ())), preferred_element_type=F32)


def norm_parts(values):
    factor = lax.rsqrt(jnp.mean(values * values, axis=-1, keepdims=True) + EPSILON)
    return (values * factor, factor)


def norm_back(grad_rows, gain, normed, factor):
    scaled = grad_rows * gain
    return factor * (scaled - normed * jnp.mean(scaled * normed, axis=-1, keepdims=True))


def after(value, *deps):
    return lax.optimization_barrier((value,) + deps)[0]


class Line:
    def __init__(self, size):
        self.size = size
        self.index = lax.axis_index("tensor")

    def shift(self, v, r):
        return lax.ppermute(v, "tensor", [(i, (i + r) % self.size) for i in range(self.size)])

    def gather(self, v):
        return [v] + [self.shift(v, r) for r in range(1, self.size)]

    def scatter(self, parts):
        return [parts[0]] + [self.shift(parts[r], -r) for r in range(1, self.size)]

    def total(self, v):
        return functools.reduce(lambda a, b: a + b, [v] + [self.shift(v, r) for r in range(1, self.size)])


class Cube:
    def __init__(self, size):
        self.size = size
        self.me = lax.axis_index("dp")
        self.bits = [1 << b for b in range(size.bit_length() - 1)]
        self.keys = [2 * q for q in range(size // 2)] + [2 * q + 1 for q in range(size // 2)]

    def swap(self, v, m):
        return lax.ppermute(v, "dp", [(i, i ^ m) for i in range(self.size)])

    def gather_row(self, v):
        width = v.shape[1]
        for m in self.bits:
            v = jnp.concatenate([v, self.swap(v, m)], axis=1)
        cuts = [lax.dynamic_slice_in_dim(v, (self.me ^ b) * width, width, 1) for b in range(self.size)]
        return jnp.concatenate(cuts, axis=1)

    def places(self):
        return 2 * jnp.arange(self.size // 2, dtype=jnp.int32) + (self.me & 1)

    def over_chips(self, own):
        groups = [list(range(c, self.size, 2)) for c in range(2)]
        return lax.psum_scatter(own, "dp", scatter_dimension=0, axis_index_groups=groups, tiled=True)


class Order:
    def __init__(self):
        self.last = None

    def __call__(self, step, *args):
        if self.last is not None:
            args, _ = lax.optimization_barrier((args, self.last))
        out = step(*args)
        self.last = jax.tree.leaves(out)[0]
        return out


def total32(terms):
    return functools.reduce(lambda a, b: a + b, [t.astype(F32) for t in terms])


def tile_of(size, most):
    while size % most:
        most //= 2
    return most


def kernel_call(body, name, flops, operands, out_shape, vmem=48, **kwargs):
    shapes = jax.tree.leaves(out_shape)
    moved = sum(math.prod(a.shape) * a.dtype.itemsize for a in list(operands) + shapes)
    return pl.pallas_call(
        body,
        out_shape=out_shape,
        name=name,
        cost_estimate=pl.CostEstimate(flops=flops, bytes_accessed=moved, transcendentals=0),
        compiler_params=pltpu.CompilerParams(vmem_limit_bytes=vmem << 20),
        **kwargs,
    )(*operands)


def whole(shape):
    return pl.BlockSpec(shape, lambda *_: (0,) * len(shape))


def attention_in(x_blocks, gain, w, skip):
    count = len(x_blocks)
    rows, features = x_blocks[0].shape
    total, width = rows * count, w.shape[1] - skip
    tile = math.gcd(math.gcd(width, skip), 256)

    def body(*refs):
        x_refs, (gain_ref, w_ref, h_ref, out_ref) = refs[:count], refs[count:]

        @pl.when(pl.program_id(0) == 0)
        def _():
            for r in range(count):
                normed, _ = norm_parts(x_refs[r][...].astype(F32))
                h_ref[r * rows : (r + 1) * rows, :] = (normed * gain_ref[...]).astype(BF16)

        out_ref[...] = mm(h_ref[...], w_ref[...])

    return kernel_call(
        body,
        "attention_in",
        2 * total * features * width,
        (*x_blocks, gain, w),
        (jax.ShapeDtypeStruct((total, features), BF16), jax.ShapeDtypeStruct((total, width), F32)),
        grid=(width // tile,),
        in_specs=[whole((rows, features))] * count
        + [whole((1, features)), pl.BlockSpec((features, tile), lambda j: (0, skip // tile + j))],
        out_specs=[whole((total, features)), pl.BlockSpec((total, tile), lambda j: (0, j))],
    )


def feed_forward(h_blocks, c, w):
    count = len(h_blocks)
    rows, features = h_blocks[0].shape
    units = w.shape[1] // 3
    tile = tile_of(units, 256)
    steps = units // tile

    def body(*refs):
        h_refs = refs[:count]
        c_ref, gate_ref, up_ref, down_ref, h_all, out_ref = refs[count:]

        @pl.when(pl.program_id(0) == 0)
        def _():
            for r in range(count):
                h_all[r * rows : (r + 1) * rows, :] = h_refs[r][...]

        gate = mm(h_all[...], gate_ref[...])
        up = mm(h_all[...], up_ref[...])
        grad_hidden = mm(c_ref[...], down_ref[...])
        sig = 1.0 / (1.0 + jnp.exp(-gate))
        silu = gate * sig
        out_ref[0] = (grad_hidden * up * (sig * (1.0 + gate * (1.0 - sig)))).astype(BF16)
        out_ref[1] = (grad_hidden * silu).astype(BF16)
        out_ref[2] = (silu * up).astype(BF16)

    total = rows * count
    return kernel_call(
        body,
        "feed_forward",
        6 * total * features * units,
        (*h_blocks, c, w, w, w),
        (jax.ShapeDtypeStruct((total, features), BF16), jax.ShapeDtypeStruct((3, total, units), BF16)),
        grid=(steps,),
        in_specs=[whole((rows, features))] * count
        + [whole((total, features))]
        + [pl.BlockSpec((features, tile), lambda j, k=k: (0, k * steps + j)) for k in range(3)],
        out_specs=[whole((total, features)), pl.BlockSpec((3, total, tile), lambda j: (0, 0, j))],
    )


def rows_product(a, leads, w, first, count, name):
    rows, units = a.shape[1:]
    features = w.shape[0]
    tile = tile_of(features, 256)
    block = rows // count
    width = units * len(leads)
    aligned = first % width == 0

    def body(*refs):
        a_refs, w_ref, outs = refs[: len(leads)], refs[len(leads)], refs[len(leads) + 1 :]
        at = 0 if aligned else first
        acc = None
        for a_ref in a_refs:
            term = outer(a_ref[0], w_ref[:, at : at + units])
            acc = term if acc is None else acc + term
            at += units
        for r in range(count):
            outs[r][...] = acc[r * block : (r + 1) * block, :].astype(BF16)

    spec = pl.BlockSpec((tile, width), lambda j: (j, first // width))
    if not aligned:
        spec = pl.BlockSpec((tile, w.shape[1]), lambda j: (j, 0))
    return kernel_call(
        body,
        name,
        2 * rows * features * width,
        [a] * len(leads) + [w],
        [jax.ShapeDtypeStruct((block, features), BF16)] * count,
        grid=(features // tile,),
        in_specs=[pl.BlockSpec((1, rows, units), lambda j, k=k: (k, 0, 0)) for k in leads] + [spec],
        out_specs=[pl.BlockSpec((block, tile), lambda j: (0, j))] * count,
    )


def weight_grad(sides, parts, places, pieces, most, name):
    terms = len(sides[0])
    rows, width = sides[0][0].shape[0], sides[0][0].shape[1] // pieces
    count = places.shape[0]
    sizes = [n[0][0].shape[-1] for _, n in parts]
    tile = functools.reduce(math.gcd, sizes, most)
    starts = [0]
    for size in sizes:
        starts.append(starts[-1] + size // tile)
    n_sides, n_parts = len(sides), len(parts)

    def body(places_ref, *refs):
        d_refs = refs[: n_sides * terms * count]
        n_refs = refs[n_sides * terms * count :][: n_parts * terms]
        out_ref, turned = refs[-2:]
        j = pl.program_id(0)

        @pl.when(j == 0)
        def _():
            for k in range(n_sides * terms):
                for q in range(count):
                    turned[k, q * width : (q + 1) * width, :] = d_refs[k * count + q][...].T

        for p, (side, _) in enumerate(parts):

            @pl.when((j >= starts[p]) & (j < starts[p + 1]))
            def _(p=p, side=side):
                acc = None
                for t in range(terms):
                    term = mm(turned[side * terms + t], n_refs[p * terms + t][0])
                    acc = term if acc is None else acc + term
                out_ref[...] = acc.astype(BF16)

    def n_spec(p, lead):
        last = starts[p + 1] - starts[p] - 1
        return pl.BlockSpec((1, rows, tile), lambda j, _: (lead, 0, jnp.clip(j - starts[p], 0, last)))

    in_specs = [
        pl.BlockSpec((rows, width), lambda j, p, q=q: (0, p[q])) for _ in range(n_sides * terms) for q in range(count)
    ]
    in_specs += [n_spec(p, lead) for p, (_, n) in enumerate(parts) for _, lead in n]
    operands = [places] + [d for side in sides for d in side for _ in range(count)]
    operands += [a for _, n in parts for a, _ in n]
    return kernel_call(
        body,
        name,
        2 * terms * rows * count * width * starts[-1] * tile,
        operands,
        jax.ShapeDtypeStruct((count * width, starts[-1] * tile), BF16),
        grid_spec=pltpu.PrefetchScalarGridSpec(
            num_scalar_prefetch=1,
            grid=(starts[-1],),
            in_specs=in_specs,
            out_specs=pl.BlockSpec((count * width, tile), lambda j, _: (0, j)),
            scratch_shapes=[pltpu.VMEM((n_sides * terms, count * width, rows), BF16)],
        ),
    )


def attention_masked(queries, keys_all, segment, place):
    scale = 1.0 / math.sqrt(HEAD_DIM)
    allowed = (segment[:, None] == segment[None, :]) & (place[None, :] <= place[:, None])
    scores = jnp.einsum("qcgd,kcd->cgqk", queries, keys_all, preferred_element_type=F32) * scale
    return jnp.where(allowed, scores, -1e30)


def per_device(
    dp_size,
    tensor_size,
    tokens,
    seq_lengths,
    seq_group,
    attn_gain,
    w_query,
    w_key,
    w_value,
    w_out,
    mlp_gain,
    w_gate,
    w_up,
    w_down,
    cotangent,
):
    cube = Cube(dp_size)
    line = Line(tensor_size)
    scale = 1.0 / math.sqrt(HEAD_DIM)
    width_q, width_k = w_query.shape[1], w_key.shape[1]
    own_rows = tokens.shape[0]
    row_count = own_rows * tensor_size

    width_out, units = w_out.shape[0], w_gate.shape[1]

    rows_all = line.gather(tokens)
    gain_one = cube.gather_row(attn_gain[None, :]).astype(F32)
    w_attn = lax.all_gather(jnp.concatenate([w_out.T, w_query, w_key, w_value], axis=1), "dp", axis=0, tiled=True)
    gain_two = cube.gather_row(mlp_gain[None, :]).astype(F32)
    w_mlp = lax.all_gather(jnp.concatenate([w_gate, w_up, w_down.T], axis=1), "dp", axis=0, tiled=True)
    incoming = jnp.concatenate(line.gather(after(cotangent, *rows_all)), axis=0)
    incoming_other = cube.swap(incoming, 1)

    order = Order()
    attn_input, qkv = order(lambda *a: attention_in(a[:-2], a[-2], a[-1], width_out), *rows_all, gain_one, w_attn)
    tokens_f = tokens.astype(F32)
    normed_one, factor_one = norm_parts(tokens_f)
    heads_here = width_q // HEAD_DIM
    kv_here = width_k // HEAD_DIM
    head_group = heads_here // kv_here
    row = jnp.arange(row_count, dtype=jnp.int32)
    owner = lax.rem(line.index - row // own_rows + tensor_size, tensor_size)
    place = owner * own_rows + row % own_rows
    segment, position = layout(seq_lengths, seq_group, cube.me, place)
    cosine_table, sine_table = rope_tables(position, HEAD_DIM)
    queries = (
        rotate(qkv[:, :width_q].reshape(row_count, heads_here, HEAD_DIM), cosine_table, sine_table)
        .astype(BF16)
        .reshape(row_count, kv_here, head_group, HEAD_DIM)
    )
    keys_all = rotate(
        qkv[:, width_q : width_q + width_k].reshape(row_count, kv_here, HEAD_DIM), cosine_table, sine_table
    ).astype(BF16)
    values_all = qkv[:, width_q + width_k :].astype(BF16).reshape(row_count, kv_here, HEAD_DIM)
    scores = attention_masked(queries, keys_all, segment, place)
    row_max = jnp.max(scores, axis=-1, keepdims=True)
    exponent = jnp.exp(scores - row_max)
    row_sum = jnp.sum(exponent, axis=-1, keepdims=True)
    weights_low = (exponent / row_sum).astype(BF16)
    mixed = jnp.einsum("cgqk,kcd->qcgd", weights_low, values_all, preferred_element_type=F32)
    attended = mixed.reshape(row_count, heads_here * HEAD_DIM).astype(BF16)
    log_mass = row_max + jnp.log(row_sum)

    out_parts = order(
        lambda a, w: rows_product(a, [0], w, 0, tensor_size, "attention_out"), attended[None], w_attn
    )
    residual = order(lambda x, *terms: x + total32(terms), tokens_f, *line.scatter(out_parts))
    normed_two, factor_two = norm_parts(residual)
    mlp_blocks = line.gather((normed_two * gain_two).astype(BF16))

    mlp_input, unit_grads = order(feed_forward, mlp_blocks, incoming, w_mlp)
    mlp_input_other, unit_grads_other = cube.swap(mlp_input, 1), cube.swap(unit_grads, 1)
    two_parts = order(
        lambda a, w: rows_product(a, [0, 1], w, 0, tensor_size, "feed_forward_rows_grad"), unit_grads, w_mlp
    )
    two_terms = line.scatter(two_parts)

    def mlp_grad(h, h_other, c, c_other, n, n_other):
        parts = [(side, [(n, lead), (n_other, lead)]) for side, lead in ((0, 0), (0, 1), (1, 2))]
        sides = [[h, h_other], [c, c_other]]
        return weight_grad(sides, parts, cube.places(), dp_size, 512, "feed_forward_grad")

    mlp_sum = cube.over_chips(
        order(mlp_grad, mlp_input, mlp_input_other, incoming, incoming_other, unit_grads, unit_grads_other)
    )

    grad_residual = order(
        lambda c, g, n, f, *terms: c.astype(F32) + norm_back(total32(terms), g, n, f),
        cotangent,
        gain_two,
        normed_two,
        factor_two,
        *two_terms,
    )
    gathered = line.gather(grad_residual.astype(BF16))
    block_parts = order(
        lambda a, w: rows_product(a, [2], w, 2 * units, tensor_size, "block_out"), unit_grads, w_mlp
    )
    grad_attn_rows = order(lambda *b: jnp.concatenate(b, axis=0), *gathered)
    block_terms = line.scatter(lax.optimization_barrier((block_parts, grad_attn_rows))[0])

    grad_attended = mm(grad_attn_rows, w_attn[:, :width_out]).astype(BF16)
    grad_block = grad_attended.reshape(row_count, kv_here, head_group, HEAD_DIM)
    scores = attention_masked(queries, keys_all, segment, place)
    probs = jnp.exp(scores - log_mass)
    weights_low = probs.astype(BF16)
    grad_probs = jnp.einsum("qcgd,kcd->cgqk", grad_block, values_all, preferred_element_type=F32)
    delta = jnp.sum(probs * grad_probs, axis=-1, keepdims=True)
    grad_scores = (probs * (grad_probs - delta)).astype(BF16)
    grad_queries = jnp.einsum("cgqk,kcd->qcgd", grad_scores, keys_all, preferred_element_type=F32) * scale
    grad_keys = jnp.einsum("cgqk,qcgd->kcd", grad_scores, queries, preferred_element_type=F32) * scale
    grad_values = jnp.einsum("cgqk,qcgd->kcd", weights_low, grad_block, preferred_element_type=F32)
    grad_queries = (
        rotate(grad_queries.reshape(row_count, heads_here, HEAD_DIM), cosine_table, -sine_table)
        .astype(BF16)
        .reshape(row_count, width_q)
    )
    grad_keys = rotate(grad_keys, cosine_table, -sine_table).astype(BF16).reshape(row_count, width_k)
    grad_qkv = jnp.concatenate(
        [grad_queries, grad_keys, grad_values.astype(BF16).reshape(row_count, width_k)], axis=1
    )
    one_parts = order(
        lambda a, w: rows_product(a, [0], w, width_out, tensor_size, "attention_rows_grad"),
        after(grad_qkv, *block_terms)[None],
        w_attn,
    )
    one_terms = line.scatter(one_parts)

    def attn_grad(y, h, a, g):
        parts = [(0, [(a[None], 0)]), (1, [(g[None], 0)])]
        places = jnp.arange(dp_size, dtype=jnp.int32)
        return weight_grad([[y], [h]], parts, places, dp_size, 256, "attention_grad")

    attn_terms = order(attn_grad, grad_attn_rows, attn_input, attended, grad_qkv)
    attn_sum = lax.psum_scatter(after(attn_terms, mlp_sum), "dp", scatter_dimension=0, tiled=True)
    mlp_sum = mlp_sum.astype(F32)
    gate_grad, up_grad, down_grad = mlp_sum[:, :units], mlp_sum[:, units : 2 * units], mlp_sum[:, 2 * units :].T
    block_out = (residual + total32(block_terms)).astype(BF16)
    attn_sum = attn_sum.astype(F32)
    out_grad, qkv_grad = attn_sum[:, :width_out].T, attn_sum[:, width_out:]
    query_grad = qkv_grad[:, :width_q]
    key_grad = qkv_grad[:, width_q : width_q + width_k]
    value_grad = qkv_grad[:, width_q + width_k :]

    def gain_terms(*pairs):
        return functools.reduce(lambda a, b: a + b, [jnp.sum(w.astype(F32) * g, axis=1) for w, g in pairs])

    gain_sums = line.total(
        jnp.stack(
            [
                gain_terms((w_query, query_grad), (w_key, key_grad), (w_value, value_grad)),
                gain_terms((w_gate, gate_grad), (w_up, up_grad)),
            ]
        )
    )
    attn_gain_grad = gain_sums[0] / attn_gain.astype(F32)
    mlp_gain_grad = gain_sums[1] / mlp_gain.astype(F32)
    grad_tokens = order(
        lambda c, g, n, f, *terms: (c + norm_back(total32(terms), g, n, f)).astype(BF16),
        grad_residual,
        gain_one,
        normed_one,
        factor_one,
        *one_terms,
    )
    return (
        block_out,
        grad_tokens,
        attn_gain_grad,
        query_grad,
        key_grad,
        value_grad,
        out_grad,
        mlp_gain_grad,
        gate_grad,
        up_grad,
        down_grad,
    )


def solution(mesh):
    return jax.shard_map(
        functools.partial(per_device, mesh.shape["dp"], mesh.shape["tensor"]),
        mesh=mesh,
        in_specs=(
            P(("dp", "tensor"), None),
            P(),
            P(),
            P("dp"),
            P("dp", "tensor"),
            P("dp", "tensor"),
            P("dp", "tensor"),
            P("tensor", "dp"),
            P("dp"),
            P("dp", "tensor"),
            P("dp", "tensor"),
            P("tensor", "dp"),
            P(("dp", "tensor"), None),
        ),
        out_specs=(
            P(("dp", "tensor"), None),
            P(("dp", "tensor"), None),
            P("dp"),
            P("dp", "tensor"),
            P("dp", "tensor"),
            P("dp", "tensor"),
            P("tensor", "dp"),
            P("dp"),
            P("dp", "tensor"),
            P("dp", "tensor"),
            P("tensor", "dp"),
        ),
        check_vma=False,
    )
```

time: 752 us -> 541 us (0.72); the launches traced: 740 us -> 540 us
  matrix products: 111 us -> 13.7 us
  waiting for transfers between devices: 339 us -> 242 us
  starting transfers between devices: 180 us -> 83.8 us
  Pallas kernels: 0 us -> 93.9 us
  local copies, waits for them, and re-layouts: 72.4 us -> 52.4 us
  between operations: 3.18 us -> 14.7 us
    ppermute x97 -> x9, waiting for transfers between devices: 211 us -> 3.59 us  [swap(): return lax.ppermute(v, 'dp', [(i, i ^ m) for i in range(self.size)])]
    ppermute x54 -> x27, waiting for transfers between devices: 128 us -> 238 us  [shift(): lax.ppermute(v, 'tensor', [(i, (i + r) % self.size) for i in range(self.s...]
    pallas_call x0 -> x8, Pallas kernels: none -> 93.9 us  [kernel_call(): pl.pallas_call(body, out_shape=out_shape, name=name, cost_estimate=pl.Cos...]
    dot_general x15 -> x0, matrix products: 64.5 us -> none  [the longest x5 33.3 us: outer(): lax.dot_general(left, right, (((1,), (1,)), ((), ())), preferred_element_...]
    ppermute x97 -> x9, starting transfers between devices: 54.6 us -> 6.29 us  [swap(): return lax.ppermute(v, 'dp', [(i, i ^ m) for i in range(self.size)])]
    ppermute x54 -> x27, starting transfers between devices: 125 us -> 77.3 us  [shift(): lax.ppermute(v, 'tensor', [(i, (i + r) % self.size) for i in range(self.s...]
    dot_general x5 -> x1, matrix products: 36.6 us -> 2.95 us  [mm(): return jnp.dot(left, right, preferred_element_type=F32)]
    unnamed x173 -> x158, local copies, waits for them, and re-layouts: 58 us -> 42.4 us
  transfers between devices with their start and end apart: 151 -> 40, of which waited for: 60 -> 15; matrix products, arithmetic and copies ran while one was open for 20% -> 14% of each run, Pallas kernels for 0% -> 9%
where the time goes in v2:
time: 541 us; the launch traced here: 540 us
  waiting for transfers between devices  242 us (45%)
  Pallas kernels  93.9 us (17%)
  starting transfers between devices  83.8 us (15%)
  local copies, waits for them, and re-layouts  52.4 us (10%)
  other arithmetic  39 us (7%)
  between operations  14.7 us (3%)
  matrix products  13.7 us (3%)
    ppermute x27, waiting for transfers between devices, shift(): lax.ppermute(v, 'tensor', [(i, (i + r) % self.size) for i in range(self.s...  238 us
    pallas_call x8, Pallas kernels, kernel_call(): pl.pallas_call(body, out_shape=out_shape, name=name, cost_estimate=pl.Cos...  93.9 us
    ppermute x27, starting transfers between devices, shift(): lax.ppermute(v, 'tensor', [(i, (i + r) % self.size) for i in range(self.s...  77.3 us
    unnamed x158, local copies, waits for them, and re-layouts  42.4 us
  transfers between devices with their start and end apart: 40, of which 15 were waited for; matrix products, arithmetic and copies ran while one was open for 14% of the time, Pallas kernels for 9%

profile of v2, /device:TPU:0, one launch (start us, length us, event | category | flops | bytes accessed | tf_op | source)
XLA Modules:
  0.0 539.6 jit_solution(3373767402224341229)
XLA Ops:
  35.3 20.0 %collective-permute-done.1.refs_2_ = bf16[128,2048]{1,0:T(8,128)(2,1)S(1)} collective-permute-done((bf16[128,2048]{1,0:T(8,128)(2,1)S(1)}, bf16[128,2048]{1,0:T(8,128)(2,1)S(1)}, u32[]{:S(2)}, u32[]{:S(2)}) %collective-permute-start.1) | collective-permute-done | bytes 524320 | tf_op jit(solution)/shard_map/ppermute | solution.py:81
  55.3 4.8 attention_in.1
  73.3 5.7 %attention_out.1 = (bf16[128,2048]{1,0:T(8,128)(2,1)S(1)}, bf16[128,2048]{1,0:T(8,128)(2,1)S(1)}, bf16[128,2048]{1,0:T(8,128)(2,1)S(1)}, bf16[128,2048]{1,0:T(8,128)(2,1)S(1)}) custom-call(bf16[1,512,512]{2,1,0:T(8,128)(2,1)S(1)} %copy.71.refs_0_, bf16[2048,1280]{1,0:T(8,128)(2,1)} %all-gather.3.cloned.1.call-done.refs_5_.refs_1_), custom_call_target="tpu_custom_call" | custom-call | flops 1073741824 | bytes 7864320 | tf_op jit(solution)/shard_map/attention_out/pallas_call | solution.py:143
  79.0 12.4 %collective-permute-start.6 = (bf16[128,2048]{1,0:T(8,128)(2,1)S(1)}, bf16[128,2048]{1,0:T(8,128)(2,1)S(1)}, u32[]{:S(2)}, u32[]{:S(2)}) collective-permute-start(bf16[128,2048]{1,0:T(8,128)(2,1)S(1)} %get-tuple-element.92), channel_id=1, source_target_pairs={{0,3},{1,0},{2,1},{3,2},{4,7},{5,4},{6,5},{7,6},{8,11},{9,8},{10,9... | collective-permute-start | bytes 1572872 | tf_op jit(solution)/shard_map/ppermute | solution.py:81
  113.3 47.9 %collective-permute-done.7 = bf16[128,2048]{1,0:T(8,128)(2,1)} collective-permute-done((bf16[128,2048]{1,0:T(8,128)(2,1)S(1)}, bf16[128,2048]{1,0:T(8,128)(2,1)}, u32[]{:S(2)}, u32[]{:S(2)}) %collective-permute-start.7) | collective-permute-done | bytes 524320 | tf_op jit(solution)/shard_map/ppermute | solution.py:81
  169.5 25.2 %collective-permute-done.16 = bf16[128,2048]{1,0:T(8,128)(2,1)S(1)} collective-permute-done((bf16[128,2048]{1,0:T(8,128)(2,1)}, bf16[128,2048]{1,0:T(8,128)(2,1)S(1)}, u32[]{:S(2)}, u32[]{:S(2)}) %collective-permute-start.16) | collective-permute-done | bytes 524320 | tf_op jit(solution)/shard_map/ppermute | solution.py:81
  197.2 20.0 %collective-permute-done.13.refs_2_ = bf16[128,2048]{1,0:T(8,128)(2,1)S(1)} collective-permute-done((bf16[128,2048]{1,0:T(8,128)(2,1)S(1)}, bf16[128,2048]{1,0:T(8,128)(2,1)S(1)}, u32[]{:S(2)}, u32[]{:S(2)}) %collective-permute-start.13) | collective-permute-done | bytes 524320 | tf_op jit(solution)/shard_map/ppermute | solution.py:81
  221.9 20.1 %feed_forward.1 = (bf16[512,2048]{1,0:T(8,128)(2,1)S(1)}, bf16[3,512,2048]{2,1,0:T(8,128)(2,1)}) custom-call(bf16[128,2048]{1,0:T(8,128)(2,1)S(1)} %get-tuple-element.101.refs_0_, bf16[128,2048]{1,0:T(8,128)(2,1)S(1)} %copy-done.7, bf16[128,2048]{1,0:T(8,128)(2,1)S(1)} %copy-done.9, bf16[128,2048]{1,0:T(8,128)(2,1)S(1)} %copy-done.11, ...), custom_call_target="tpu_custom_call" | custom-call | flops 12884901888 | bytes 88080384 | tf_op jit(solution)/shard_map/feed_forward/pallas_call | solution.py:143
  242.5 14.4 %feed_forward_rows_grad.1 = (bf16[128,2048]{1,0:T(8,128)(2,1)S(1)}, bf16[128,2048]{1,0:T(8,128)(2,1)S(1)}, bf16[128,2048]{1,0:T(8,128)(2,1)S(1)}, bf16[128,2048]{1,0:T(8,128)(2,1)S(1)}) custom-call(bf16[3,512,2048]{2,1,0:T(8,128)(2,1)} %get-tuple-element.129.refs_0_.refs_1_.refs_16_.refs_18_.refs_20_, ...), custom_call_target="tpu_custom_call" | custom-call | flops 8589934592 | bytes 39845888 | tf_op jit(solution)/shard_map/feed_forward_rows_grad/pallas_call | solution.py:143
  259.3 23.5 %feed_forward_grad.1 = bf16[1024,6144]{1,0:T(8,128)(2,1)} custom-call(s32[4]{0:T(128)S(1)} %multiply_add_fusion.1.places_ref, bf16[512,2048]{1,0:T(8,128)(2,1)S(1)} %get-tuple-element.115.refs_0_.refs_1_.refs_2_.refs_3_, bf16[512,2048]{1,0:T(8,128)(2,1)S(1)} %get-tuple-element.115.refs_0_.refs_1_.refs_2_.refs_3_, ...), custom_call_target="tpu_custom_call" | custom-call | flops 12884901888 | bytes 83886096 | tf_op jit(solution)/shard_map/feed_forward_grad/pallas_call | solution.py:143
  283.9 11.9 %collective-permute-start.18 = (bf16[128,2048]{1,0:T(8,128)(2,1)S(1)}, bf16[128,2048]{1,0:T(8,128)(2,1)S(1)}, u32[]{:S(2)}, u32[]{:S(2)}) collective-permute-start(bf16[128,2048]{1,0:T(8,128)(2,1)S(1)} %copy-done.25), channel_id=1, source_target_pairs={{0,3},{1,0},{2,1},{3,2},{4,7},{5,4},{6,5},{7,6},{8,11},{9,8},{10,9... | collective-permute-start | bytes 1572872 | tf_op jit(solution)/shard_map/ppermute | solution.py:81
  296.5 11.6 %collective-permute-done.18 = bf16[128,2048]{1,0:T(8,128)(2,1)S(1)} collective-permute-done((bf16[128,2048]{1,0:T(8,128)(2,1)S(1)}, bf16[128,2048]{1,0:T(8,128)(2,1)S(1)}, u32[]{:S(2)}, u32[]{:S(2)}) %collective-permute-start.18) | collective-permute-done | bytes 524320 | tf_op jit(solution)/shard_map/ppermute | solution.py:81
  308.1 33.3 %collective-permute-done.19 = bf16[128,2048]{1,0:T(8,128)(2,1)S(1)} collective-permute-done((bf16[128,2048]{1,0:T(8,128)(2,1)S(1)}, bf16[128,2048]{1,0:T(8,128)(2,1)S(1)}, u32[]{:S(2)}, u32[]{:S(2)}) %collective-permute-start.19) | collective-permute-done | bytes 524320 | tf_op jit(solution)/shard_map/ppermute | solution.py:81
  350.3 10.8 %block_out.1 = (bf16[128,2048]{1,0:T(8,128)(2,1)S(1)}, bf16[128,2048]{1,0:T(8,128)(2,1)}, bf16[128,2048]{1,0:T(8,128)(2,1)}, bf16[128,2048]{1,0:T(8,128)(2,1)}) custom-call(bf16[3,512,2048]{2,1,0:T(8,128)(2,1)} %get-tuple-element.129.refs_0_.refs_1_.refs_16_.refs_18_.refs_20_, ...), custom_call_target="tpu_custom_call" | custom-call | flops 4294967296 | bytes 33554432 | tf_op jit(solution)/shard_map/block_out/pallas_call | solution.py:143
  361.5 21.3 %collective-permute-done.25 = bf16[128,2048]{1,0:T(8,128)(2,1)S(1)} collective-permute-done((bf16[128,2048]{1,0:T(8,128)(2,1)S(1)}, bf16[128,2048]{1,0:T(8,128)(2,1)S(1)}, u32[]{:S(2)}, u32[]{:S(2)}) %collective-permute-start.25) | collective-permute-done | bytes 524320 | tf_op jit(solution)/shard_map/ppermute | solution.py:81
  383.0 11.4 %collective-permute-start.29 = (bf16[128,2048]{1,0:T(8,128)(2,1)}, bf16[128,2048]{1,0:T(8,128)(2,1)}, u32[]{:S(2)}, u32[]{:S(2)}) collective-permute-start(bf16[128,2048]{1,0:T(8,128)(2,1)} %get-tuple-element.142), channel_id=1, source_target_pairs={{0,1},{1,2},{2,3},{3,0},{4,5},{5,6},{6,7},{7,4},{8,9},{9,10},{10,1... | collective-permute-start | bytes 1572872 | tf_op jit(solution)/shard_map/ppermute | solution.py:81
  414.2 15.6 %collective-permute-done.28 = bf16[128,2048]{1,0:T(8,128)(2,1)} collective-permute-done((bf16[128,2048]{1,0:T(8,128)(2,1)}, bf16[128,2048]{1,0:T(8,128)(2,1)}, u32[]{:S(2)}, u32[]{:S(2)}) %collective-permute-start.28) | collective-permute-done | bytes 524320 | tf_op jit(solution)/shard_map/ppermute | solution.py:81
  429.8 6.7 %attention_rows_grad.1 = (bf16[128,2048]{1,0:T(8,128)(2,1)S(1)}, bf16[128,2048]{1,0:T(8,128)(2,1)S(1)}, bf16[128,2048]{1,0:T(8,128)(2,1)S(1)}, bf16[128,2048]{1,0:T(8,128)(2,1)S(1)}) custom-call(bf16[1,512,768]{2,1,0:T(8,128)(2,1)S(1)} %bitcast.88, bf16[2048,1280]{1,0:T(8,128)(2,1)} %all-gather.3.cloned.1.call-done.refs_5_.refs_1_), custom_call_target="tpu_custom_call" | custom-call | flops 1610612736 | bytes 8126464 | tf_op jit(solution)/shard_map/attention_rows_grad/pallas_call | solution.py:143
  444.4 8.0 %attention_grad.1 = bf16[2048,1280]{1,0:T(8,128)(2,1)} custom-call(s32[8]{0:T(128)S(1)} %iota.25.places_ref, bf16[512,2048]{1,0:T(8,128)(2,1)S(1)} %constant_dynamic-update-slice_fusion.28.refs_0_.refs_1_.refs_2_.refs_3_.refs_4_.refs_5_.refs_6_.refs_7_, ...), custom_call_target="tpu_custom_call" | custom-call | flops 2684354560 | bytes 40108064 | tf_op jit(solution)/shard_map/attention_grad/pallas_call | solution.py:143
  453.4 12.8 %collective-permute-start.30 = (bf16[128,2048]{1,0:T(8,128)(2,1)S(1)}, bf16[128,2048]{1,0:T(8,128)(2,1)S(1)}, u32[]{:S(2)}, u32[]{:S(2)}) collective-permute-start(bf16[128,2048]{1,0:T(8,128)(2,1)S(1)} %copy-done.21), channel_id=1, source_target_pairs={{0,3},{1,0},{2,1},{3,2},{4,7},{5,4},{6,5},{7,6},{8,11},{9,8},{10,9... | collective-permute-start | bytes 1572872 | tf_op jit(solution)/shard_map/ppermute | solution.py:81
  466.9 3.3 add_convert_fusion.1
  470.2 8.4 %collective-permute-done.30 = bf16[128,2048]{1,0:T(8,128)(2,1)S(1)} collective-permute-done((bf16[128,2048]{1,0:T(8,128)(2,1)S(1)}, bf16[128,2048]{1,0:T(8,128)(2,1)S(1)}, u32[]{:S(2)}, u32[]{:S(2)}) %collective-permute-start.30) | collective-permute-done | bytes 524320 | tf_op jit(solution)/shard_map/ppermute | solution.py:81
  478.6 33.5 %collective-permute-done.31 = bf16[128,2048]{1,0:T(8,128)(2,1)S(1)} collective-permute-done((bf16[128,2048]{1,0:T(8,128)(2,1)S(1)}, bf16[128,2048]{1,0:T(8,128)(2,1)S(1)}, u32[]{:S(2)}, u32[]{:S(2)}) %collective-permute-start.31) | collective-permute-done | bytes 524320 | tf_op jit(solution)/shard_map/ppermute | solution.py:81
  517.4 4.5 multiply_reduce_fusion
  (315 shorter events, 137.9 us)
Async XLA Ops:
  7.2 48.1 %all-gather.3.cloned.1.call-start = ((), (), s32[]{:S(2)}) async-start(), calls=%async_computation.2 | async-start | bytes 5898240 | tf_op jit(solution)/shard_map/all_gather | solution.py:355
  10.4 208.4 %all-gather.5.cloned.1.call-start = ((), (), s32[]{:S(2)}) async-start(), calls=%async_computation.3 | async-start | bytes 28311552 | tf_op jit(solution)/shard_map/all_gather | solution.py:357
  14.8 437.6 %reduce-scatter.3.cloned.1.call-start = ((), (), s32[]{:S(2)}) async-start(), calls=%async_computation.4 | async-start | bytes 15728640 | tf_op jit(solution)/shard_map/reduce_scatter | solution.py:115
  18.8 36.6 %collective-permute-start.1 = (bf16[128,2048]{1,0:T(8,128)(2,1)S(1)}, bf16[128,2048]{1,0:T(8,128)(2,1)S(1)}, u32[]{:S(2)}, u32[]{:S(2)}) collective-permute-start(bf16[128,2048]{1,0:T(8,128)(2,1)S(1)} %copy-done.2), channel_id=1, source_target_pairs={{0,2},{1,3},{2,0},{3,1},{4,6},{5,7},{6,4},{7,5},{8,10},{9,11},{10,... | collective-permute-start | bytes 1572872 | tf_op jit(solution)/shard_map/ppermute | solution.py:81
  21.4 34.0 %collective-permute-start.2 = (bf16[128,2048]{1,0:T(8,128)(2,1)S(1)}, bf16[128,2048]{1,0:T(8,128)(2,1)S(1)}, u32[]{:S(2)}, u32[]{:S(2)}) collective-permute-start(bf16[128,2048]{1,0:T(8,128)(2,1)S(1)} %copy-done.2), channel_id=1, source_target_pairs={{0,3},{1,0},{2,1},{3,2},{4,7},{5,4},{6,5},{7,6},{8,11},{9,8},{10,9... | collective-permute-start | bytes 1572872 | tf_op jit(solution)/shard_map/ppermute | solution.py:81
  79.0 33.6 %collective-permute-start.6 = (bf16[128,2048]{1,0:T(8,128)(2,1)S(1)}, bf16[128,2048]{1,0:T(8,128)(2,1)S(1)}, u32[]{:S(2)}, u32[]{:S(2)}) collective-permute-start(bf16[128,2048]{1,0:T(8,128)(2,1)S(1)} %get-tuple-element.92), channel_id=1, source_target_pairs={{0,3},{1,0},{2,1},{3,2},{4,7},{5,4},{6,5},{7,6},{8,11},{9,8},{10,9... | collective-permute-start | bytes 1572872 | tf_op jit(solution)/shard_map/ppermute | solution.py:81
  91.4 69.8 %collective-permute-start.7 = (bf16[128,2048]{1,0:T(8,128)(2,1)S(1)}, bf16[128,2048]{1,0:T(8,128)(2,1)}, u32[]{:S(2)}, u32[]{:S(2)}) collective-permute-start(bf16[128,2048]{1,0:T(8,128)(2,1)S(1)} %get-tuple-element.93), channel_id=1, source_target_pairs={{0,2},{1,3},{2,0},{3,1},{4,6},{5,7},{6,4},{7,5},{8,10},{9,11},{10,... | collective-permute-start | bytes 1572872 | tf_op jit(solution)/shard_map/ppermute | solution.py:81
  92.0 69.1 %collective-permute-start.8 = (bf16[128,2048]{1,0:T(8,128)(2,1)S(1)}, bf16[128,2048]{1,0:T(8,128)(2,1)}, u32[]{:S(2)}, u32[]{:S(2)}) collective-permute-start(bf16[128,2048]{1,0:T(8,128)(2,1)S(1)} %get-tuple-element.94), channel_id=1, source_target_pairs={{0,1},{1,2},{2,3},{3,0},{4,5},{5,6},{6,7},{7,4},{8,9},{9,10},{10,1... | collective-permute-start | bytes 1572872 | tf_op jit(solution)/shard_map/ppermute | solution.py:81
  106.1 59.2 %collective-permute-start.15 = (bf16[128,2048]{1,0:T(8,128)(2,1)}, bf16[128,2048]{1,0:T(8,128)(2,1)S(1)}, u32[]{:S(2)}, u32[]{:S(2)}) collective-permute-start(bf16[128,2048]{1,0:T(8,128)(2,1)} %param.25), channel_id=1, source_target_pairs={{0,1},{1,2},{2,3},{3,0},{4,5},{5,6},{6,7},{7,4},{8,9},{9,10},{10,1... | collective-permute-start | bytes 1572872 | tf_op jit(solution)/shard_map/ppermute | solution.py:81
  109.0 85.7 %collective-permute-start.16 = (bf16[128,2048]{1,0:T(8,128)(2,1)}, bf16[128,2048]{1,0:T(8,128)(2,1)S(1)}, u32[]{:S(2)}, u32[]{:S(2)}) collective-permute-start(bf16[128,2048]{1,0:T(8,128)(2,1)} %param.25), channel_id=1, source_target_pairs={{0,2},{1,3},{2,0},{3,1},{4,6},{5,7},{6,4},{7,5},{8,10},{9,11},{10,... | collective-permute-start | bytes 1572872 | tf_op jit(solution)/shard_map/ppermute | solution.py:81
  112.6 83.0 %collective-permute-start.17 = (bf16[128,2048]{1,0:T(8,128)(2,1)}, bf16[128,2048]{1,0:T(8,128)(2,1)S(1)}, u32[]{:S(2)}, u32[]{:S(2)}) collective-permute-start(bf16[128,2048]{1,0:T(8,128)(2,1)} %param.25), channel_id=1, source_target_pairs={{0,3},{1,0},{2,1},{3,2},{4,7},{5,4},{6,5},{7,6},{8,11},{9,8},{10,9... | collective-permute-start | bytes 1572872 | tf_op jit(solution)/shard_map/ppermute | solution.py:81
  164.8 31.5 %collective-permute-start.12 = (bf16[128,2048]{1,0:T(8,128)(2,1)S(1)}, bf16[128,2048]{1,0:T(8,128)(2,1)S(1)}, u32[]{:S(2)}, u32[]{:S(2)}) collective-permute-start(bf16[128,2048]{1,0:T(8,128)(2,1)S(1)} %get-tuple-element.101.refs_0_), channel_id=1, source_target_pairs={{0,1},{1,2},{2,3},{3,0},{4,5},{5,6},{6,7},{7,4},{8,9},{9,10},{10,1... | collective-permute-start | bytes 1572872 | tf_op jit(solution)/shard_map/ppermute | solution.py:81
  164.8 52.3 %collective-permute-start.13 = (bf16[128,2048]{1,0:T(8,128)(2,1)S(1)}, bf16[128,2048]{1,0:T(8,128)(2,1)S(1)}, u32[]{:S(2)}, u32[]{:S(2)}) collective-permute-start(bf16[128,2048]{1,0:T(8,128)(2,1)S(1)} %get-tuple-element.101.refs_0_), channel_id=1, source_target_pairs={{0,2},{1,3},{2,0},{3,1},{4,6},{5,7},{6,4},{7,5},{8,10},{9,11},{10,... | collective-permute-start | bytes 1572872 | tf_op jit(solution)/shard_map/ppermute | solution.py:81
  165.4 52.6 %collective-permute-start.14 = (bf16[128,2048]{1,0:T(8,128)(2,1)S(1)}, bf16[128,2048]{1,0:T(8,128)(2,1)S(1)}, u32[]{:S(2)}, u32[]{:S(2)}) collective-permute-start(bf16[128,2048]{1,0:T(8,128)(2,1)S(1)} %get-tuple-element.101.refs_0_), channel_id=1, source_target_pairs={{0,3},{1,0},{2,1},{3,2},{4,7},{5,4},{6,5},{7,6},{8,11},{9,8},{10,9... | collective-permute-start | bytes 1572872 | tf_op jit(solution)/shard_map/ppermute | solution.py:81
  282.9 239.1 %reduce-scatter.5.cloned.1.call-start = ((), (), s32[]{:S(2)}) async-start(), calls=%async_computation.5 | async-start | bytes 5898240 | tf_op jit(solution)/shard_map/reduce_scatter | solution.py:462
  295.8 45.6 %collective-permute-start.19 = (bf16[128,2048]{1,0:T(8,128)(2,1)S(1)}, bf16[128,2048]{1,0:T(8,128)(2,1)S(1)}, u32[]{:S(2)}, u32[]{:S(2)}) collective-permute-start(bf16[128,2048]{1,0:T(8,128)(2,1)S(1)} %copy-done.23), channel_id=1, source_target_pairs={{0,2},{1,3},{2,0},{3,1},{4,6},{5,7},{6,4},{7,5},{8,10},{9,11},{10,... | collective-permute-start | bytes 1572872 | tf_op jit(solution)/shard_map/ppermute | solution.py:81
  295.8 45.6 %collective-permute-start.20 = (bf16[128,2048]{1,0:T(8,128)(2,1)S(1)}, bf16[128,2048]{1,0:T(8,128)(2,1)S(1)}, u32[]{:S(2)}, u32[]{:S(2)}) collective-permute-start(bf16[128,2048]{1,0:T(8,128)(2,1)S(1)} %copy-done.19), channel_id=1, source_target_pairs={{0,1},{1,2},{2,3},{3,0},{4,5},{5,6},{6,7},{7,4},{8,9},{9,10},{10,1... | collective-permute-start | bytes 1572872 | tf_op jit(solution)/shard_map/ppermute | solution.py:81
  345.6 37.1 %collective-permute-start.25 = (bf16[128,2048]{1,0:T(8,128)(2,1)S(1)}, bf16[128,2048]{1,0:T(8,128)(2,1)S(1)}, u32[]{:S(2)}, u32[]{:S(2)}) collective-permute-start(bf16[128,2048]{1,0:T(8,128)(2,1)S(1)} %get-tuple-element.135), channel_id=1, source_target_pairs={{0,2},{1,3},{2,0},{3,1},{4,6},{5,7},{6,4},{7,5},{8,10},{9,11},{10,... | collective-permute-start | bytes 1572872 | tf_op jit(solution)/shard_map/ppermute | solution.py:81
  347.4 35.4 %collective-permute-start.26 = (bf16[128,2048]{1,0:T(8,128)(2,1)S(1)}, bf16[128,2048]{1,0:T(8,128)(2,1)S(1)}, u32[]{:S(2)}, u32[]{:S(2)}) collective-permute-start(bf16[128,2048]{1,0:T(8,128)(2,1)S(1)} %get-tuple-element.135), channel_id=1, source_target_pairs={{0,3},{1,0},{2,1},{3,2},{4,7},{5,4},{6,5},{7,6},{8,11},{9,8},{10,9... | collective-permute-start | bytes 1572872 | tf_op jit(solution)/shard_map/ppermute | solution.py:81
  383.0 31.2 %collective-permute-start.29 = (bf16[128,2048]{1,0:T(8,128)(2,1)}, bf16[128,2048]{1,0:T(8,128)(2,1)}, u32[]{:S(2)}, u32[]{:S(2)}) collective-permute-start(bf16[128,2048]{1,0:T(8,128)(2,1)} %get-tuple-element.142), channel_id=1, source_target_pairs={{0,1},{1,2},{2,3},{3,0},{4,5},{5,6},{6,7},{7,4},{8,9},{9,10},{10,1... | collective-permute-start | bytes 1572872 | tf_op jit(solution)/shard_map/ppermute | solution.py:81
  394.3 35.5 %collective-permute-start.28 = (bf16[128,2048]{1,0:T(8,128)(2,1)}, bf16[128,2048]{1,0:T(8,128)(2,1)}, u32[]{:S(2)}, u32[]{:S(2)}) collective-permute-start(bf16[128,2048]{1,0:T(8,128)(2,1)} %get-tuple-element.141), channel_id=1, source_target_pairs={{0,2},{1,3},{2,0},{3,1},{4,6},{5,7},{6,4},{7,5},{8,10},{9,11},{10,... | collective-permute-start | bytes 1572872 | tf_op jit(solution)/shard_map/ppermute | solution.py:81
  396.4 33.4 %collective-permute-start.27 = (bf16[128,2048]{1,0:T(8,128)(2,1)}, bf16[128,2048]{1,0:T(8,128)(2,1)}, u32[]{:S(2)}, u32[]{:S(2)}) collective-permute-start(bf16[128,2048]{1,0:T(8,128)(2,1)} %get-tuple-element.140), channel_id=1, source_target_pairs={{0,3},{1,0},{2,1},{3,2},{4,7},{5,4},{6,5},{7,6},{8,11},{9,8},{10,9... | collective-permute-start | bytes 1572872 | tf_op jit(solution)/shard_map/ppermute | solution.py:81
  466.2 45.9 %collective-permute-start.31 = (bf16[128,2048]{1,0:T(8,128)(2,1)S(1)}, bf16[128,2048]{1,0:T(8,128)(2,1)S(1)}, u32[]{:S(2)}, u32[]{:S(2)}) collective-permute-start(bf16[128,2048]{1,0:T(8,128)(2,1)S(1)} %copy-done.17), channel_id=1, source_target_pairs={{0,2},{1,3},{2,0},{3,1},{4,6},{5,7},{6,4},{7,5},{8,10},{9,11},{10,... | collective-permute-start | bytes 1572872 | tf_op jit(solution)/shard_map/ppermute | solution.py:81
  466.6 45.5 %collective-permute-start.32 = (bf16[128,2048]{1,0:T(8,128)(2,1)S(1)}, bf16[128,2048]{1,0:T(8,128)(2,1)S(1)}, u32[]{:S(2)}, u32[]{:S(2)}) collective-permute-start(bf16[128,2048]{1,0:T(8,128)(2,1)S(1)} %copy-done.15), channel_id=1, source_target_pairs={{0,1},{1,2},{2,3},{3,0},{4,5},{5,6},{6,7},{7,4},{8,9},{9,10},{10,1... | collective-permute-start | bytes 1572872 | tf_op jit(solution)/shard_map/ppermute | solution.py:81
  (77 other events, 965.0 us)
Sparse Core Ops, SparseCore 0:
  10.5 43.9 all-gather.2
  56.3 125.3 all-gather.4
  283.0 130.4 reduce-scatter.2
  452.5 66.6 reduce-scatter.4

commit v3 on v2

--- a/solution.py
+++ b/solution.py
@@ -76,6 +76,7 @@
     def __init__(self, size):
         self.size = size
         self.index = lax.axis_index("tensor")
+        self.owners = lax.rem(self.index - jnp.arange(size, dtype=jnp.int32) + size, size)
 
     def shift(self, v, r):
         return lax.ppermute(v, "tensor", [(i, (i + r) % self.size) for i in range(self.size)])
@@ -95,24 +96,38 @@
         self.size = size
         self.me = lax.axis_index("dp")
         self.bits = [1 << b for b in range(size.bit_length() - 1)]
-        self.keys = [2 * q for q in range(size // 2)] + [2 * q + 1 for q in range(size // 2)]
 
     def swap(self, v, m):
         return lax.ppermute(v, "dp", [(i, i ^ m) for i in range(self.size)])
 
-    def gather_row(self, v):
-        width = v.shape[1]
+    def gather_columns(self, v):
         for m in self.bits:
-            v = jnp.concatenate([v, self.swap(v, m)], axis=1)
-        cuts = [lax.dynamic_slice_in_dim(v, (self.me ^ b) * width, width, 1) for b in range(self.size)]
-        return jnp.concatenate(cuts, axis=1)
-
-    def places(self):
-        return 2 * jnp.arange(self.size // 2, dtype=jnp.int32) + (self.me & 1)
-
-    def over_chips(self, own):
-        groups = [list(range(c, self.size, 2)) for c in range(2)]
-        return lax.psum_scatter(own, "dp", scatter_dimension=0, axis_index_groups=groups, tiled=True)
+            other = self.swap(v, m)
+            both = jnp.concatenate([v, other], axis=1), jnp.concatenate([other, v], axis=1)
+            v = jnp.where((self.me & m) == 0, *both)
+        return v
+
+    def places(self, half):
+        count = self.size // 2
+        bits = self.hops(half)
+        keys = [0]
+        for m in reversed(bits):
+            keys = keys + [k | m for k in keys]
+        return self.me ^ jnp.array(keys[:count], jnp.int32)
+
+    def hops(self, half):
+        return self.bits[1:] if half else self.bits[:0:-1]
+
+    def first_hop(self, pairs):
+        return [(keep, self.swap(send, self.hops(half)[0])) for half, (keep, send) in enumerate(pairs)]
+
+    def other_hops(self, pairs, order):
+        pairs = list(pairs)
+        for hop in range(1, len(self.bits) - 1):
+            totals = order(lambda *p: [total32(terms).astype(BF16) for terms in p], *pairs)
+            cut = totals[0].shape[0] // 2
+            pairs = [(t[:cut], self.swap(t[cut:], self.hops(half)[hop])) for half, t in enumerate(totals)]
+        return pairs
 
 
 class Order:
@@ -154,20 +169,21 @@
     return pl.BlockSpec(shape, lambda *_: (0,) * len(shape))
 
 
-def attention_in(x_blocks, gain, w, skip):
+def attention_in(x_blocks, gain, w, skip, owners):
     count = len(x_blocks)
     rows, features = x_blocks[0].shape
     total, width = rows * count, w.shape[1] - skip
     tile = math.gcd(math.gcd(width, skip), 256)
 
-    def body(*refs):
+    def body(owners_ref, *refs):
         x_refs, (gain_ref, w_ref, h_ref, out_ref) = refs[:count], refs[count:]
 
         @pl.when(pl.program_id(0) == 0)
         def _():
             for r in range(count):
                 normed, _ = norm_parts(x_refs[r][...].astype(F32))
-                h_ref[r * rows : (r + 1) * rows, :] = (normed * gain_ref[...]).astype(BF16)
+                at = pl.multiple_of(owners_ref[r] * rows, rows)
+                h_ref[pl.ds(at, rows), :] = (normed * gain_ref[...]).astype(BF16)
 
         out_ref[...] = mm(h_ref[...], w_ref[...])
 
@@ -175,34 +191,39 @@
         body,
         "attention_in",
         2 * total * features * width,
-        (*x_blocks, gain, w),
+        (owners, *x_blocks, gain, w),
         (jax.ShapeDtypeStruct((total, features), BF16), jax.ShapeDtypeStruct((total, width), F32)),
-        grid=(width // tile,),
-        in_specs=[whole((rows, features))] * count
-        + [whole((1, features)), pl.BlockSpec((features, tile), lambda j: (0, skip // tile + j))],
-        out_specs=[whole((total, features)), pl.BlockSpec((total, tile), lambda j: (0, j))],
-    )
-
-
-def feed_forward(h_blocks, c, w):
+        grid_spec=pltpu.PrefetchScalarGridSpec(
+            num_scalar_prefetch=1,
+            grid=(width // tile,),
+            in_specs=[whole((rows, features))] * count
+            + [whole((1, features)), pl.BlockSpec((features, tile), lambda j, _: (0, skip // tile + j))],
+            out_specs=[whole((total, features)), pl.BlockSpec((total, tile), lambda j, _: (0, j))],
+        ),
+    )
+
+
+def feed_forward(h_blocks, c_blocks, w, owners):
     count = len(h_blocks)
     rows, features = h_blocks[0].shape
     units = w.shape[1] // 3
     tile = tile_of(units, 256)
     steps = units // tile
 
-    def body(*refs):
-        h_refs = refs[:count]
-        c_ref, gate_ref, up_ref, down_ref, h_all, out_ref = refs[count:]
+    def body(owners_ref, *refs):
+        h_refs, c_refs = refs[:count], refs[count : 2 * count]
+        gate_ref, up_ref, down_ref, h_all, c_all, out_ref = refs[2 * count :]
 
         @pl.when(pl.program_id(0) == 0)
         def _():
             for r in range(count):
-                h_all[r * rows : (r + 1) * rows, :] = h_refs[r][...]
+                at = pl.multiple_of(owners_ref[r] * rows, rows)
+                h_all[pl.ds(at, rows), :] = h_refs[r][...]
+                c_all[pl.ds(at, rows), :] = c_refs[r][...]
 
         gate = mm(h_all[...], gate_ref[...])
         up = mm(h_all[...], up_ref[...])
-        grad_hidden = mm(c_ref[...], down_ref[...])
+        grad_hidden = mm(c_all[...], down_ref[...])
         sig = 1.0 / (1.0 + jnp.exp(-gate))
         silu = gate * sig
         out_ref[0] = (grad_hidden * up * (sig * (1.0 + gate * (1.0 - sig)))).astype(BF16)
@@ -210,69 +231,96 @@
         out_ref[2] = (silu * up).astype(BF16)
 
     total = rows * count
+    wide = jax.ShapeDtypeStruct((total, features), BF16)
     return kernel_call(
         body,
         "feed_forward",
         6 * total * features * units,
-        (*h_blocks, c, w, w, w),
-        (jax.ShapeDtypeStruct((total, features), BF16), jax.ShapeDtypeStruct((3, total, units), BF16)),
-        grid=(steps,),
-        in_specs=[whole((rows, features))] * count
-        + [whole((total, features))]
-        + [pl.BlockSpec((features, tile), lambda j, k=k: (0, k * steps + j)) for k in range(3)],
-        out_specs=[whole((total, features)), pl.BlockSpec((3, total, tile), lambda j: (0, 0, j))],
-    )
-
-
-def rows_product(a, leads, w, first, count, name):
+        (owners, *h_blocks, *c_blocks, w, w, w),
+        (wide, wide, jax.ShapeDtypeStruct((3, total, units), BF16)),
+        grid_spec=pltpu.PrefetchScalarGridSpec(
+            num_scalar_prefetch=1,
+            grid=(steps,),
+            in_specs=[whole((rows, features))] * (2 * count)
+            + [pl.BlockSpec((features, tile), lambda j, _, k=k: (0, k * steps + j)) for k in range(3)],
+            out_specs=[whole((total, features))] * 2 + [pl.BlockSpec((3, total, tile), lambda j, _: (0, 0, j))],
+        ),
+    )
+
+
+def rows_product(a, leads, w, first, name, owners=None):
     rows, units = a.shape[1:]
     features = w.shape[0]
     tile = tile_of(features, 256)
+    count = 1 if owners is None else owners.shape[0]
     block = rows // count
     width = units * len(leads)
     aligned = first % width == 0
 
-    def body(*refs):
-        a_refs, w_ref, outs = refs[: len(leads)], refs[len(leads)], refs[len(leads) + 1 :]
+    def body(owners_ref, *refs):
+        a_refs, w_ref, outs, turned = refs[: len(leads)], refs[len(leads)], refs[len(leads) + 1 : -1], refs[-1]
+        if owners is not None:
+
+            @pl.when(pl.program_id(0) == 0)
+            def _():
+                for r in range(count):
+                    at = pl.multiple_of(owners_ref[r] * block, block)
+                    for k in range(len(leads)):
+                        turned[k, r * block : (r + 1) * block, :] = a_refs[k][0, pl.ds(at, block), :]
+
         at = 0 if aligned else first
         acc = None
-        for a_ref in a_refs:
-            term = outer(a_ref[0], w_ref[:, at : at + units])
+        for k, a_ref in enumerate(a_refs):
+            term = outer(a_ref[0] if owners is None else turned[k], w_ref[:, at : at + units])
             acc = term if acc is None else acc + term
             at += units
         for r in range(count):
             outs[r][...] = acc[r * block : (r + 1) * block, :].astype(BF16)
 
-    spec = pl.BlockSpec((tile, width), lambda j: (j, first // width))
+    spec = pl.BlockSpec((tile, width), lambda j, _: (j, first // width))
     if not aligned:
-        spec = pl.BlockSpec((tile, w.shape[1]), lambda j: (j, 0))
-    return kernel_call(
+        spec = pl.BlockSpec((tile, w.shape[1]), lambda j, _: (j, 0))
+    outs = kernel_call(
         body,
         name,
         2 * rows * features * width,
-        [a] * len(leads) + [w],
+        [jnp.zeros((1,), jnp.int32) if owners is None else owners] + [a] * len(leads) + [w],
         [jax.ShapeDtypeStruct((block, features), BF16)] * count,
-        grid=(features // tile,),
-        in_specs=[pl.BlockSpec((1, rows, units), lambda j, k=k: (k, 0, 0)) for k in leads] + [spec],
-        out_specs=[pl.BlockSpec((block, tile), lambda j: (0, j))] * count,
-    )
-
-
-def weight_grad(sides, parts, places, pieces, most, name):
+        grid_spec=pltpu.PrefetchScalarGridSpec(
+            num_scalar_prefetch=1,
+            grid=(features // tile,),
+            in_specs=[pl.BlockSpec((1, rows, units), lambda j, _, k=k: (k, 0, 0)) for k in leads] + [spec],
+            out_specs=[pl.BlockSpec((block, tile), lambda j, _: (0, j))] * count,
+            scratch_shapes=[pltpu.VMEM((len(leads), rows, units) if owners is not None else (1, 16, 128), BF16)],
+        ),
+    )
+    return outs[0] if owners is None else outs
+
+
+def weight_grad(sides, parts, cube, most, name):
     terms = len(sides[0])
-    rows, width = sides[0][0].shape[0], sides[0][0].shape[1] // pieces
-    count = places.shape[0]
+    rows, width = sides[0][0].shape[0], sides[0][0].shape[1] // cube.size
+    count = cube.size // 2
     sizes = [n[0][0].shape[-1] for _, n in parts]
     tile = functools.reduce(math.gcd, sizes, most)
     starts = [0]
     for size in sizes:
         starts.append(starts[-1] + size // tile)
-    n_sides, n_parts = len(sides), len(parts)
+    n_sides, n_parts, steps = len(sides), len(parts), starts[-1]
+    half_steps = (steps + 1) // 2
+    bounds = [0, half_steps, steps]
+    place_a, place_b = ([0], [0])
+    for m in reversed(cube.hops(0)):
+        place_a = place_a + [k | m for k in place_a]
+    for m in reversed(cube.hops(1)):
+        place_b = place_b + [k | m for k in place_b]
+    order_b = [place_a.index(k) for k in place_b]
+    cut = count // 2
 
     def body(places_ref, *refs):
         d_refs = refs[: n_sides * terms * count]
         n_refs = refs[n_sides * terms * count :][: n_parts * terms]
-        out_ref, turned = refs[-2:]
+        outs, turned = refs[-5:-1], refs[-1]
         j = pl.program_id(0)
 
         @pl.when(j == 0)
@@ -282,14 +330,23 @@
                     turned[k, q * width : (q + 1) * width, :] = d_refs[k * count + q][...].T
 
         for p, (side, _) in enumerate(parts):
-
-            @pl.when((j >= starts[p]) & (j < starts[p + 1]))
-            def _(p=p, side=side):
-                acc = None
-                for t in range(terms):
-                    term = mm(turned[side * terms + t], n_refs[p * terms + t][0])
-                    acc = term if acc is None else acc + term
-                out_ref[...] = acc.astype(BF16)
+            for half in range(2):
+                first, last = max(starts[p], bounds[half]), min(starts[p + 1], bounds[half + 1])
+                if first >= last:
+                    continue
+
+                @pl.when((j >= first) & (j < last))
+                def _(p=p, side=side, half=half):
+                    acc = None
+                    for t in range(terms):
+                        term = mm(turned[side * terms + t], n_refs[p * terms + t][0])
+                        acc = term if acc is None else acc + term
+                    acc = acc.astype(BF16)
+                    for to in range(count):
+                        q = order_b[to] if half else to
+                        out = outs[2 * half + to // cut]
+                        at = to % cut
+                        out[at * width : (at + 1) * width, :] = acc[q * width : (q + 1) * width, :]
 
     def n_spec(p, lead):
         last = starts[p + 1] - starts[p] - 1
@@ -299,22 +356,27 @@
         pl.BlockSpec((rows, width), lambda j, p, q=q: (0, p[q])) for _ in range(n_sides * terms) for q in range(count)
     ]
     in_specs += [n_spec(p, lead) for p, (_, n) in enumerate(parts) for _, lead in n]
-    operands = [places] + [d for side in sides for d in side for _ in range(count)]
+    operands = [cube.places(0)] + [d for side in sides for d in side for _ in range(count)]
     operands += [a for _, n in parts for a, _ in n]
-    return kernel_call(
+    out_a = jax.ShapeDtypeStruct((cut * width, half_steps * tile), BF16)
+    out_b = jax.ShapeDtypeStruct((cut * width, (steps - half_steps) * tile), BF16)
+    spec_a = pl.BlockSpec((cut * width, tile), lambda j, _: (0, jnp.minimum(j, half_steps - 1)))
+    spec_b = pl.BlockSpec((cut * width, tile), lambda j, _: (0, jnp.maximum(j - half_steps, 0)))
+    keep_a, send_a, keep_b, send_b = kernel_call(
         body,
         name,
-        2 * terms * rows * count * width * starts[-1] * tile,
+        2 * terms * rows * count * width * steps * tile,
         operands,
-        jax.ShapeDtypeStruct((count * width, starts[-1] * tile), BF16),
+        [out_a, out_a, out_b, out_b],
         grid_spec=pltpu.PrefetchScalarGridSpec(
             num_scalar_prefetch=1,
-            grid=(starts[-1],),
+            grid=(steps,),
             in_specs=in_specs,
-            out_specs=pl.BlockSpec((count * width, tile), lambda j, _: (0, j)),
+            out_specs=[spec_a, spec_a, spec_b, spec_b],
             scratch_shapes=[pltpu.VMEM((n_sides * terms, count * width, rows), BF16)],
         ),
     )
+    return (keep_a, send_a), (keep_b, send_b)
 
 
 def attention_masked(queries, keys_all, segment, place):
@@ -351,23 +413,23 @@
     width_out, units = w_out.shape[0], w_gate.shape[1]
 
     rows_all = line.gather(tokens)
-    gain_one = cube.gather_row(attn_gain[None, :]).astype(F32)
+    gains = cube.gather_columns(jnp.stack([attn_gain, mlp_gain])).astype(F32)
+    gain_one, gain_two = gains[:1], gains[1:]
     w_attn = lax.all_gather(jnp.concatenate([w_out.T, w_query, w_key, w_value], axis=1), "dp", axis=0, tiled=True)
-    gain_two = cube.gather_row(mlp_gain[None, :]).astype(F32)
     w_mlp = lax.all_gather(jnp.concatenate([w_gate, w_up, w_down.T], axis=1), "dp", axis=0, tiled=True)
-    incoming = jnp.concatenate(line.gather(after(cotangent, *rows_all)), axis=0)
-    incoming_other = cube.swap(incoming, 1)
+    incoming_blocks = line.gather(after(cotangent, *rows_all))
 
     order = Order()
-    attn_input, qkv = order(lambda *a: attention_in(a[:-2], a[-2], a[-1], width_out), *rows_all, gain_one, w_attn)
+    attn_input, qkv = order(
+        lambda *a: attention_in(a[:-2], a[-2], a[-1], width_out, line.owners), *rows_all, gain_one, w_attn
+    )
+    attn_input_other = cube.swap(attn_input, 1)
     tokens_f = tokens.astype(F32)
     normed_one, factor_one = norm_parts(tokens_f)
     heads_here = width_q // HEAD_DIM
     kv_here = width_k // HEAD_DIM
     head_group = heads_here // kv_here
-    row = jnp.arange(row_count, dtype=jnp.int32)
-    owner = lax.rem(line.index - row // own_rows + tensor_size, tensor_size)
-    place = owner * own_rows + row % own_rows
+    place = jnp.arange(row_count, dtype=jnp.int32)
     segment, position = layout(seq_lengths, seq_group, cube.me, place)
     cosine_table, sine_table = rope_tables(position, HEAD_DIM)
     queries = (
@@ -389,42 +451,40 @@
     log_mass = row_max + jnp.log(row_sum)
 
     out_parts = order(
-        lambda a, w: rows_product(a, [0], w, 0, tensor_size, "attention_out"), attended[None], w_attn
-    )
+        lambda a, w: rows_product(a, [0], w, 0, "attention_out", line.owners),
+        after(attended, *incoming_blocks[1:3])[None],
+        w_attn,
+    )
+    attended_other = cube.swap(attended, 1)
     residual = order(lambda x, *terms: x + total32(terms), tokens_f, *line.scatter(out_parts))
     normed_two, factor_two = norm_parts(residual)
     mlp_blocks = line.gather((normed_two * gain_two).astype(BF16))
 
-    mlp_input, unit_grads = order(feed_forward, mlp_blocks, incoming, w_mlp)
-    mlp_input_other, unit_grads_other = cube.swap(mlp_input, 1), cube.swap(unit_grads, 1)
-    two_parts = order(
-        lambda a, w: rows_product(a, [0, 1], w, 0, tensor_size, "feed_forward_rows_grad"), unit_grads, w_mlp
-    )
-    two_terms = line.scatter(two_parts)
-
-    def mlp_grad(h, h_other, c, c_other, n, n_other):
+    mlp_input, incoming, unit_grads = order(
+        lambda h, c, w: feed_forward(h, c, w, line.owners), mlp_blocks, incoming_blocks, w_mlp
+    )
+    mlp_others = [cube.swap(v, 1) for v in (mlp_input, incoming, unit_grads)]
+    two_parts = order(lambda a, w: rows_product(a, [0, 1], w, 0, "feed_forward_rows_grad"), unit_grads, w_mlp)
+    two_sum = lax.psum_scatter(two_parts, "tensor", scatter_dimension=0, tiled=True)
+
+    def mlp_grad(h, c, n, h_other, c_other, n_other):
         parts = [(side, [(n, lead), (n_other, lead)]) for side, lead in ((0, 0), (0, 1), (1, 2))]
-        sides = [[h, h_other], [c, c_other]]
-        return weight_grad(sides, parts, cube.places(), dp_size, 512, "feed_forward_grad")
-
-    mlp_sum = cube.over_chips(
-        order(mlp_grad, mlp_input, mlp_input_other, incoming, incoming_other, unit_grads, unit_grads_other)
-    )
-
+        return weight_grad([[h, h_other], [c, c_other]], parts, cube, 512, "feed_forward_grad")
+
+    mlp_pairs = cube.first_hop(order(mlp_grad, mlp_input, incoming, unit_grads, *mlp_others))
     grad_residual = order(
-        lambda c, g, n, f, *terms: c.astype(F32) + norm_back(total32(terms), g, n, f),
+        lambda c, g, n, f, t: c.astype(F32) + norm_back(t.astype(F32), g, n, f),
         cotangent,
         gain_two,
         normed_two,
         factor_two,
-        *two_terms,
-    )
-    gathered = line.gather(grad_residual.astype(BF16))
-    block_parts = order(
-        lambda a, w: rows_product(a, [2], w, 2 * units, tensor_size, "block_out"), unit_grads, w_mlp
-    )
-    grad_attn_rows = order(lambda *b: jnp.concatenate(b, axis=0), *gathered)
-    block_terms = line.scatter(lax.optimization_barrier((block_parts, grad_attn_rows))[0])
+        two_sum,
+    )
+    grad_attn_rows = lax.all_gather(grad_residual.astype(BF16), "tensor", axis=0, tiled=True)
+    block_parts = order(lambda a, w: rows_product(a, [2], w, 2 * units, "block_out"), unit_grads, w_mlp)
+    block_parts, grad_attn_rows = lax.optimization_barrier((block_parts, grad_attn_rows))
+    block_sum = lax.psum_scatter(block_parts, "tensor", scatter_dimension=0, tiled=True)
+    rows_other = cube.swap(grad_attn_rows, 1)
 
     grad_attended = mm(grad_attn_rows, w_attn[:, :width_out]).astype(BF16)
     grad_block = grad_attended.reshape(row_count, kv_here, head_group, HEAD_DIM)
@@ -447,49 +507,57 @@
         [grad_queries, grad_keys, grad_values.astype(BF16).reshape(row_count, width_k)], axis=1
     )
     one_parts = order(
-        lambda a, w: rows_product(a, [0], w, width_out, tensor_size, "attention_rows_grad"),
-        after(grad_qkv, *block_terms)[None],
-        w_attn,
-    )
-    one_terms = line.scatter(one_parts)
-
-    def attn_grad(y, h, a, g):
-        parts = [(0, [(a[None], 0)]), (1, [(g[None], 0)])]
-        places = jnp.arange(dp_size, dtype=jnp.int32)
-        return weight_grad([[y], [h]], parts, places, dp_size, 256, "attention_grad")
-
-    attn_terms = order(attn_grad, grad_attn_rows, attn_input, attended, grad_qkv)
-    attn_sum = lax.psum_scatter(after(attn_terms, mlp_sum), "dp", scatter_dimension=0, tiled=True)
-    mlp_sum = mlp_sum.astype(F32)
-    gate_grad, up_grad, down_grad = mlp_sum[:, :units], mlp_sum[:, units : 2 * units], mlp_sum[:, 2 * units :].T
-    block_out = (residual + total32(block_terms)).astype(BF16)
-    attn_sum = attn_sum.astype(F32)
+        lambda a, w: rows_product(a, [0], w, width_out, "attention_rows_grad"), grad_qkv[None], w_attn
+    )
+    one_sum = lax.psum_scatter(after(one_parts, block_sum), "tensor", scatter_dimension=0, tiled=True)
+
+    def attn_grad(y, y_other, h, h_other, a, a_other, g, g_other):
+        parts = [(0, [(a[None], 0), (a_other[None], 0)]), (1, [(g[None], 0), (g_other[None], 0)])]
+        return weight_grad([[y, y_other], [h, h_other]], parts, cube, 256, "attention_grad")
+
+    attn_pairs = cube.first_hop(
+        order(
+            attn_grad,
+            grad_attn_rows,
+            rows_other,
+            attn_input,
+            attn_input_other,
+            attended,
+            attended_other,
+            grad_qkv,
+            cube.swap(grad_qkv, 1),
+        )
+    )
+    block_out = order(lambda x, t: (x + t.astype(F32)).astype(BF16), residual, block_sum)
+    mlp_terms = cube.other_hops(mlp_pairs, order)
+    attn_terms = cube.other_hops(attn_pairs, order)
+
+    def gain_terms(*pairs):
+        return functools.reduce(lambda a, b: a + b, [jnp.sum(w.astype(F32) * g, axis=1) for w, g in pairs])
+
+    def mlp_finals(terms, gate, up):
+        sums = jnp.concatenate([total32(t) for t in terms], axis=1)
+        gate_grad, up_grad, down_grad = sums[:, :units], sums[:, units : 2 * units], sums[:, 2 * units :].T
+        return gain_terms((gate, gate_grad), (up, up_grad)), gate_grad, up_grad, down_grad
+
+    mlp_gain_terms, gate_grad, up_grad, down_grad = order(mlp_finals, mlp_terms, w_gate, w_up)
+    grad_tokens = order(
+        lambda c, g, n, f, t: (c + norm_back(t.astype(F32), g, n, f)).astype(BF16),
+        grad_residual,
+        gain_one,
+        normed_one,
+        factor_one,
+        one_sum,
+    )
+    attn_sum = jnp.concatenate([total32(t) for t in attn_terms], axis=1)
     out_grad, qkv_grad = attn_sum[:, :width_out].T, attn_sum[:, width_out:]
     query_grad = qkv_grad[:, :width_q]
     key_grad = qkv_grad[:, width_q : width_q + width_k]
     value_grad = qkv_grad[:, width_q + width_k :]
-
-    def gain_terms(*pairs):
-        return functools.reduce(lambda a, b: a + b, [jnp.sum(w.astype(F32) * g, axis=1) for w, g in pairs])
-
-    gain_sums = line.total(
-        jnp.stack(
-            [
-                gain_terms((w_query, query_grad), (w_key, key_grad), (w_value, value_grad)),
-                gain_terms((w_gate, gate_grad), (w_up, up_grad)),
-            ]
-        )
-    )
+    attn_gain_terms = gain_terms((w_query, query_grad), (w_key, key_grad), (w_value, value_grad))
+    gain_sums = line.total(jnp.stack([attn_gain_terms, mlp_gain_terms]))
     attn_gain_grad = gain_sums[0] / attn_gain.astype(F32)
     mlp_gain_grad = gain_sums[1] / mlp_gain.astype(F32)
-    grad_tokens = order(
-        lambda c, g, n, f, *terms: (c + norm_back(total32(terms), g, n, f)).astype(BF16),
-        grad_residual,
-        gain_one,
-        normed_one,
-        factor_one,
-        *one_terms,
-    )
     return (
         block_out,
         grad_tokens,

time: 541 us -> 497 us (0.919); the launches traced: 540 us -> 487 us
  waiting for transfers between devices: 242 us -> 199 us
  starting transfers between devices: 83.8 us -> 63.2 us
    ppermute x27 -> x15, waiting for transfers between devices: 238 us -> 97.5 us  [shift(): lax.ppermute(v, 'tensor', [(i, (i + r) % self.size) for i in range(self.s...]
    ppermute x9 -> x18, waiting for transfers between devices: 3.59 us -> 48.1 us  [swap(): return lax.ppermute(v, 'dp', [(i, i ^ m) for i in range(self.size)])]
    ppermute x27 -> x15, starting transfers between devices: 77.3 us -> 45.6 us  [shift(): lax.ppermute(v, 'tensor', [(i, (i + r) % self.size) for i in range(self.s...]
    all_gather x0 -> x1, waiting for transfers between devices: none -> 28.5 us  [per_device(): lax.all_gather(grad_residual.astype(BF16), 'tensor', axis=0, tiled=True)]
    reduce_scatter x2 -> x3, waiting for transfers between devices: 0.04 us -> 24.9 us  [the longest x1 24.8 us: per_device(): lax.psum_scatter(two_parts, 'tensor', scatter_dimension=0, tiled=True)]
    ppermute x9 -> x18, starting transfers between devices: 6.29 us -> 17.1 us  [swap(): return lax.ppermute(v, 'dp', [(i, i ^ m) for i in range(self.size)])]
    unnamed x158 -> x108, local copies, waits for them, and re-layouts: 42.4 us -> 32.3 us
    convert_element_type x8, other arithmetic: 8.76 us -> 15.7 us  [the longest x4 8.47 us: other_hops(): total32(terms).astype(BF16)]
  transfers between devices with their start and end apart: 40 -> 39, of which waited for: 15 -> 18; matrix products, arithmetic and copies ran while one was open for 14% -> 15% of each run, Pallas kernels for 9% -> 16%
where the time goes in v3:
time: 497 us; the launch traced here: 487 us
  waiting for transfers between devices  199 us (40%)
  Pallas kernels  99 us (20%)
  starting transfers between devices  63.2 us (13%)
  local copies, waits for them, and re-layouts  48.6 us (10%)
  other arithmetic  43.6 us (9%)
  matrix products  18.4 us (4%)
  between operations  15.3 us (3%)
    pallas_call x8, Pallas kernels, kernel_call(): pl.pallas_call(body, out_shape=out_shape, name=name, cost_estimate=pl.Cos...  99 us
    ppermute x15, waiting for transfers between devices, shift(): lax.ppermute(v, 'tensor', [(i, (i + r) % self.size) for i in range(self.s...  97.5 us
    ppermute x18, waiting for transfers between devices, swap(): return lax.ppermute(v, 'dp', [(i, i ^ m) for i in range(self.size)])  48.1 us
    ppermute x15, starting transfers between devices, shift(): lax.ppermute(v, 'tensor', [(i, (i + r) % self.size) for i in range(self.s...  45.6 us
    unnamed x108, local copies, waits for them, and re-layouts  32.3 us
    all_gather x1, waiting for transfers between devices, per_device(): lax.all_gather(grad_residual.astype(BF16), 'tensor', axis=0, tiled=True)  28.5 us
    reduce_scatter x1, waiting for transfers between devices, per_device(): lax.psum_scatter(two_parts, 'tensor', scatter_dimension=0, tiled=True)  24.8 us
    ppermute x18, starting transfers between devices, swap(): return lax.ppermute(v, 'dp', [(i, i ^ m) for i in range(self.size)])  17.1 us
  transfers between devices with their start and end apart: 39, of which 18 were waited for; matrix products, arithmetic and copies ran while one was open for 15% of the time, Pallas kernels for 16%

profile of v3, /device:TPU:0, one launch (start us, length us, event | category | flops | bytes accessed | tf_op | source)
XLA Modules:
  0.0 487.2 jit_solution(18356235166259908828)
XLA Ops:
  35.4 20.8 %collective-permute-done.1.refs_2_ = bf16[128,2048]{1,0:T(8,128)(2,1)S(1)} collective-permute-done((bf16[128,2048]{1,0:T(8,128)(2,1)S(1)}, bf16[128,2048]{1,0:T(8,128)(2,1)S(1)}, u32[]{:S(2)}, u32[]{:S(2)}) %collective-permute-start.1) | collective-permute-done | bytes 524320 | tf_op jit(solution)/shard_map/ppermute | solution.py:82
  57.9 10.9 %collective-permute-start.6 = (bf16[128,2048]{1,0:T(8,128)(2,1)S(1)}, bf16[128,2048]{1,0:T(8,128)(2,1)}, u32[]{:S(2)}, u32[]{:S(2)}) collective-permute-start(bf16[128,2048]{1,0:T(8,128)(2,1)S(1)} %copy-done.5), channel_id=1, source_target_pairs={{0,1},{1,2},{2,3},{3,0},{4,5},{5,6},{6,7},{7,4},{8,9},{9,10},{10,1... | collective-permute-start | bytes 1572872 | tf_op jit(solution)/shard_map/ppermute | solution.py:82
  74.3 5.3 %attention_in.1 = (bf16[512,2048]{1,0:T(8,128)(2,1)S(1)}, f32[512,768]{1,0:T(8,128)S(1)}) custom-call(s32[4]{0:T(128)S(1)} %compare_select_fusion.owners_ref, bf16[128,2048]{1,0:T(8,128)(2,1)S(1)} %copy-done.3, bf16[128,2048]{1,0:T(8,128)(2,1)S(1)} %copy-done.18, bf16[128,2048]{1,0:T(8,128)(2,1)S(1)} %copy-done.20, bf16[128,2048]{1,0:T(8,128)(2,1)S(1)} %copy-done.22, ...), custom_call_target="tpu_custom_call" | custom-call | flops 1610612736 | bytes 11018256 | tf_op jit(solution)/shard_map/attention_in/pallas_call | solution.py:158
  96.2 8.0 %collective-permute-done.7.refs_6_ = bf16[128,2048]{1,0:T(8,128)(2,1)} collective-permute-done((bf16[128,2048]{1,0:T(8,128)(2,1)S(1)}, bf16[128,2048]{1,0:T(8,128)(2,1)}, u32[]{:S(2)}, u32[]{:S(2)}) %collective-permute-start.7) | collective-permute-done | bytes 524320 | tf_op jit(solution)/shard_map/ppermute | solution.py:82
  107.3 6.5 %attention_out.1 = (bf16[128,2048]{1,0:T(8,128)(2,1)S(1)}, bf16[128,2048]{1,0:T(8,128)(2,1)S(1)}, bf16[128,2048]{1,0:T(8,128)(2,1)S(1)}, bf16[128,2048]{1,0:T(8,128)(2,1)S(1)}) custom-call(s32[4]{0:T(128)S(1)} %compare_select_fusion.owners_ref, bf16[1,512,512]{2,1,0:T(8,128)(2,1)S(1)} %bitcast.93, bf16[2048,1280]{1,0:T(8,128)(2,1)} %all-gather.4.cloned.1.call-done.refs_5_.refs_1_), custom_call_target="tpu_custom_call" | custom-call | flops 1073741824 | bytes 7864336 | tf_op jit(solution)/shard_map/attention_out/pallas_call | solution.py:158
  119.4 11.0 %collective-permute-done.8 = bf16[128,2048]{1,0:T(8,128)(2,1)S(1)} collective-permute-done((bf16[128,2048]{1,0:T(8,128)(2,1)S(1)}, bf16[128,2048]{1,0:T(8,128)(2,1)S(1)}, u32[]{:S(2)}, u32[]{:S(2)}) %collective-permute-start.8) | collective-permute-done | bytes 524320 | tf_op jit(solution)/shard_map/ppermute | solution.py:82
  130.4 30.0 %collective-permute-done.9 = bf16[128,2048]{1,0:T(8,128)(2,1)S(1)} collective-permute-done((bf16[128,2048]{1,0:T(8,128)(2,1)S(1)}, bf16[128,2048]{1,0:T(8,128)(2,1)S(1)}, u32[]{:S(2)}, u32[]{:S(2)}) %collective-permute-start.9) | collective-permute-done | bytes 524320 | tf_op jit(solution)/shard_map/ppermute | solution.py:82
  162.3 11.8 %collective-permute-start.11 = (bf16[128,2048]{1,0:T(8,128)(2,1)S(1)}, bf16[128,2048]{1,0:T(8,128)(2,1)S(1)}, u32[]{:S(2)}, u32[]{:S(2)}) collective-permute-start(bf16[128,2048]{1,0:T(8,128)(2,1)S(1)} %get-tuple-element.110.refs_0_), channel_id=1, source_target_pairs={{0,1},{1,2},{2,3},{3,0},{4,5},{5,6},{6,7},{7,4},{8,9},{9,10},{10,1... | collective-permute-start | bytes 1572872 | tf_op jit(solution)/shard_map/ppermute | solution.py:82
  180.7 5.8 %collective-permute-done.11.refs_1_ = bf16[128,2048]{1,0:T(8,128)(2,1)S(1)} collective-permute-done((bf16[128,2048]{1,0:T(8,128)(2,1)S(1)}, bf16[128,2048]{1,0:T(8,128)(2,1)S(1)}, u32[]{:S(2)}, u32[]{:S(2)}) %collective-permute-start.11) | collective-permute-done | bytes 524320 | tf_op jit(solution)/shard_map/ppermute | solution.py:82
  187.3 18.1 %collective-permute-done.12.refs_2_ = bf16[128,2048]{1,0:T(8,128)(2,1)S(1)} collective-permute-done((bf16[128,2048]{1,0:T(8,128)(2,1)S(1)}, bf16[128,2048]{1,0:T(8,128)(2,1)S(1)}, u32[]{:S(2)}, u32[]{:S(2)}) %collective-permute-start.12) | collective-permute-done | bytes 524320 | tf_op jit(solution)/shard_map/ppermute | solution.py:82
  213.7 21.3 %feed_forward.1 = (bf16[512,2048]{1,0:T(8,128)(2,1)}, bf16[512,2048]{1,0:T(8,128)(2,1)}, bf16[3,512,2048]{2,1,0:T(8,128)(2,1)}) custom-call(s32[4]{0:T(128)S(1)} %compare_select_fusion.owners_ref, bf16[128,2048]{1,0:T(8,128)(2,1)S(1)} %copy-done.7, bf16[128,2048]{1,0:T(8,128)(2,1)S(1)} %copy-done.12, bf16[128,2048]{1,0:T(8,128)(2,1)S(1)} %copy-done.14, ...), custom_call_target="tpu_custom_call" | custom-call | flops 12884901888 | bytes 90177552 | tf_op jit(solution)/shard_map/feed_forward/pallas_call | solution.py:158
  235.0 14.4 %feed_forward_rows_grad.1 = bf16[512,2048]{1,0:T(8,128)(2,1)S(1)} custom-call(s32[1]{0:T(128)} %constant.55.clone.1.owners_ref, bf16[3,512,2048]{2,1,0:T(8,128)(2,1)} %get-tuple-element.136.refs_0_.refs_1_.refs_16_.refs_18_.refs_20_, bf16[3,512,2048]{2,1,0:T(8,128)(2,1)} %get-tuple-element.136.refs_0_.refs_1_.refs_16_.refs_18_.refs_20_, ...), custom_call_target="tpu_custom_call" | custom-call | flops 8589934592 | bytes 39845892 | tf_op jit(solution)/shard_map/feed_forward_rows_grad/pallas_call | solution.py:158
  251.4 3.9 collective-permute-done.15.refs_4_.refs_5_.refs_6_.refs_7_
  261.2 23.9 %feed_forward_grad.1 = (bf16[512,3072]{1,0:T(8,128)(2,1)}, bf16[512,3072]{1,0:T(8,128)(2,1)}, bf16[512,3072]{1,0:T(8,128)(2,1)}, bf16[512,3072]{1,0:T(8,128)(2,1)}) custom-call(s32[4]{0:T(128)S(1)} %multiply_xor_fusion.places_ref, bf16[512,2048]{1,0:T(8,128)(2,1)S(1)} %copy-done.1, bf16[512,2048]{1,0:T(8,128)(2,1)S(1)} %copy-done.1, ...), custom_call_target="tpu_custom_call" | custom-call | flops 12884901888 | bytes 83886096 | tf_op jit(solution)/shard_map/feed_forward_grad/pallas_call | solution.py:158
  285.1 24.8 %reduce-scatter.4.cloned.1.call-done = bf16[128,2048]{1,0:T(8,128)(2,1)} async-done(((bf16[512,2048]{1,0:T(8,128)(2,1)}), bf16[128,2048]{1,0:T(8,128)(2,1)}) %reduce-scatter.4.cloned.1.call-update) | async-done | bytes 524304 | tf_op jit(solution)/shard_map/reduce_scatter | solution.py:468
  320.1 9.9 %block_out.1 = bf16[512,2048]{1,0:T(8,128)(2,1)S(1)} custom-call(s32[1]{0:T(128)} %constant.55.clone.1.owners_ref, bf16[3,512,2048]{2,1,0:T(8,128)(2,1)} %get-tuple-element.136.refs_0_.refs_1_.refs_16_.refs_18_.refs_20_, bf16[2048,6144]{1,0:T(8,128)(2,1)} %all-gather.6.cloned.1.call-done.refs_8_.refs_9_.refs_10_.refs_2_.refs_1_), custom_call_target="tpu_custom_call" | custom-call | flops 4294967296 | bytes 33554436 | tf_op jit(solution)/shard_map/block_out/pallas_call | solution.py:158
  331.3 28.5 %all-gather.8.cloned.1.call-done.refs_0_.refs_1_.refs_2_.refs_3_ = bf16[512,2048]{1,0:T(8,128)(2,1)} async-done(((bf16[128,2048]{1,0:T(8,128)(2,1)}), bf16[512,2048]{1,0:T(8,128)(2,1)}) %all-gather.8.cloned.1.call-update) | async-done | bytes 2097168 | tf_op jit(solution)/shard_map/all_gather | solution.py:483
  363.7 5.3 %fusion = (f32[2,4,512]{2,1,0:T(4,128)S(1)}, f32[2,512,512,4]{2,1,3,0:T(8,128)S(1)}) fusion(f32[2,4,512,512]{2,3,1,0:T(8,128)} %copy-done.23, f32[2,4,512]{2,1,0:T(4,128)S(1)} %bitcast.117, bf16[512,2,64,1]{0,2,3,1:T(8,128)(2,1)S(1)} %bitcast.114, bf16[512,2,4,64]{0,3,2,1:T(8,128)(2,1)S(1)} %bitcast.104), kind=kOutput, calls=%fused_computation.2 | convolution fusion | flops 274722816 | bytes 17465344 | tf_op jit(solution)/shard_map/qcgd,kcd->cgqk/dot_general | solution.py:494
  383.1 7.8 %attention_rows_grad.1 = bf16[512,2048]{1,0:T(8,128)(2,1)} custom-call(s32[1]{0:T(128)} %constant.55.clone.1.owners_ref, bf16[1,512,768]{2,1,0:T(8,128)(2,1)S(1)} %get-tuple-element.140.refs_0_, bf16[2048,1280]{1,0:T(8,128)(2,1)} %all-gather.4.cloned.1.call-done.refs_5_.refs_1_), custom_call_target="tpu_custom_call" | custom-call | flops 1610612736 | bytes 8126468 | tf_op jit(solution)/shard_map/attention_rows_grad/pallas_call | solution.py:158
  392.2 9.9 %attention_grad.1 = (bf16[512,768]{1,0:T(8,128)(2,1)S(1)}, bf16[512,768]{1,0:T(8,128)(2,1)}, bf16[512,512]{1,0:T(8,128)(2,1)S(1)}, bf16[512,512]{1,0:T(8,128)(2,1)}) custom-call(s32[4]{0:T(128)S(1)} %multiply_xor_fusion.places_ref, bf16[512,2048]{1,0:T(8,128)(2,1)} %all-gather.8.cloned.1.call-done.refs_0_.refs_1_.refs_2_.refs_3_, ...), custom_call_target="tpu_custom_call" | custom-call | flops 2684354560 | bytes 38797328 | tf_op jit(solution)/shard_map/attention_grad/pallas_call | solution.py:158
  407.5 4.0 add_convert_fusion.1
  418.6 4.1 collective-permute-done.22
  428.1 33.0 %collective-permute-done.27 = bf16[256,512]{1,0:T(8,128)(2,1)S(1)} collective-permute-done((bf16[256,512]{1,0:T(8,128)(2,1)S(1)}, bf16[256,512]{1,0:T(8,128)(2,1)S(1)}, u32[]{:S(2)}, u32[]{:S(2)}) %collective-permute-start.27) | collective-permute-done | bytes 262176 | tf_op jit(solution)/shard_map/ppermute | solution.py:101
  464.5 3.6 multiply_reduce_fusion
  (262 shorter events, 149.2 us)
Async XLA Ops:
  7.2 64.0 %all-gather.4.cloned.1.call-start = ((), (), s32[]{:S(2)}) async-start(), calls=%async_computation.3 | async-start | bytes 5898240 | tf_op jit(solution)/shard_map/all_gather | solution.py:418
  10.4 198.0 %all-gather.6.cloned.1.call-start = ((), (), s32[]{:S(2)}) async-start(), calls=%async_computation.4 | async-start | bytes 28311552 | tf_op jit(solution)/shard_map/all_gather | solution.py:419
  15.7 294.2 %reduce-scatter.4.cloned.1.call-start = ((), (), s32[]{:S(2)}) async-start(), calls=%async_computation.5 | async-start | bytes 2621440 | tf_op jit(solution)/shard_map/reduce_scatter | solution.py:468
  19.7 36.6 %collective-permute-start.1 = (bf16[128,2048]{1,0:T(8,128)(2,1)S(1)}, bf16[128,2048]{1,0:T(8,128)(2,1)S(1)}, u32[]{:S(2)}, u32[]{:S(2)}) collective-permute-start(bf16[128,2048]{1,0:T(8,128)(2,1)S(1)} %copy-done.3), channel_id=1, source_target_pairs={{0,2},{1,3},{2,0},{3,1},{4,6},{5,7},{6,4},{7,5},{8,10},{9,11},{10,... | collective-permute-start | bytes 1572872 | tf_op jit(solution)/shard_map/ppermute | solution.py:82
  22.3 34.8 %collective-permute-start.2 = (bf16[128,2048]{1,0:T(8,128)(2,1)S(1)}, bf16[128,2048]{1,0:T(8,128)(2,1)S(1)}, u32[]{:S(2)}, u32[]{:S(2)}) collective-permute-start(bf16[128,2048]{1,0:T(8,128)(2,1)S(1)} %copy-done.3), channel_id=1, source_target_pairs={{0,3},{1,0},{2,1},{3,2},{4,7},{5,4},{6,5},{7,6},{8,11},{9,8},{10,9... | collective-permute-start | bytes 1572872 | tf_op jit(solution)/shard_map/ppermute | solution.py:82
  57.9 38.3 %collective-permute-start.6 = (bf16[128,2048]{1,0:T(8,128)(2,1)S(1)}, bf16[128,2048]{1,0:T(8,128)(2,1)}, u32[]{:S(2)}, u32[]{:S(2)}) collective-permute-start(bf16[128,2048]{1,0:T(8,128)(2,1)S(1)} %copy-done.5), channel_id=1, source_target_pairs={{0,1},{1,2},{2,3},{3,0},{4,5},{5,6},{6,7},{7,4},{8,9},{9,10},{10,1... | collective-permute-start | bytes 1572872 | tf_op jit(solution)/shard_map/ppermute | solution.py:82
  68.8 35.4 %collective-permute-start.7 = (bf16[128,2048]{1,0:T(8,128)(2,1)S(1)}, bf16[128,2048]{1,0:T(8,128)(2,1)}, u32[]{:S(2)}, u32[]{:S(2)}) collective-permute-start(bf16[128,2048]{1,0:T(8,128)(2,1)S(1)} %copy-done.5), channel_id=1, source_target_pairs={{0,2},{1,3},{2,0},{3,1},{4,6},{5,7},{6,4},{7,5},{8,10},{9,11},{10,... | collective-permute-start | bytes 1572872 | tf_op jit(solution)/shard_map/ppermute | solution.py:82
  115.4 45.0 %collective-permute-start.9 = (bf16[128,2048]{1,0:T(8,128)(2,1)S(1)}, bf16[128,2048]{1,0:T(8,128)(2,1)S(1)}, u32[]{:S(2)}, u32[]{:S(2)}) collective-permute-start(bf16[128,2048]{1,0:T(8,128)(2,1)S(1)} %get-tuple-element.103), channel_id=1, source_target_pairs={{0,2},{1,3},{2,0},{3,1},{4,6},{5,7},{6,4},{7,5},{8,10},{9,11},{10,... | collective-permute-start | bytes 1572872 | tf_op jit(solution)/shard_map/ppermute | solution.py:82
  115.4 45.0 %collective-permute-start.10 = (bf16[128,2048]{1,0:T(8,128)(2,1)S(1)}, bf16[128,2048]{1,0:T(8,128)(2,1)S(1)}, u32[]{:S(2)}, u32[]{:S(2)}) collective-permute-start(bf16[128,2048]{1,0:T(8,128)(2,1)S(1)} %get-tuple-element.104), channel_id=1, source_target_pairs={{0,1},{1,2},{2,3},{3,0},{4,5},{5,6},{6,7},{7,4},{8,9},{9,10},{10,1... | collective-permute-start | bytes 1572872 | tf_op jit(solution)/shard_map/ppermute | solution.py:82
  116.1 63.8 %collective-permute-start.14 = (bf16[128,2048]{1,0:T(8,128)(2,1)S(1)}, bf16[128,2048]{1,0:T(8,128)(2,1)S(1)}, u32[]{:S(2)}, u32[]{:S(2)}) collective-permute-start(bf16[128,2048]{1,0:T(8,128)(2,1)S(1)} %copy-done.5), channel_id=1, source_target_pairs={{0,3},{1,0},{2,1},{3,2},{4,7},{5,4},{6,5},{7,6},{8,11},{9,8},{10,9... | collective-permute-start | bytes 1572872 | tf_op jit(solution)/shard_map/ppermute | solution.py:82
  174.1 31.2 %collective-permute-start.12 = (bf16[128,2048]{1,0:T(8,128)(2,1)S(1)}, bf16[128,2048]{1,0:T(8,128)(2,1)S(1)}, u32[]{:S(2)}, u32[]{:S(2)}) collective-permute-start(bf16[128,2048]{1,0:T(8,128)(2,1)S(1)} %get-tuple-element.110.refs_0_), channel_id=1, source_target_pairs={{0,2},{1,3},{2,0},{3,1},{4,6},{5,7},{6,4},{7,5},{8,10},{9,11},{10,... | collective-permute-start | bytes 1572872 | tf_op jit(solution)/shard_map/ppermute | solution.py:82
  176.0 31.6 %collective-permute-start.13 = (bf16[128,2048]{1,0:T(8,128)(2,1)S(1)}, bf16[128,2048]{1,0:T(8,128)(2,1)S(1)}, u32[]{:S(2)}, u32[]{:S(2)}) collective-permute-start(bf16[128,2048]{1,0:T(8,128)(2,1)S(1)} %get-tuple-element.110.refs_0_), channel_id=1, source_target_pairs={{0,3},{1,0},{2,1},{3,2},{4,7},{5,4},{6,5},{7,6},{8,11},{9,8},{10,9... | collective-permute-start | bytes 1572872 | tf_op jit(solution)/shard_map/ppermute | solution.py:82
  250.7 109.0 %all-gather.8.cloned.1.call-start = ((), (), s32[]{:S(2)}) async-start(), calls=%async_computation.6 | async-start | bytes 2621440 | tf_op jit(solution)/shard_map/all_gather | solution.py:483
  314.4 90.9 %reduce-scatter.6.cloned.1.call-start = ((), (), s32[]{:S(2)}) async-start(), calls=%async_computation.7 | async-start | bytes 2621440 | tf_op jit(solution)/shard_map/reduce_scatter | solution.py:486
  314.4 76.5 %collective-permute-start.19 = (bf16[512,2048]{1,0:T(8,128)(2,1)S(1)}, bf16[512,2048]{1,0:T(8,128)(2,1)}, u32[]{:S(2)}, u32[]{:S(2)}) collective-permute-start(bf16[512,2048]{1,0:T(8,128)(2,1)S(1)} %get-tuple-element.144.refs_8_.refs_9_.refs_10_.refs_11_), channel_id=1, source_target_pairs={{0,4},{4,0},{8,12},{12,8},{16,20},{20,16},{24,28},{28,24},{1,5},{5... | collective-permute-start | bytes 6291464 | tf_op jit(solution)/shard_map/ppermute | solution.py:101
  316.5 65.7 %collective-permute-start.20 = (bf16[512,512]{1,0:T(8,128)(2,1)}, bf16[512,512]{1,0:T(8,128)(2,1)}, u32[]{:S(2)}, u32[]{:S(2)}) collective-permute-start(bf16[512,512]{1,0:T(8,128)(2,1)} %copy.75), channel_id=1, source_target_pairs={{0,4},{4,0},{8,12},{12,8},{16,20},{20,16},{24,28},{28,24},{1,5},{5... | collective-permute-start | bytes 1572872 | tf_op jit(solution)/shard_map/ppermute | solution.py:101
  317.1 90.4 %collective-permute-start.24 = (bf16[512,3072]{1,0:T(8,128)(2,1)}, bf16[512,3072]{1,0:T(8,128)(2,1)}, u32[]{:S(2)}, u32[]{:S(2)}) collective-permute-start(bf16[512,3072]{1,0:T(8,128)(2,1)} %get-tuple-element.162), channel_id=1, source_target_pairs={{0,16},{4,20},{8,24},{12,28},{16,0},{20,4},{24,8},{28,12},{1,17},{... | collective-permute-start | bytes 9437192 | tf_op jit(solution)/shard_map/ppermute | solution.py:101
  318.6 88.9 %collective-permute-start.25 = (bf16[512,3072]{1,0:T(8,128)(2,1)}, bf16[512,3072]{1,0:T(8,128)(2,1)}, u32[]{:S(2)}, u32[]{:S(2)}) collective-permute-start(bf16[512,3072]{1,0:T(8,128)(2,1)} %get-tuple-element.164), channel_id=1, source_target_pairs={{0,8},{4,12},{8,0},{12,4},{16,24},{20,28},{24,16},{28,20},{1,9},{5... | collective-permute-start | bytes 9437192 | tf_op jit(solution)/shard_map/ppermute | solution.py:101
  359.8 116.7 %reduce-scatter.8.cloned.1.call-start = ((), (), s32[]{:S(2)}) async-start(), calls=%async_computation.8 | async-start | bytes 2621440 | tf_op jit(solution)/shard_map/reduce_scatter | solution.py:512
  360.1 30.8 %collective-permute-start.18 = (bf16[512,2048]{1,0:T(8,128)(2,1)}, bf16[512,2048]{1,0:T(8,128)(2,1)}, u32[]{:S(2)}, u32[]{:S(2)}) collective-permute-start(bf16[512,2048]{1,0:T(8,128)(2,1)} %all-gather.8.cloned.1.call-done.refs_0_.refs_1_.refs_2_.refs_3_), channel_id=1, source_target_pairs={{0,4},{4,0},{8,12},{12,8},{16,20},{20,16},{24,28},{28,24},{1,5},{5... | collective-permute-start | bytes 6291464 | tf_op jit(solution)/shard_map/ppermute | solution.py:101
  411.7 51.2 %collective-permute-start.28 = (bf16[256,3072]{1,0:T(8,128)(2,1)S(1)}, bf16[256,3072]{1,0:T(8,128)(2,1)S(1)}, u32[]{:S(2)}, u32[]{:S(2)}) collective-permute-start(bf16[256,3072]{1,0:T(8,128)(2,1)S(1)} %get-tuple-element.235), channel_id=1, source_target_pairs={{0,8},{4,12},{8,0},{12,4},{16,24},{20,28},{24,16},{28,20},{1,9},{5... | collective-permute-start | bytes 4718600 | tf_op jit(solution)/shard_map/ppermute | solution.py:101
  417.0 45.9 %collective-permute-start.29 = (bf16[256,3072]{1,0:T(8,128)(2,1)S(1)}, bf16[256,3072]{1,0:T(8,128)(2,1)S(1)}, u32[]{:S(2)}, u32[]{:S(2)}) collective-permute-start(bf16[256,3072]{1,0:T(8,128)(2,1)S(1)} %get-tuple-element.233), channel_id=1, source_target_pairs={{0,16},{4,20},{8,24},{12,28},{16,0},{20,4},{24,8},{28,12},{1,17},{... | collective-permute-start | bytes 4718600 | tf_op jit(solution)/shard_map/ppermute | solution.py:101
  423.7 37.4 %collective-permute-start.27 = (bf16[256,512]{1,0:T(8,128)(2,1)S(1)}, bf16[256,512]{1,0:T(8,128)(2,1)S(1)}, u32[]{:S(2)}, u32[]{:S(2)}) collective-permute-start(bf16[256,512]{1,0:T(8,128)(2,1)S(1)} %slice.146), channel_id=1, source_target_pairs={{0,16},{4,20},{8,24},{12,28},{16,0},{20,4},{24,8},{28,12},{1,17},{... | collective-permute-start | bytes 786440 | tf_op jit(solution)/shard_map/ppermute | solution.py:101
  426.6 35.4 %collective-permute-start.26 = (bf16[256,768]{1,0:T(8,128)(2,1)S(1)}, bf16[256,768]{1,0:T(8,128)(2,1)S(1)}, u32[]{:S(2)}, u32[]{:S(2)}) collective-permute-start(bf16[256,768]{1,0:T(8,128)(2,1)S(1)} %slice.144), channel_id=1, source_target_pairs={{0,8},{4,12},{8,0},{12,4},{16,24},{20,28},{24,16},{28,20},{1,9},{5... | collective-permute-start | bytes 1179656 | tf_op jit(solution)/shard_map/ppermute | solution.py:101
  (67 other events, 725.1 us)
Sparse Core Ops, SparseCore 0:
  10.5 43.8 all-gather.3
  56.4 125.3 all-gather.5
  250.8 59.0 reduce-scatter.3
  314.5 45.2 all-gather.7
  362.6 42.5 reduce-scatter.5
  407.4 43.1 reduce-scatter.7

commit v4 on v3

--- a/solution.py
+++ b/solution.py
@@ -20,30 +20,29 @@
     steps_f = jnp.arange(half_width, dtype=F32)
     inverse = 1.0 / ROPE_BASE ** (steps_f * 2.0 / width)
     angles = position.astype(F32)[:, None] * inverse[None, :]
-    return (jnp.cos(angles)[:, None, :], jnp.sin(angles)[:, None, :])
-
-
-def rotate(values, cosine_table, sine_table):
-    half_width = values.shape[-1] // 2
-    first_half = values[..., :half_width]
-    second_half = values[..., half_width:]
-    return jnp.concatenate(
-        [
-            first_half * cosine_table - second_half * sine_table,
-            second_half * cosine_table + first_half * sine_table,
-        ],
-        axis=-1,
-    )
-
-
-def layout(seq_lengths, seq_group, group_id, place):
-    owned_mask = (seq_group == group_id).astype(jnp.int32)
-    owned_len = seq_lengths * owned_mask
-    seq_ends = jnp.cumsum(owned_len)
-    finished = (seq_ends[None, :] <= place[:, None]).astype(jnp.int32)
-    segment = jnp.sum(finished * owned_mask[None, :], axis=1)
-    offsets = jnp.sum(finished * owned_len[None, :], axis=1)
-    return (segment, place - offsets)
+    cosine, sine = jnp.cos(angles), jnp.sin(angles)
+    return jnp.concatenate([cosine] * 4 + [-sine, sine] * 2, axis=1)
+
+
+def turned(values, cosine, sine):
+    width = values.shape[1]
+    half = HEAD_DIM // 2
+    lane = lax.broadcasted_iota(jnp.int32, values.shape, 1)
+    if width > HEAD_DIM:
+        up, down = pltpu.roll(values, half, axis=1), pltpu.roll(values, width - half, axis=1)
+        swapped = jnp.where(lane % HEAD_DIM < half, down, up)
+    else:
+        swapped = jnp.concatenate([values[:, half:], values[:, :half]], axis=1)
+    return values * cosine[:, :width] + swapped * sine[:, :width]
+
+
+def layout(seq_lengths, seq_group, group_id, row_count):
+    owned = seq_group == group_id
+    owned_len = jnp.where(owned, seq_lengths, 0)
+    ends = jnp.where(owned, jnp.cumsum(owned_len), row_count + 1)
+    row = jnp.arange(row_count, dtype=jnp.int32)
+    offsets = jnp.sum((ends[None, :] <= row[:, None]).astype(jnp.int32) * owned_len[None, :], axis=1)
+    return (ends.astype(jnp.int32), row - offsets)
 
 
 def mm(left, right):
@@ -122,12 +121,13 @@
         return [(keep, self.swap(send, self.hops(half)[0])) for half, (keep, send) in enumerate(pairs)]
 
     def other_hops(self, pairs, order):
-        pairs = list(pairs)
+        terms = [list(pair) for pair in pairs]
         for hop in range(1, len(self.bits) - 1):
-            totals = order(lambda *p: [total32(terms).astype(BF16) for terms in p], *pairs)
-            cut = totals[0].shape[0] // 2
-            pairs = [(t[:cut], self.swap(t[cut:], self.hops(half)[hop])) for half, t in enumerate(totals)]
-        return pairs
+            rows = terms[0][-1].shape[0]
+            sent = order(lambda *p: [total32([t[rows // 2 : rows] for t in ts]).astype(BF16) for ts in p], *terms)
+            for half in range(2):
+                terms[half].append(self.swap(sent[half], self.hops(half)[hop]))
+        return terms
 
 
 class Order:
@@ -140,6 +140,10 @@
         out = step(*args)
         self.last = jax.tree.leaves(out)[0]
         return out
+
+
+def block_sum32(halves):
+    return jnp.concatenate([total32([t[: terms[-1].shape[0]] for t in terms]) for terms in halves], axis=1)
 
 
 def total32(terms):
@@ -251,7 +255,7 @@
 def rows_product(a, leads, w, first, name, owners=None):
     rows, units = a.shape[1:]
     features = w.shape[0]
-    tile = tile_of(features, 256)
+    tile = tile_of(features, 512 if units * len(leads) > 1024 else 1024)
     count = 1 if owners is None else owners.shape[0]
     block = rows // count
     width = units * len(leads)
@@ -379,11 +383,164 @@
     return (keep_a, send_a), (keep_b, send_b)
 
 
-def attention_masked(queries, keys_all, segment, place):
+def head_columns(heads, kv):
+    keys, values = heads * HEAD_DIM, (heads + kv) * HEAD_DIM
+    for h in range(heads):
+        c = h // (heads // kv)
+        yield (
+            slice(h * HEAD_DIM, (h + 1) * HEAD_DIM),
+            slice(keys + c * HEAD_DIM, keys + (c + 1) * HEAD_DIM),
+            slice(values + c * HEAD_DIM, values + (c + 1) * HEAD_DIM),
+        )
+
+
+def segments(ends_ref, count, place):
+    found = jnp.zeros_like(place)
+    for i in range(count):
+        found += (ends_ref[i] <= place).astype(jnp.int32)
+    return found
+
+
+def allowed_pairs(ends_ref, count, j, block, rows):
+    query = j * block + lax.broadcasted_iota(jnp.int32, (block, 128), 0)
+    key = lax.broadcasted_iota(jnp.int32, (8, rows), 1)
+    query_segment, key_segment = segments(ends_ref, count, query)[:, :1], segments(ends_ref, count, key)[:1]
+    return (query_segment == key_segment) & (key[:1] <= query[:, :1])
+
+
+def turn_heads(read, write, columns, cosine, sine):
+    step = 2 * HEAD_DIM
+    for at in range(0, columns, step):
+        cut = slice(at, min(at + step, columns))
+        write(cut, turned(read(cut), cosine, sine).astype(BF16))
+
+
+def attention_forward(ends, qkv, table, heads, kv):
+    rows, width = qkv.shape
+    block = tile_of(rows, 256)
+    turn_width = (heads + kv) * HEAD_DIM
+    at_sine = table.shape[1] // 2
     scale = 1.0 / math.sqrt(HEAD_DIM)
-    allowed = (segment[:, None] == segment[None, :]) & (place[None, :] <= place[:, None])
-    scores = jnp.einsum("qcgd,kcd->cgqk", queries, keys_all, preferred_element_type=F32) * scale
-    return jnp.where(allowed, scores, -1e30)
+
+    def body(ends_ref, qkv_ref, table_ref, low_ref, out_ref, mass_ref):
+        j = pl.program_id(0)
+
+        @pl.when(j == 0)
+        def _():
+            def write(cut, v):
+                low_ref[:, cut] = v
+
+            turn_heads(lambda cut: qkv_ref[:, cut], write, turn_width, table_ref[:, :at_sine], table_ref[:, at_sine:])
+            low_ref[:, turn_width:] = qkv_ref[:, turn_width:].astype(BF16)
+
+        allowed = allowed_pairs(ends_ref, ends.shape[0], j, block, rows)
+        here = pl.ds(pl.multiple_of(j * block, block), block)
+        lane = lax.broadcasted_iota(jnp.int32, (block, 128), 1)
+        mass = jnp.zeros((block, 128), F32)
+        for h, (q_at, k_at, v_at) in enumerate(head_columns(heads, kv)):
+            scores = outer(low_ref[here, q_at], low_ref[:, k_at]) * scale
+            scores = jnp.where(allowed, scores, -1e30)
+            row_max = jnp.max(scores, axis=1, keepdims=True)
+            weights = jnp.exp(scores - row_max)
+            row_sum = jnp.sum(weights, axis=1, keepdims=True)
+            weights_low = (weights / row_sum).astype(BF16)
+            out_ref[:, q_at] = mm(weights_low, low_ref[:, v_at]).astype(BF16)
+            mass = jnp.where(lane == h, row_max + jnp.log(row_sum), mass)
+        mass_ref[...] = mass
+
+    return kernel_call(
+        body,
+        "attention_forward",
+        4 * rows * rows * heads * HEAD_DIM,
+        (ends, qkv, table),
+        (
+            jax.ShapeDtypeStruct((rows, width), BF16),
+            jax.ShapeDtypeStruct((rows, heads * HEAD_DIM), BF16),
+            jax.ShapeDtypeStruct((rows, 128), F32),
+        ),
+        grid_spec=pltpu.PrefetchScalarGridSpec(
+            num_scalar_prefetch=1,
+            grid=(rows // block,),
+            in_specs=[whole((rows, width)), whole(table.shape)],
+            out_specs=[
+                whole((rows, width)),
+                pl.BlockSpec((block, heads * HEAD_DIM), lambda j, _: (j, 0)),
+                pl.BlockSpec((block, 128), lambda j, _: (j, 0)),
+            ],
+        ),
+    )
+
+
+def attention_backward(ends, grad_rows, w, low, mass, table, heads, kv):
+    rows, features = grad_rows.shape
+    width, out_width = low.shape[1], heads * HEAD_DIM
+    block = tile_of(rows, 256)
+    scale = 1.0 / math.sqrt(HEAD_DIM)
+
+    at_sine = table.shape[1] // 2
+
+    def body(ends_ref, grad_ref, w_ref, low_ref, mass_ref, table_ref, out_ref, low_grad, q_grad, k_grad, v_grad):
+        j = pl.program_id(0)
+
+        @pl.when(j == 0)
+        def _():
+            low_grad[...] = mm(grad_ref[...], w_ref[...]).astype(BF16)
+            k_grad[...] = jnp.zeros_like(k_grad)
+            v_grad[...] = jnp.zeros_like(v_grad)
+
+        allowed = allowed_pairs(ends_ref, ends.shape[0], j, block, rows)
+        here = pl.ds(pl.multiple_of(j * block, block), block)
+        for h, (q_at, k_at, v_at) in enumerate(head_columns(heads, kv)):
+            query, grad = low_ref[here, q_at], low_grad[here, q_at]
+            scores = outer(query, low_ref[:, k_at]) * scale
+            probs = jnp.exp(jnp.where(allowed, scores, -1e30) - mass_ref[:, h : h + 1])
+            grad_probs = outer(grad, low_ref[:, v_at])
+            delta = jnp.sum(probs * grad_probs, axis=1, keepdims=True)
+            grad_scores = (probs * (grad_probs - delta)).astype(BF16)
+            q_grad[:, q_at] = mm(grad_scores, low_ref[:, k_at]) * scale
+            c = h // (heads // kv)
+            kv_at = slice(c * HEAD_DIM, (c + 1) * HEAD_DIM)
+            k_grad[:, kv_at] += inner(grad_scores, query)
+            v_grad[:, kv_at] += inner(probs.astype(BF16), grad)
+
+        def write_q(cut, v):
+            out_ref[here, cut] = v
+
+        def write_k(cut, v):
+            out_ref[:, out_width + cut.start : out_width + cut.stop] = v
+
+        turn_heads(lambda cut: q_grad[:, cut], write_q, out_width, table_ref[here, :at_sine], -table_ref[here, at_sine:])
+
+        @pl.when(j == pl.num_programs(0) - 1)
+        def _():
+            turn_heads(lambda cut: k_grad[:, cut] * scale, write_k, kv * HEAD_DIM, table_ref[:, :at_sine], -table_ref[:, at_sine:])
+            out_ref[:, out_width + kv * HEAD_DIM :] = v_grad[...].astype(BF16)
+
+    return kernel_call(
+        body,
+        "attention_backward",
+        10 * rows * rows * heads * HEAD_DIM + 2 * rows * features * out_width,
+        (ends, grad_rows, w, low, mass, table),
+        jax.ShapeDtypeStruct((rows, width), BF16),
+        grid_spec=pltpu.PrefetchScalarGridSpec(
+            num_scalar_prefetch=1,
+            grid=(rows // block,),
+            in_specs=[
+                whole((rows, features)),
+                pl.BlockSpec((features, out_width), lambda j, _: (0, 0)),
+                whole((rows, width)),
+                pl.BlockSpec((block, 128), lambda j, _: (j, 0)),
+                whole(table.shape),
+            ],
+            out_specs=whole((rows, width)),
+            scratch_shapes=[
+                pltpu.VMEM((rows, out_width), BF16),
+                pltpu.VMEM((block, out_width), F32),
+                pltpu.VMEM((rows, kv * HEAD_DIM), F32),
+                pltpu.VMEM((rows, kv * HEAD_DIM), F32),
+            ],
+        ),
+    )
 
 
 def per_device(
@@ -405,7 +562,6 @@
 ):
     cube = Cube(dp_size)
     line = Line(tensor_size)
-    scale = 1.0 / math.sqrt(HEAD_DIM)
     width_q, width_k = w_query.shape[1], w_key.shape[1]
     own_rows = tokens.shape[0]
     row_count = own_rows * tensor_size
@@ -428,31 +584,13 @@
     normed_one, factor_one = norm_parts(tokens_f)
     heads_here = width_q // HEAD_DIM
     kv_here = width_k // HEAD_DIM
-    head_group = heads_here // kv_here
-    place = jnp.arange(row_count, dtype=jnp.int32)
-    segment, position = layout(seq_lengths, seq_group, cube.me, place)
-    cosine_table, sine_table = rope_tables(position, HEAD_DIM)
-    queries = (
-        rotate(qkv[:, :width_q].reshape(row_count, heads_here, HEAD_DIM), cosine_table, sine_table)
-        .astype(BF16)
-        .reshape(row_count, kv_here, head_group, HEAD_DIM)
-    )
-    keys_all = rotate(
-        qkv[:, width_q : width_q + width_k].reshape(row_count, kv_here, HEAD_DIM), cosine_table, sine_table
-    ).astype(BF16)
-    values_all = qkv[:, width_q + width_k :].astype(BF16).reshape(row_count, kv_here, HEAD_DIM)
-    scores = attention_masked(queries, keys_all, segment, place)
-    row_max = jnp.max(scores, axis=-1, keepdims=True)
-    exponent = jnp.exp(scores - row_max)
-    row_sum = jnp.sum(exponent, axis=-1, keepdims=True)
-    weights_low = (exponent / row_sum).astype(BF16)
-    mixed = jnp.einsum("cgqk,kcd->qcgd", weights_low, values_all, preferred_element_type=F32)
-    attended = mixed.reshape(row_count, heads_here * HEAD_DIM).astype(BF16)
-    log_mass = row_max + jnp.log(row_sum)
+    ends, position = layout(seq_lengths, seq_group, cube.me, row_count)
+    table = rope_tables(position, HEAD_DIM)
+    low_qkv, attended, log_mass = order(lambda *a: attention_forward(*a, heads_here, kv_here), ends, qkv, table)
 
     out_parts = order(
         lambda a, w: rows_product(a, [0], w, 0, "attention_out", line.owners),
-        after(attended, *incoming_blocks[1:3])[None],
+        after(attended, incoming_blocks[1])[None],
         w_attn,
     )
     attended_other = cube.swap(attended, 1)
@@ -461,7 +599,10 @@
     mlp_blocks = line.gather((normed_two * gain_two).astype(BF16))
 
     mlp_input, incoming, unit_grads = order(
-        lambda h, c, w: feed_forward(h, c, w, line.owners), mlp_blocks, incoming_blocks, w_mlp
+        lambda h, c, w: feed_forward(h, c, w, line.owners),
+        mlp_blocks,
+        incoming_blocks,
+        after(w_mlp, attn_input_other, attended_other),
     )
     mlp_others = [cube.swap(v, 1) for v in (mlp_input, incoming, unit_grads)]
     two_parts = order(lambda a, w: rows_product(a, [0, 1], w, 0, "feed_forward_rows_grad"), unit_grads, w_mlp)
@@ -486,30 +627,15 @@
     block_sum = lax.psum_scatter(block_parts, "tensor", scatter_dimension=0, tiled=True)
     rows_other = cube.swap(grad_attn_rows, 1)
 
-    grad_attended = mm(grad_attn_rows, w_attn[:, :width_out]).astype(BF16)
-    grad_block = grad_attended.reshape(row_count, kv_here, head_group, HEAD_DIM)
-    scores = attention_masked(queries, keys_all, segment, place)
-    probs = jnp.exp(scores - log_mass)
-    weights_low = probs.astype(BF16)
-    grad_probs = jnp.einsum("qcgd,kcd->cgqk", grad_block, values_all, preferred_element_type=F32)
-    delta = jnp.sum(probs * grad_probs, axis=-1, keepdims=True)
-    grad_scores = (probs * (grad_probs - delta)).astype(BF16)
-    grad_queries = jnp.einsum("cgqk,kcd->qcgd", grad_scores, keys_all, preferred_element_type=F32) * scale
-    grad_keys = jnp.einsum("cgqk,qcgd->kcd", grad_scores, queries, preferred_element_type=F32) * scale
-    grad_values = jnp.einsum("cgqk,qcgd->kcd", weights_low, grad_block, preferred_element_type=F32)
-    grad_queries = (
-        rotate(grad_queries.reshape(row_count, heads_here, HEAD_DIM), cosine_table, -sine_table)
-        .astype(BF16)
-        .reshape(row_count, width_q)
-    )
-    grad_keys = rotate(grad_keys, cosine_table, -sine_table).astype(BF16).reshape(row_count, width_k)
-    grad_qkv = jnp.concatenate(
-        [grad_queries, grad_keys, grad_values.astype(BF16).reshape(row_count, width_k)], axis=1
-    )
+    grad_qkv = order(
+        lambda *a: attention_backward(*a, heads_here, kv_here), ends, grad_attn_rows, w_attn, low_qkv, log_mass, table
+    )
+    mlp_terms = cube.other_hops(mlp_pairs, order)
     one_parts = order(
         lambda a, w: rows_product(a, [0], w, width_out, "attention_rows_grad"), grad_qkv[None], w_attn
     )
     one_sum = lax.psum_scatter(after(one_parts, block_sum), "tensor", scatter_dimension=0, tiled=True)
+
 
     def attn_grad(y, y_other, h, h_other, a, a_other, g, g_other):
         parts = [(0, [(a[None], 0), (a_other[None], 0)]), (1, [(g[None], 0), (g_other[None], 0)])]
@@ -529,14 +655,13 @@
         )
     )
     block_out = order(lambda x, t: (x + t.astype(F32)).astype(BF16), residual, block_sum)
-    mlp_terms = cube.other_hops(mlp_pairs, order)
     attn_terms = cube.other_hops(attn_pairs, order)
 
     def gain_terms(*pairs):
         return functools.reduce(lambda a, b: a + b, [jnp.sum(w.astype(F32) * g, axis=1) for w, g in pairs])
 
     def mlp_finals(terms, gate, up):
-        sums = jnp.concatenate([total32(t) for t in terms], axis=1)
+        sums = block_sum32(terms)
         gate_grad, up_grad, down_grad = sums[:, :units], sums[:, units : 2 * units], sums[:, 2 * units :].T
         return gain_terms((gate, gate_grad), (up, up_grad)), gate_grad, up_grad, down_grad
 
@@ -549,7 +674,7 @@
         factor_one,
         one_sum,
     )
-    attn_sum = jnp.concatenate([total32(t) for t in attn_terms], axis=1)
+    attn_sum = block_sum32(attn_terms)
     out_grad, qkv_grad = attn_sum[:, :width_out].T, attn_sum[:, width_out:]
     query_grad = qkv_grad[:, :width_q]
     key_grad = qkv_grad[:, width_q : width_q + width_k]

time: 497 us -> 476 us (0.958); the launches traced: 487 us -> 475 us
  local copies, waits for them, and re-layouts: 48.6 us -> 24.5 us
  waiting for transfers between devices: 199 us -> 219 us
  matrix products: 18.4 us -> 0 us
  Pallas kernels: 99 us -> 116 us
    dot_general x7 -> x0, matrix products: 18.4 us -> none  [the longest x1 5.34 us: per_device(): jnp.einsum('qcgd,kcd->cgqk', grad_block, values_all, preferred_element_ty...]
    pallas_call x8 -> x10, Pallas kernels: 99 us -> 116 us  [kernel_call(): pl.pallas_call(body, out_shape=out_shape, name=name, cost_estimate=pl.Cos...]
    unnamed x108 -> x78, local copies, waits for them, and re-layouts: 32.3 us -> 22.7 us
    slice x10 -> x0, local copies, waits for them, and re-layouts: 8.34 us -> none  [the longest x2 3.66 us: per_device(): qkv[:, :width_q].reshape(row_count, heads_here, HEAD_DIM)]
    ppermute x15, waiting for transfers between devices: 97.5 us -> 106 us  [shift(): lax.ppermute(v, 'tensor', [(i, (i + r) % self.size) for i in range(self.s...]
    all_gather x1, waiting for transfers between devices: 0.01 us -> 6.28 us  [per_device(): lax.all_gather(jnp.concatenate([w_gate, w_up, w_down.T], axis=1), 'dp', a...]
    add x3, other arithmetic: 1.29 us -> 6.27 us  [total32(): return functools.reduce(lambda a, b: a + b, [t.astype(F32) for t in terms])]
    convert_element_type x6 -> x4, other arithmetic: 10.9 us -> 7.49 us  [other_hops(): total32([t[rows // 2:rows] for t in ts]).astype(BF16)]
  transfers between devices with their start and end apart: 39 -> 39, of which waited for: 18 -> 18; matrix products, arithmetic and copies ran while one was open for 15% -> 8% of each run, Pallas kernels for 16% -> 20%
where the time goes in v4:
time: 476 us; the launch traced here: 475 us
  waiting for transfers between devices  219 us (46%)
  Pallas kernels  116 us (24%)
  starting transfers between devices  60.9 us (13%)
  other arithmetic  39.6 us (8%)
  local copies, waits for them, and re-layouts  24.5 us (5%)
  between operations  14.6 us (3%)
    pallas_call x10, Pallas kernels, kernel_call(): pl.pallas_call(body, out_shape=out_shape, name=name, cost_estimate=pl.Cos...  116 us
    ppermute x15, waiting for transfers between devices, shift(): lax.ppermute(v, 'tensor', [(i, (i + r) % self.size) for i in range(self.s...  106 us
    ppermute x18, waiting for transfers between devices, swap(): return lax.ppermute(v, 'dp', [(i, i ^ m) for i in range(self.size)])  50.1 us
    ppermute x15, starting transfers between devices, shift(): lax.ppermute(v, 'tensor', [(i, (i + r) % self.size) for i in range(self.s...  47.7 us
    all_gather x1, waiting for transfers between devices, per_device(): lax.all_gather(grad_residual.astype(BF16), 'tensor', axis=0, tiled=True)  33.4 us
    reduce_scatter x1, waiting for transfers between devices, per_device(): lax.psum_scatter(two_parts, 'tensor', scatter_dimension=0, tiled=True)  23.1 us
    unnamed x78, local copies, waits for them, and re-layouts  22.7 us
    ppermute x18, starting transfers between devices, swap(): return lax.ppermute(v, 'dp', [(i, i ^ m) for i in range(self.size)])  12.7 us
  transfers between devices with their start and end apart: 39, of which 18 were waited for; matrix products, arithmetic and copies ran while one was open for 8% of the time, Pallas kernels for 20%

profile of v4, /device:TPU:0, one launch (start us, length us, event | category | flops | bytes accessed | tf_op | source)
XLA Modules:
  0.0 474.7 jit_solution(3549805316160924955)
XLA Ops:
  34.5 21.6 %collective-permute-done.1.refs_2_ = bf16[128,2048]{1,0:T(8,128)(2,1)S(1)} collective-permute-done((bf16[128,2048]{1,0:T(8,128)(2,1)S(1)}, bf16[128,2048]{1,0:T(8,128)(2,1)S(1)}, u32[]{:S(2)}, u32[]{:S(2)}) %collective-permute-start.1) | collective-permute-done | bytes 524320 | tf_op jit(solution)/shard_map/ppermute | solution.py:81
  57.8 10.9 %collective-permute-start.6 = (bf16[128,2048]{1,0:T(8,128)(2,1)}, bf16[128,2048]{1,0:T(8,128)(2,1)}, u32[]{:S(2)}, u32[]{:S(2)}) collective-permute-start(bf16[128,2048]{1,0:T(8,128)(2,1)} %refs_4_), channel_id=1, source_target_pairs={{0,1},{1,2},{2,3},{3,0},{4,5},{5,6},{6,7},{7,4},{8,9},{9,10},{10,1... | collective-permute-start | bytes 1572872 | tf_op jit(solution)/shard_map/ppermute | solution.py:81
  71.0 5.3 %attention_in.1 = (bf16[512,2048]{1,0:T(8,128)(2,1)S(1)}, f32[512,768]{1,0:T(8,128)S(1)}) custom-call(s32[4]{0:T(128)S(1)} %compare_select_fusion.owners_ref, bf16[128,2048]{1,0:T(8,128)(2,1)S(1)} %copy-done.3, bf16[128,2048]{1,0:T(8,128)(2,1)S(1)} %collective-permute-done.refs_1_, bf16[128,2048]{1,0:T(8,128)(2,1)S(1)} %copy-done.14, ...), custom_call_target="tpu_custom_call" | custom-call | flops 1610612736 | bytes 11018256 | tf_op jit(solution)/shard_map/attention_in/pallas_call | solution.py:162
  82.4 9.5 %attention_forward.1 = (bf16[512,768]{1,0:T(8,128)(2,1)S(1)}, bf16[512,512]{1,0:T(8,128)(2,1)S(1)}, f32[512,128]{1,0:T(8,128)S(1)}) custom-call(s32[24]{0:T(128)S(1)} %compare_select_fusion.2.ends_ref, f32[512,768]{1,0:T(8,128)S(1)} %copy-done.8, f32[512,256]{1,0:T(8,128)S(1)} %concatenate.40.table_ref), custom_call_target="tpu_custom_call" | custom-call | flops 536870912 | bytes 3670112 | tf_op jit(solution)/shard_map/attention_forward/pallas_call | solution.py:162
  101.4 9.2 %collective-permute-done.7 = bf16[128,2048]{1,0:T(8,128)(2,1)S(1)} collective-permute-done((bf16[128,2048]{1,0:T(8,128)(2,1)S(1)}, bf16[128,2048]{1,0:T(8,128)(2,1)S(1)}, u32[]{:S(2)}, u32[]{:S(2)}) %collective-permute-start.7) | collective-permute-done | bytes 524320 | tf_op jit(solution)/shard_map/ppermute | solution.py:81
  114.9 41.6 %collective-permute-done.8 = bf16[128,2048]{1,0:T(8,128)(2,1)S(1)} collective-permute-done((bf16[128,2048]{1,0:T(8,128)(2,1)S(1)}, bf16[128,2048]{1,0:T(8,128)(2,1)S(1)}, u32[]{:S(2)}, u32[]{:S(2)}) %collective-permute-start.8) | collective-permute-done | bytes 524320 | tf_op jit(solution)/shard_map/ppermute | solution.py:81
  158.5 11.3 %collective-permute-start.10 = (bf16[128,2048]{1,0:T(8,128)(2,1)}, bf16[128,2048]{1,0:T(8,128)(2,1)}, u32[]{:S(2)}, u32[]{:S(2)}) collective-permute-start(bf16[128,2048]{1,0:T(8,128)(2,1)} %get-tuple-element.131.refs_0_), channel_id=1, source_target_pairs={{0,1},{1,2},{2,3},{3,0},{4,5},{5,6},{6,7},{7,4},{8,9},{9,10},{10,1... | collective-permute-start | bytes 1572872 | tf_op jit(solution)/shard_map/ppermute | solution.py:81
  175.5 6.3 %all-gather.6.cloned.1.call-done.refs_8_.refs_9_.refs_10_.refs_2_.refs_1_ = bf16[2048,6144]{1,0:T(8,128)(2,1)} async-done(((bf16[256,6144]{1,0:T(8,128)(2,1)}), bf16[2048,6144]{1,0:T(8,128)(2,1)}) %all-gather.6.cloned.1.call-update) | async-done | bytes 25165840 | tf_op jit(solution)/shard_map/all_gather | solution.py:575
  181.7 8.5 %collective-permute-done.13.refs_6_ = bf16[128,2048]{1,0:T(8,128)(2,1)} collective-permute-done((bf16[128,2048]{1,0:T(8,128)(2,1)}, bf16[128,2048]{1,0:T(8,128)(2,1)}, u32[]{:S(2)}, u32[]{:S(2)}) %collective-permute-start.13) | collective-permute-done | bytes 524320 | tf_op jit(solution)/shard_map/ppermute | solution.py:81
  190.3 22.5 %collective-permute-done.11.refs_2_ = bf16[128,2048]{1,0:T(8,128)(2,1)} collective-permute-done((bf16[128,2048]{1,0:T(8,128)(2,1)}, bf16[128,2048]{1,0:T(8,128)(2,1)}, u32[]{:S(2)}, u32[]{:S(2)}) %collective-permute-start.11) | collective-permute-done | bytes 524320 | tf_op jit(solution)/shard_map/ppermute | solution.py:81
  212.8 22.1 %feed_forward.1 = (bf16[512,2048]{1,0:T(8,128)(2,1)}, bf16[512,2048]{1,0:T(8,128)(2,1)}, bf16[3,512,2048]{2,1,0:T(8,128)(2,1)}) custom-call(s32[4]{0:T(128)S(1)} %compare_select_fusion.owners_ref, bf16[128,2048]{1,0:T(8,128)(2,1)} %get-tuple-element.131.refs_0_, bf16[128,2048]{1,0:T(8,128)(2,1)} %collective-permute-done.10.refs_1_, ...), custom_call_target="tpu_custom_call" | custom-call | flops 12884901888 | bytes 90177552 | tf_op jit(solution)/shard_map/feed_forward/pallas_call | solution.py:162
  234.9 13.2 %feed_forward_rows_grad.1 = bf16[512,2048]{1,0:T(8,128)(2,1)S(1)} custom-call(s32[1]{0:T(128)} %constant.46.clone.1.owners_ref, bf16[3,512,2048]{2,1,0:T(8,128)(2,1)} %get-tuple-element.157.refs_0_.refs_1_.refs_16_.refs_18_.refs_20_, bf16[3,512,2048]{2,1,0:T(8,128)(2,1)} %get-tuple-element.157.refs_0_.refs_1_.refs_16_.refs_18_.refs_20_, ...), custom_call_target="tpu_custom_call" | custom-call | flops 8589934592 | bytes 39845892 | tf_op jit(solution)/shard_map/feed_forward_rows_grad/pallas_call | solution.py:162
  250.1 5.9 %collective-permute-done.17.refs_4_.refs_5_.refs_6_.refs_7_ = bf16[512,2048]{1,0:T(8,128)(2,1)S(1)} collective-permute-done((bf16[512,2048]{1,0:T(8,128)(2,1)S(1)}, bf16[512,2048]{1,0:T(8,128)(2,1)S(1)}, u32[]{:S(2)}, u32[]{:S(2)}) %collective-permute-start.17) | collective-permute-done | bytes 2097184 | tf_op jit(solution)/shard_map/ppermute | solution.py:100
  258.4 23.9 %feed_forward_grad.1 = (bf16[512,3072]{1,0:T(8,128)(2,1)}, bf16[512,3072]{1,0:T(8,128)(2,1)}, bf16[512,3072]{1,0:T(8,128)(2,1)}, bf16[512,3072]{1,0:T(8,128)(2,1)}) custom-call(s32[4]{0:T(128)S(1)} %multiply_xor_fusion.places_ref, bf16[512,2048]{1,0:T(8,128)(2,1)S(1)} %copy-done.2, bf16[512,2048]{1,0:T(8,128)(2,1)S(1)} %copy-done.2, ...), custom_call_target="tpu_custom_call" | custom-call | flops 12884901888 | bytes 83886096 | tf_op jit(solution)/shard_map/feed_forward_grad/pallas_call | solution.py:162
  282.3 23.1 %reduce-scatter.4.cloned.1.call-done = bf16[128,2048]{1,0:T(8,128)(2,1)} async-done(((bf16[512,2048]{1,0:T(8,128)(2,1)}), bf16[128,2048]{1,0:T(8,128)(2,1)}) %reduce-scatter.4.cloned.1.call-update) | async-done | bytes 524304 | tf_op jit(solution)/shard_map/reduce_scatter | solution.py:609
  313.0 8.9 %block_out.1 = bf16[512,2048]{1,0:T(8,128)(2,1)} custom-call(s32[1]{0:T(128)} %constant.46.clone.1.owners_ref, bf16[3,512,2048]{2,1,0:T(8,128)(2,1)} %get-tuple-element.157.refs_0_.refs_1_.refs_16_.refs_18_.refs_20_, bf16[2048,6144]{1,0:T(8,128)(2,1)} %all-gather.6.cloned.1.call-done.refs_8_.refs_9_.refs_10_.refs_2_.refs_1_), custom_call_target="tpu_custom_call" | custom-call | flops 4294967296 | bytes 33554436 | tf_op jit(solution)/shard_map/block_out/pallas_call | solution.py:162
  321.9 33.4 %all-gather.8.cloned.1.call-done.grad_ref.refs_0_.refs_1_.refs_2_.refs_3_ = bf16[512,2048]{1,0:T(8,128)(2,1)} async-done(((bf16[128,2048]{1,0:T(8,128)(2,1)}), bf16[512,2048]{1,0:T(8,128)(2,1)}) %all-gather.8.cloned.1.call-update) | async-done | bytes 2097168 | tf_op jit(solution)/shard_map/all_gather | solution.py:624
  357.4 15.5 %attention_backward.1 = bf16[512,768]{1,0:T(8,128)(2,1)S(1)} custom-call(s32[24]{0:T(128)S(1)} %compare_select_fusion.2.ends_ref, bf16[512,2048]{1,0:T(8,128)(2,1)S(1)} %copy-done, bf16[2048,1280]{1,0:T(8,128)(2,1)} %all-gather.4.cloned.1.call-done.refs_5_.refs_1_.w_ref, bf16[512,768]{1,0:T(8,128)(2,1)S(1)} %copy-done.10, ...), custom_call_target="tpu_custom_call" | custom-call | flops 2415919104 | bytes 9699424 | tf_op jit(solution)/shard_map/attention_backward/pallas_call | solution.py:162
  373.4 6.7 %collective-permute-done.22 = bf16[512,3072]{1,0:T(8,128)(2,1)} collective-permute-done((bf16[512,3072]{1,0:T(8,128)(2,1)}, bf16[512,3072]{1,0:T(8,128)(2,1)}, u32[]{:S(2)}, u32[]{:S(2)}) %collective-permute-start.22) | collective-permute-done | bytes 3145760 | tf_op jit(solution)/shard_map/ppermute | solution.py:100
  389.6 4.9 %attention_rows_grad.1 = bf16[512,2048]{1,0:T(8,128)(2,1)} custom-call(s32[1]{0:T(128)} %constant.46.clone.1.owners_ref, bf16[1,512,768]{2,1,0:T(8,128)(2,1)S(1)} %bitcast.26, bf16[2048,1280]{1,0:T(8,128)(2,1)} %all-gather.4.cloned.1.call-done.refs_5_.refs_1_.w_ref), custom_call_target="tpu_custom_call" | custom-call | flops 1610612736 | bytes 8126468 | tf_op jit(solution)/shard_map/attention_rows_grad/pallas_call | solution.py:162
  395.6 9.6 %attention_grad.1 = (bf16[512,768]{1,0:T(8,128)(2,1)S(1)}, bf16[512,768]{1,0:T(8,128)(2,1)}, bf16[512,512]{1,0:T(8,128)(2,1)S(1)}, bf16[512,512]{1,0:T(8,128)(2,1)}) custom-call(s32[4]{0:T(128)S(1)} %multiply_xor_fusion.places_ref, bf16[512,2048]{1,0:T(8,128)(2,1)} %all-gather.8.cloned.1.call-done.grad_ref.refs_0_.refs_1_.refs_2_.refs_3_, ...), custom_call_target="tpu_custom_call" | custom-call | flops 2684354560 | bytes 38797328 | tf_op jit(solution)/shard_map/attention_grad/pallas_call | solution.py:162
  410.4 20.3 %collective-permute-done.25 = bf16[512,512]{1,0:T(8,128)(2,1)S(1)} collective-permute-done((bf16[512,512]{1,0:T(8,128)(2,1)}, bf16[512,512]{1,0:T(8,128)(2,1)S(1)}, u32[]{:S(2)}, u32[]{:S(2)}) %collective-permute-start.25) | collective-permute-done | bytes 524320 | tf_op jit(solution)/shard_map/ppermute | solution.py:100
  430.6 10.1 %collective-permute-done.24 = bf16[512,768]{1,0:T(8,128)(2,1)} collective-permute-done((bf16[512,768]{1,0:T(8,128)(2,1)}, bf16[512,768]{1,0:T(8,128)(2,1)}, u32[]{:S(2)}, u32[]{:S(2)}) %collective-permute-start.24) | collective-permute-done | bytes 786464 | tf_op jit(solution)/shard_map/ppermute | solution.py:100
  443.2 5.0 %convert_add_fusion = (f32[256,3072]{1,0:T(8,128)S(1)}, f32[256,3072]{1,0:T(8,128)S(1)}) fusion(bf16[256,3072]{1,0:T(8,128)(2,1)} %collective-permute-done.29, bf16[512,3072]{1,0:T(8,128)(2,1)} %collective-permute-done.23, bf16[512,3072]{1,0:T(8,128)(2,1)} %get-tuple-element.206, bf16[256,3072]{1,0:T(8,128)(2,1)} %collective-permute-done.28, ...), kind=kLoop, calls=%fused_computation.1 | loop fusion | flops 7864320 | bytes 15728640 | tf_op jit(solution)/shard_map/add | solution.py:150
  (200 shorter events, 110.8 us)
Async XLA Ops:
  7.2 61.5 %all-gather.4.cloned.1.call-start = ((), (), s32[]{:S(2)}) async-start(), calls=%async_computation.3 | async-start | bytes 5898240 | tf_op jit(solution)/shard_map/all_gather | solution.py:574
  10.4 171.3 %all-gather.6.cloned.1.call-start = ((), (), s32[]{:S(2)}) async-start(), calls=%async_computation.4 | async-start | bytes 28311552 | tf_op jit(solution)/shard_map/all_gather | solution.py:575
  15.6 289.8 %reduce-scatter.4.cloned.1.call-start = ((), (), s32[]{:S(2)}) async-start(), calls=%async_computation.5 | async-start | bytes 2621440 | tf_op jit(solution)/shard_map/reduce_scatter | solution.py:609
  19.6 36.6 %collective-permute-start.1 = (bf16[128,2048]{1,0:T(8,128)(2,1)S(1)}, bf16[128,2048]{1,0:T(8,128)(2,1)S(1)}, u32[]{:S(2)}, u32[]{:S(2)}) collective-permute-start(bf16[128,2048]{1,0:T(8,128)(2,1)S(1)} %copy-done.3), channel_id=1, source_target_pairs={{0,2},{1,3},{2,0},{3,1},{4,6},{5,7},{6,4},{7,5},{8,10},{9,11},{10,... | collective-permute-start | bytes 1572872 | tf_op jit(solution)/shard_map/ppermute | solution.py:81
  22.2 34.8 %collective-permute-start.2 = (bf16[128,2048]{1,0:T(8,128)(2,1)S(1)}, bf16[128,2048]{1,0:T(8,128)(2,1)S(1)}, u32[]{:S(2)}, u32[]{:S(2)}) collective-permute-start(bf16[128,2048]{1,0:T(8,128)(2,1)S(1)} %copy-done.3), channel_id=1, source_target_pairs={{0,3},{1,0},{2,1},{3,2},{4,7},{5,4},{6,5},{7,6},{8,11},{9,8},{10,9... | collective-permute-start | bytes 1572872 | tf_op jit(solution)/shard_map/ppermute | solution.py:81
  57.8 35.0 %collective-permute-start.6 = (bf16[128,2048]{1,0:T(8,128)(2,1)}, bf16[128,2048]{1,0:T(8,128)(2,1)}, u32[]{:S(2)}, u32[]{:S(2)}) collective-permute-start(bf16[128,2048]{1,0:T(8,128)(2,1)} %refs_4_), channel_id=1, source_target_pairs={{0,1},{1,2},{2,3},{3,0},{4,5},{5,6},{6,7},{7,4},{8,9},{9,10},{10,1... | collective-permute-start | bytes 1572872 | tf_op jit(solution)/shard_map/ppermute | solution.py:81
  77.4 95.1 %collective-permute-start.15 = (bf16[512,2048]{1,0:T(8,128)(2,1)S(1)}, bf16[512,2048]{1,0:T(8,128)(2,1)}, u32[]{:S(2)}, u32[]{:S(2)}) collective-permute-start(bf16[512,2048]{1,0:T(8,128)(2,1)S(1)} %get-tuple-element.177.refs_8_.refs_9_.refs_10_.refs_11_), channel_id=1, source_target_pairs={{0,4},{4,0},{8,12},{12,8},{16,20},{20,16},{24,28},{28,24},{1,5},{5... | collective-permute-start | bytes 6291464 | tf_op jit(solution)/shard_map/ppermute | solution.py:100
  98.2 58.2 %collective-permute-start.8 = (bf16[128,2048]{1,0:T(8,128)(2,1)S(1)}, bf16[128,2048]{1,0:T(8,128)(2,1)S(1)}, u32[]{:S(2)}, u32[]{:S(2)}) collective-permute-start(bf16[128,2048]{1,0:T(8,128)(2,1)S(1)} %get-tuple-element.123), channel_id=1, source_target_pairs={{0,2},{1,3},{2,0},{3,1},{4,6},{5,7},{6,4},{7,5},{8,10},{9,11},{10,... | collective-permute-start | bytes 1572872 | tf_op jit(solution)/shard_map/ppermute | solution.py:81
  98.8 57.7 %collective-permute-start.9 = (bf16[128,2048]{1,0:T(8,128)(2,1)S(1)}, bf16[128,2048]{1,0:T(8,128)(2,1)S(1)}, u32[]{:S(2)}, u32[]{:S(2)}) collective-permute-start(bf16[128,2048]{1,0:T(8,128)(2,1)S(1)} %get-tuple-element.124), channel_id=1, source_target_pairs={{0,1},{1,2},{2,3},{3,0},{4,5},{5,6},{6,7},{7,4},{8,9},{9,10},{10,1... | collective-permute-start | bytes 1572872 | tf_op jit(solution)/shard_map/ppermute | solution.py:81
  100.8 89.4 %collective-permute-start.13 = (bf16[128,2048]{1,0:T(8,128)(2,1)}, bf16[128,2048]{1,0:T(8,128)(2,1)}, u32[]{:S(2)}, u32[]{:S(2)}) collective-permute-start(bf16[128,2048]{1,0:T(8,128)(2,1)} %refs_4_), channel_id=1, source_target_pairs={{0,2},{1,3},{2,0},{3,1},{4,6},{5,7},{6,4},{7,5},{8,10},{9,11},{10,... | collective-permute-start | bytes 1572872 | tf_op jit(solution)/shard_map/ppermute | solution.py:81
  110.6 79.7 %collective-permute-start.14 = (bf16[128,2048]{1,0:T(8,128)(2,1)}, bf16[128,2048]{1,0:T(8,128)(2,1)}, u32[]{:S(2)}, u32[]{:S(2)}) collective-permute-start(bf16[128,2048]{1,0:T(8,128)(2,1)} %refs_4_), channel_id=1, source_target_pairs={{0,3},{1,0},{2,1},{3,2},{4,7},{5,4},{6,5},{7,6},{8,11},{9,8},{10,9... | collective-permute-start | bytes 1572872 | tf_op jit(solution)/shard_map/ppermute | solution.py:81
  158.5 31.8 %collective-permute-start.10 = (bf16[128,2048]{1,0:T(8,128)(2,1)}, bf16[128,2048]{1,0:T(8,128)(2,1)}, u32[]{:S(2)}, u32[]{:S(2)}) collective-permute-start(bf16[128,2048]{1,0:T(8,128)(2,1)} %get-tuple-element.131.refs_0_), channel_id=1, source_target_pairs={{0,1},{1,2},{2,3},{3,0},{4,5},{5,6},{6,7},{7,4},{8,9},{9,10},{10,1... | collective-permute-start | bytes 1572872 | tf_op jit(solution)/shard_map/ppermute | solution.py:81
  170.6 42.1 %collective-permute-start.11 = (bf16[128,2048]{1,0:T(8,128)(2,1)}, bf16[128,2048]{1,0:T(8,128)(2,1)}, u32[]{:S(2)}, u32[]{:S(2)}) collective-permute-start(bf16[128,2048]{1,0:T(8,128)(2,1)} %get-tuple-element.131.refs_0_), channel_id=1, source_target_pairs={{0,2},{1,3},{2,0},{3,1},{4,6},{5,7},{6,4},{7,5},{8,10},{9,11},{10,... | collective-permute-start | bytes 1572872 | tf_op jit(solution)/shard_map/ppermute | solution.py:81
  172.5 40.2 %collective-permute-start.12 = (bf16[128,2048]{1,0:T(8,128)(2,1)}, bf16[128,2048]{1,0:T(8,128)(2,1)S(1)}, u32[]{:S(2)}, u32[]{:S(2)}) collective-permute-start(bf16[128,2048]{1,0:T(8,128)(2,1)} %get-tuple-element.131.refs_0_), channel_id=1, source_target_pairs={{0,3},{1,0},{2,1},{3,2},{4,7},{5,4},{6,5},{7,6},{8,11},{9,8},{10,9... | collective-permute-start | bytes 1572872 | tf_op jit(solution)/shard_map/ppermute | solution.py:81
  249.4 105.9 %all-gather.8.cloned.1.call-start = ((), (), s32[]{:S(2)}) async-start(), calls=%async_computation.6 | async-start | bytes 2621440 | tf_op jit(solution)/shard_map/all_gather | solution.py:624
  310.0 98.2 %reduce-scatter.6.cloned.1.call-start = ((), (), s32[]{:S(2)}) async-start(), calls=%async_computation.7 | async-start | bytes 2621440 | tf_op jit(solution)/shard_map/reduce_scatter | solution.py:627
  310.0 70.1 %collective-permute-start.22 = (bf16[512,3072]{1,0:T(8,128)(2,1)}, bf16[512,3072]{1,0:T(8,128)(2,1)}, u32[]{:S(2)}, u32[]{:S(2)}) collective-permute-start(bf16[512,3072]{1,0:T(8,128)(2,1)} %get-tuple-element.168), channel_id=1, source_target_pairs={{0,16},{4,20},{8,24},{12,28},{16,0},{20,4},{24,8},{28,12},{1,17},{... | collective-permute-start | bytes 9437192 | tf_op jit(solution)/shard_map/ppermute | solution.py:100
  311.6 69.7 %collective-permute-start.23 = (bf16[512,3072]{1,0:T(8,128)(2,1)}, bf16[512,3072]{1,0:T(8,128)(2,1)}, u32[]{:S(2)}, u32[]{:S(2)}) collective-permute-start(bf16[512,3072]{1,0:T(8,128)(2,1)} %get-tuple-element.170), channel_id=1, source_target_pairs={{0,8},{4,12},{8,0},{12,4},{16,24},{20,28},{24,16},{28,20},{1,9},{5... | collective-permute-start | bytes 9437192 | tf_op jit(solution)/shard_map/ppermute | solution.py:100
  355.4 109.0 %reduce-scatter.8.cloned.1.call-start = ((), (), s32[]{:S(2)}) async-start(), calls=%async_computation.8 | async-start | bytes 2621440 | tf_op jit(solution)/shard_map/reduce_scatter | solution.py:637
  355.7 38.8 %collective-permute-start.20 = (bf16[512,2048]{1,0:T(8,128)(2,1)}, bf16[512,2048]{1,0:T(8,128)(2,1)}, u32[]{:S(2)}, u32[]{:S(2)}) collective-permute-start(bf16[512,2048]{1,0:T(8,128)(2,1)} %all-gather.8.cloned.1.call-done.grad_ref.refs_0_.refs_1_.refs_2_.refs_3_), channel_id=1, source_target_pairs={{0,4},{4,0},{8,12},{12,8},{16,20},{20,16},{24,28},{28,24},{1,5},{5... | collective-permute-start | bytes 6291464 | tf_op jit(solution)/shard_map/ppermute | solution.py:100
  384.4 58.0 %collective-permute-start.28 = (bf16[256,3072]{1,0:T(8,128)(2,1)}, bf16[256,3072]{1,0:T(8,128)(2,1)}, u32[]{:S(2)}, u32[]{:S(2)}) collective-permute-start(bf16[256,3072]{1,0:T(8,128)(2,1)} %add_convert_fusion.1), channel_id=1, source_target_pairs={{0,8},{4,12},{8,0},{12,4},{16,24},{20,28},{24,16},{28,20},{1,9},{5... | collective-permute-start | bytes 4718600 | tf_op jit(solution)/shard_map/ppermute | solution.py:100
  389.1 53.4 %collective-permute-start.29 = (bf16[256,3072]{1,0:T(8,128)(2,1)}, bf16[256,3072]{1,0:T(8,128)(2,1)}, u32[]{:S(2)}, u32[]{:S(2)}) collective-permute-start(bf16[256,3072]{1,0:T(8,128)(2,1)} %add_convert_fusion), channel_id=1, source_target_pairs={{0,16},{4,20},{8,24},{12,28},{16,0},{20,4},{24,8},{28,12},{1,17},{... | collective-permute-start | bytes 4718600 | tf_op jit(solution)/shard_map/ppermute | solution.py:100
  406.0 34.8 %collective-permute-start.24 = (bf16[512,768]{1,0:T(8,128)(2,1)}, bf16[512,768]{1,0:T(8,128)(2,1)}, u32[]{:S(2)}, u32[]{:S(2)}) collective-permute-start(bf16[512,768]{1,0:T(8,128)(2,1)} %get-tuple-element.192), channel_id=1, source_target_pairs={{0,16},{4,20},{8,24},{12,28},{16,0},{20,4},{24,8},{28,12},{1,17},{... | collective-permute-start | bytes 2359304 | tf_op jit(solution)/shard_map/ppermute | solution.py:100
  407.7 23.0 %collective-permute-start.25 = (bf16[512,512]{1,0:T(8,128)(2,1)}, bf16[512,512]{1,0:T(8,128)(2,1)S(1)}, u32[]{:S(2)}, u32[]{:S(2)}) collective-permute-start(bf16[512,512]{1,0:T(8,128)(2,1)} %get-tuple-element.194), channel_id=1, source_target_pairs={{0,8},{4,12},{8,0},{12,4},{16,24},{20,28},{24,16},{28,20},{1,9},{5... | collective-permute-start | bytes 1572872 | tf_op jit(solution)/shard_map/ppermute | solution.py:100
  (52 other events, 509.0 us)
Sparse Core Ops, SparseCore 0:
  10.5 43.9 all-gather.3
  56.4 125.3 all-gather.5
  249.6 55.7 reduce-scatter.3
  310.1 45.2 all-gather.7
  358.2 42.4 reduce-scatter.5
  408.3 42.5 reduce-scatter.7

commit v5 on v4

--- a/solution.py
+++ b/solution.py
@@ -171,40 +171,6 @@
 
 def whole(shape):
     return pl.BlockSpec(shape, lambda *_: (0,) * len(shape))
-
-
-def attention_in(x_blocks, gain, w, skip, owners):
-    count = len(x_blocks)
-    rows, features = x_blocks[0].shape
-    total, width = rows * count, w.shape[1] - skip
-    tile = math.gcd(math.gcd(width, skip), 256)
-
-    def body(owners_ref, *refs):
-        x_refs, (gain_ref, w_ref, h_ref, out_ref) = refs[:count], refs[count:]
-
-        @pl.when(pl.program_id(0) == 0)
-        def _():
-            for r in range(count):
-                normed, _ = norm_parts(x_refs[r][...].astype(F32))
-                at = pl.multiple_of(owners_ref[r] * rows, rows)
-                h_ref[pl.ds(at, rows), :] = (normed * gain_ref[...]).astype(BF16)
-
-        out_ref[...] = mm(h_ref[...], w_ref[...])
-
-    return kernel_call(
-        body,
-        "attention_in",
-        2 * total * features * width,
-        (owners, *x_blocks, gain, w),
-        (jax.ShapeDtypeStruct((total, features), BF16), jax.ShapeDtypeStruct((total, width), F32)),
-        grid_spec=pltpu.PrefetchScalarGridSpec(
-            num_scalar_prefetch=1,
-            grid=(width // tile,),
-            in_specs=[whole((rows, features))] * count
-            + [whole((1, features)), pl.BlockSpec((features, tile), lambda j, _: (0, skip // tile + j))],
-            out_specs=[whole((total, features)), pl.BlockSpec((total, tile), lambda j, _: (0, j))],
-        ),
-    )
 
 
 def feed_forward(h_blocks, c_blocks, w, owners):
@@ -415,58 +381,87 @@
         write(cut, turned(read(cut), cosine, sine).astype(BF16))
 
 
-def attention_forward(ends, qkv, table, heads, kv):
-    rows, width = qkv.shape
+def attention_forward(ends, owners, x_blocks, gain, w, skip, table, heads, kv):
+    blocks = len(x_blocks)
+    own_rows, features = x_blocks[0].shape
+    rows, width = own_rows * blocks, w.shape[1] - skip
+    tile = math.gcd(math.gcd(width, skip), 256)
+    steps = width // tile
     block = tile_of(rows, 256)
     turn_width = (heads + kv) * HEAD_DIM
     at_sine = table.shape[1] // 2
     scale = 1.0 / math.sqrt(HEAD_DIM)
 
-    def body(ends_ref, qkv_ref, table_ref, low_ref, out_ref, mass_ref):
-        j = pl.program_id(0)
-
-        @pl.when(j == 0)
+    def body(ends_ref, owners_ref, *refs):
+        x_refs, (gain_ref, w_ref, table_ref, h_ref, low_ref, out_ref, mass_ref, qkv) = refs[:blocks], refs[blocks:]
+        step = pl.program_id(0)
+
+        @pl.when(step == 0)
+        def _():
+            for r in range(blocks):
+                normed, _ = norm_parts(x_refs[r][...].astype(F32))
+                at = pl.multiple_of(owners_ref[r] * own_rows, own_rows)
+                h_ref[pl.ds(at, own_rows), :] = (normed * gain_ref[...]).astype(BF16)
+
+        for k in range(steps):
+
+            @pl.when(step == k)
+            def _(k=k):
+                qkv[:, k * tile : (k + 1) * tile] = mm(h_ref[...], w_ref[...])
+
+        @pl.when(step == steps)
         def _():
             def write(cut, v):
                 low_ref[:, cut] = v
 
-            turn_heads(lambda cut: qkv_ref[:, cut], write, turn_width, table_ref[:, :at_sine], table_ref[:, at_sine:])
-            low_ref[:, turn_width:] = qkv_ref[:, turn_width:].astype(BF16)
-
-        allowed = allowed_pairs(ends_ref, ends.shape[0], j, block, rows)
-        here = pl.ds(pl.multiple_of(j * block, block), block)
-        lane = lax.broadcasted_iota(jnp.int32, (block, 128), 1)
-        mass = jnp.zeros((block, 128), F32)
-        for h, (q_at, k_at, v_at) in enumerate(head_columns(heads, kv)):
-            scores = outer(low_ref[here, q_at], low_ref[:, k_at]) * scale
-            scores = jnp.where(allowed, scores, -1e30)
-            row_max = jnp.max(scores, axis=1, keepdims=True)
-            weights = jnp.exp(scores - row_max)
-            row_sum = jnp.sum(weights, axis=1, keepdims=True)
-            weights_low = (weights / row_sum).astype(BF16)
-            out_ref[:, q_at] = mm(weights_low, low_ref[:, v_at]).astype(BF16)
-            mass = jnp.where(lane == h, row_max + jnp.log(row_sum), mass)
-        mass_ref[...] = mass
+            turn_heads(lambda cut: qkv[:, cut], write, turn_width, table_ref[:, :at_sine], table_ref[:, at_sine:])
+            low_ref[:, turn_width:] = qkv[:, turn_width:].astype(BF16)
+
+        @pl.when(step >= steps)
+        def _():
+            j = step - steps
+            allowed = allowed_pairs(ends_ref, ends.shape[0], j, block, rows)
+            here = pl.ds(pl.multiple_of(j * block, block), block)
+            lane = lax.broadcasted_iota(jnp.int32, (block, 128), 1)
+            mass = jnp.zeros((block, 128), F32)
+            for h, (q_at, k_at, v_at) in enumerate(head_columns(heads, kv)):
+                scores = outer(low_ref[here, q_at], low_ref[:, k_at]) * scale
+                scores = jnp.where(allowed, scores, -1e30)
+                row_max = jnp.max(scores, axis=1, keepdims=True)
+                weights = jnp.exp(scores - row_max)
+                row_sum = jnp.sum(weights, axis=1, keepdims=True)
+                weights_low = (weights / row_sum).astype(BF16)
+                out_ref[:, q_at] = mm(weights_low, low_ref[:, v_at]).astype(BF16)
+                mass = jnp.where(lane == h, row_max + jnp.log(row_sum), mass)
+            mass_ref[...] = mass
 
     return kernel_call(
         body,
         "attention_forward",
-        4 * rows * rows * heads * HEAD_DIM,
-        (ends, qkv, table),
+        4 * rows * rows * heads * HEAD_DIM + 2 * rows * features * width,
+        (ends, owners, *x_blocks, gain, w, table),
         (
+            jax.ShapeDtypeStruct((rows, features), BF16),
             jax.ShapeDtypeStruct((rows, width), BF16),
             jax.ShapeDtypeStruct((rows, heads * HEAD_DIM), BF16),
             jax.ShapeDtypeStruct((rows, 128), F32),
         ),
         grid_spec=pltpu.PrefetchScalarGridSpec(
-            num_scalar_prefetch=1,
-            grid=(rows // block,),
-            in_specs=[whole((rows, width)), whole(table.shape)],
+            num_scalar_prefetch=2,
+            grid=(steps + rows // block,),
+            in_specs=[whole((own_rows, features))] * blocks
+            + [
+                whole((1, features)),
+                pl.BlockSpec((features, tile), lambda j, *_: (0, skip // tile + jnp.minimum(j, steps - 1))),
+                whole(table.shape),
+            ],
             out_specs=[
+                whole((rows, features)),
                 whole((rows, width)),
-                pl.BlockSpec((block, heads * HEAD_DIM), lambda j, _: (j, 0)),
-                pl.BlockSpec((block, 128), lambda j, _: (j, 0)),
+                pl.BlockSpec((block, heads * HEAD_DIM), lambda j, *_: (jnp.maximum(j - steps, 0), 0)),
+                pl.BlockSpec((block, 128), lambda j, *_: (jnp.maximum(j - steps, 0), 0)),
             ],
+            scratch_shapes=[pltpu.VMEM((rows, width), F32)],
         ),
     )
 
@@ -576,18 +571,21 @@
     incoming_blocks = line.gather(after(cotangent, *rows_all))
 
     order = Order()
-    attn_input, qkv = order(
-        lambda *a: attention_in(a[:-2], a[-2], a[-1], width_out, line.owners), *rows_all, gain_one, w_attn
+    heads_here = width_q // HEAD_DIM
+    kv_here = width_k // HEAD_DIM
+    ends, position = layout(seq_lengths, seq_group, cube.me, row_count)
+    table = order(lambda p: rope_tables(p, HEAD_DIM), position)
+    attn_input, low_qkv, attended, log_mass = order(
+        lambda e, x, g, w, t: attention_forward(e, line.owners, x, g, w, width_out, t, heads_here, kv_here),
+        ends,
+        rows_all,
+        gain_one,
+        w_attn,
+        table,
     )
     attn_input_other = cube.swap(attn_input, 1)
     tokens_f = tokens.astype(F32)
     normed_one, factor_one = norm_parts(tokens_f)
-    heads_here = width_q // HEAD_DIM
-    kv_here = width_k // HEAD_DIM
-    ends, position = layout(seq_lengths, seq_group, cube.me, row_count)
-    table = rope_tables(position, HEAD_DIM)
-    low_qkv, attended, log_mass = order(lambda *a: attention_forward(*a, heads_here, kv_here), ends, qkv, table)
-
     out_parts = order(
         lambda a, w: rows_product(a, [0], w, 0, "attention_out", line.owners),
         after(attended, incoming_blocks[1])[None],

time: 476 us -> 476 us (level); the launches traced: 475 us -> 467 us
    all_gather x1, waiting for transfers between devices: 6.28 us -> 11.6 us  [per_device(): lax.all_gather(jnp.concatenate([w_gate, w_up, w_down.T], axis=1), 'dp', a...]
    ppermute x15, waiting for transfers between devices: 106 us -> 100 us  [shift(): lax.ppermute(v, 'tensor', [(i, (i + r) % self.size) for i in range(self.s...]
    pallas_call x10 -> x9, Pallas kernels: 116 us -> 117 us  [kernel_call(): pl.pallas_call(body, out_shape=out_shape, name=name, cost_estimate=pl.Cos...]
where the time goes in v5:
time: 476 us; the launch traced here: 467 us
  waiting for transfers between devices  215 us (45%)
  Pallas kernels  117 us (25%)
  starting transfers between devices  61.1 us (13%)
  other arithmetic  37.7 us (8%)
  local copies, waits for them, and re-layouts  22 us (5%)
  between operations  15.1 us (3%)
    pallas_call x9, Pallas kernels, kernel_call(): pl.pallas_call(body, out_shape=out_shape, name=name, cost_estimate=pl.Cos...  117 us
    ppermute x15, waiting for transfers between devices, shift(): lax.ppermute(v, 'tensor', [(i, (i + r) % self.size) for i in range(self.s...  100 us
    ppermute x15, starting transfers between devices, shift(): lax.ppermute(v, 'tensor', [(i, (i + r) % self.size) for i in range(self.s...  47.8 us
    ppermute x18, waiting for transfers between devices, swap(): return lax.ppermute(v, 'dp', [(i, i ^ m) for i in range(self.size)])  46 us
    all_gather x1, waiting for transfers between devices, per_device(): lax.all_gather(grad_residual.astype(BF16), 'tensor', axis=0, tiled=True)  33.4 us
    reduce_scatter x1, waiting for transfers between devices, per_device(): lax.psum_scatter(two_parts, 'tensor', scatter_dimension=0, tiled=True)  23 us
    unnamed x78, local copies, waits for them, and re-layouts  20.2 us
    ppermute x18, starting transfers between devices, swap(): return lax.ppermute(v, 'dp', [(i, i ^ m) for i in range(self.size)])  12.8 us
  transfers between devices with their start and end apart: 39, of which 18 were waited for; matrix products, arithmetic and copies ran while one was open for 8% of the time, Pallas kernels for 20%

profile of v5, /device:TPU:0, one launch (start us, length us, event | category | flops | bytes accessed | tf_op | source)
XLA Modules:
  0.0 467.4 jit_solution(4223531318279644591)
XLA Ops:
  34.5 21.6 %collective-permute-done.1.refs_2_ = bf16[128,2048]{1,0:T(8,128)(2,1)S(1)} collective-permute-done((bf16[128,2048]{1,0:T(8,128)(2,1)S(1)}, bf16[128,2048]{1,0:T(8,128)(2,1)S(1)}, u32[]{:S(2)}, u32[]{:S(2)}) %collective-permute-start.1) | collective-permute-done | bytes 524320 | tf_op jit(solution)/shard_map/ppermute | solution.py:81
  57.7 10.9 %collective-permute-start.6 = (bf16[128,2048]{1,0:T(8,128)(2,1)S(1)}, bf16[128,2048]{1,0:T(8,128)(2,1)S(1)}, u32[]{:S(2)}, u32[]{:S(2)}) collective-permute-start(bf16[128,2048]{1,0:T(8,128)(2,1)S(1)} %copy-done.4), channel_id=1, source_target_pairs={{0,1},{1,2},{2,3},{3,0},{4,5},{5,6},{6,7},{7,4},{8,9},{9,10},{10,1... | collective-permute-start | bytes 1572872 | tf_op jit(solution)/shard_map/ppermute | solution.py:81
  71.0 15.6 %attention_forward.1 = (bf16[512,2048]{1,0:T(8,128)(2,1)}, bf16[512,768]{1,0:T(8,128)(2,1)S(1)}, bf16[512,512]{1,0:T(8,128)(2,1)S(1)}, f32[512,128]{1,0:T(8,128)S(1)}) custom-call(s32[24]{0:T(128)S(1)} %compare_select_fusion.2.ends_ref, s32[4]{0:T(128)S(1)} %compare_select_fusion.owners_ref, bf16[128,2048]{1,0:T(8,128)(2,1)S(1)} %copy-done.3, ...), custom_call_target="tpu_custom_call" | custom-call | flops 2147483648 | bytes 11542640 | tf_op jit(solution)/shard_map/attention_forward/pallas_call | solution.py:162
  96.1 9.2 %collective-permute-done.7 = bf16[128,2048]{1,0:T(8,128)(2,1)S(1)} collective-permute-done((bf16[128,2048]{1,0:T(8,128)(2,1)S(1)}, bf16[128,2048]{1,0:T(8,128)(2,1)S(1)}, u32[]{:S(2)}, u32[]{:S(2)}) %collective-permute-start.7) | collective-permute-done | bytes 524320 | tf_op jit(solution)/shard_map/ppermute | solution.py:81
  105.3 4.3 collective-permute-start.14
  109.6 41.6 %collective-permute-done.8 = bf16[128,2048]{1,0:T(8,128)(2,1)S(1)} collective-permute-done((bf16[128,2048]{1,0:T(8,128)(2,1)S(1)}, bf16[128,2048]{1,0:T(8,128)(2,1)S(1)}, u32[]{:S(2)}, u32[]{:S(2)}) %collective-permute-start.8) | collective-permute-done | bytes 524320 | tf_op jit(solution)/shard_map/ppermute | solution.py:81
  153.0 11.3 %collective-permute-start.10 = (bf16[128,2048]{1,0:T(8,128)(2,1)S(1)}, bf16[128,2048]{1,0:T(8,128)(2,1)}, u32[]{:S(2)}, u32[]{:S(2)}) collective-permute-start(bf16[128,2048]{1,0:T(8,128)(2,1)S(1)} %get-tuple-element.138.refs_0_), channel_id=1, source_target_pairs={{0,1},{1,2},{2,3},{3,0},{4,5},{5,6},{6,7},{7,4},{8,9},{9,10},{10,1... | collective-permute-start | bytes 1572872 | tf_op jit(solution)/shard_map/ppermute | solution.py:81
  170.1 11.6 %all-gather.6.cloned.1.call-done.refs_8_.refs_9_.refs_10_.refs_2_.refs_1_ = bf16[2048,6144]{1,0:T(8,128)(2,1)} async-done(((bf16[256,6144]{1,0:T(8,128)(2,1)}), bf16[2048,6144]{1,0:T(8,128)(2,1)}) %all-gather.6.cloned.1.call-update) | async-done | bytes 25165840 | tf_op jit(solution)/shard_map/all_gather | solution.py:570
  184.8 22.6 %collective-permute-done.11.refs_2_ = bf16[128,2048]{1,0:T(8,128)(2,1)} collective-permute-done((bf16[128,2048]{1,0:T(8,128)(2,1)S(1)}, bf16[128,2048]{1,0:T(8,128)(2,1)}, u32[]{:S(2)}, u32[]{:S(2)}) %collective-permute-start.11) | collective-permute-done | bytes 524320 | tf_op jit(solution)/shard_map/ppermute | solution.py:81
  207.4 21.6 %feed_forward.1 = (bf16[512,2048]{1,0:T(8,128)(2,1)}, bf16[512,2048]{1,0:T(8,128)(2,1)}, bf16[3,512,2048]{2,1,0:T(8,128)(2,1)}) custom-call(s32[4]{0:T(128)S(1)} %compare_select_fusion.owners_ref, bf16[128,2048]{1,0:T(8,128)(2,1)S(1)} %get-tuple-element.138.refs_0_, bf16[128,2048]{1,0:T(8,128)(2,1)} %collective-permute-done.10.refs_1_, ...), custom_call_target="tpu_custom_call" | custom-call | flops 12884901888 | bytes 90177552 | tf_op jit(solution)/shard_map/feed_forward/pallas_call | solution.py:162
  229.1 13.2 %feed_forward_rows_grad.1 = bf16[512,2048]{1,0:T(8,128)(2,1)S(1)} custom-call(s32[1]{0:T(128)} %constant.46.clone.1.owners_ref, bf16[3,512,2048]{2,1,0:T(8,128)(2,1)} %get-tuple-element.164.refs_0_.refs_1_.refs_16_.refs_18_.refs_20_, bf16[3,512,2048]{2,1,0:T(8,128)(2,1)} %get-tuple-element.164.refs_0_.refs_1_.refs_16_.refs_18_.refs_20_, ...), custom_call_target="tpu_custom_call" | custom-call | flops 8589934592 | bytes 39845892 | tf_op jit(solution)/shard_map/feed_forward_rows_grad/pallas_call | solution.py:162
  244.4 5.9 %collective-permute-done.17.refs_4_.refs_5_.refs_6_.refs_7_ = bf16[512,2048]{1,0:T(8,128)(2,1)S(1)} collective-permute-done((bf16[512,2048]{1,0:T(8,128)(2,1)S(1)}, bf16[512,2048]{1,0:T(8,128)(2,1)S(1)}, u32[]{:S(2)}, u32[]{:S(2)}) %collective-permute-start.17) | collective-permute-done | bytes 2097184 | tf_op jit(solution)/shard_map/ppermute | solution.py:100
  252.6 24.0 %feed_forward_grad.1 = (bf16[512,3072]{1,0:T(8,128)(2,1)}, bf16[512,3072]{1,0:T(8,128)(2,1)}, bf16[512,3072]{1,0:T(8,128)(2,1)}, bf16[512,3072]{1,0:T(8,128)(2,1)}) custom-call(s32[4]{0:T(128)S(1)} %multiply_xor_fusion.places_ref, bf16[512,2048]{1,0:T(8,128)(2,1)S(1)} %copy-done.1, bf16[512,2048]{1,0:T(8,128)(2,1)S(1)} %copy-done.1, ...), custom_call_target="tpu_custom_call" | custom-call | flops 12884901888 | bytes 83886096 | tf_op jit(solution)/shard_map/feed_forward_grad/pallas_call | solution.py:162
  276.6 23.0 %reduce-scatter.4.cloned.1.call-done = bf16[128,2048]{1,0:T(8,128)(2,1)} async-done(((bf16[512,2048]{1,0:T(8,128)(2,1)}), bf16[128,2048]{1,0:T(8,128)(2,1)}) %reduce-scatter.4.cloned.1.call-update) | async-done | bytes 524304 | tf_op jit(solution)/shard_map/reduce_scatter | solution.py:607
  307.3 8.9 %block_out.1 = bf16[512,2048]{1,0:T(8,128)(2,1)} custom-call(s32[1]{0:T(128)} %constant.46.clone.1.owners_ref, bf16[3,512,2048]{2,1,0:T(8,128)(2,1)} %get-tuple-element.164.refs_0_.refs_1_.refs_16_.refs_18_.refs_20_, bf16[2048,6144]{1,0:T(8,128)(2,1)} %all-gather.6.cloned.1.call-done.refs_8_.refs_9_.refs_10_.refs_2_.refs_1_), custom_call_target="tpu_custom_call" | custom-call | flops 4294967296 | bytes 33554436 | tf_op jit(solution)/shard_map/block_out/pallas_call | solution.py:162
  316.2 33.4 %all-gather.8.cloned.1.call-done.grad_ref.refs_0_.refs_1_.refs_2_.refs_3_ = bf16[512,2048]{1,0:T(8,128)(2,1)} async-done(((bf16[128,2048]{1,0:T(8,128)(2,1)}), bf16[512,2048]{1,0:T(8,128)(2,1)}) %all-gather.8.cloned.1.call-update) | async-done | bytes 2097168 | tf_op jit(solution)/shard_map/all_gather | solution.py:622
  351.6 15.4 %attention_backward.1 = bf16[512,768]{1,0:T(8,128)(2,1)S(1)} custom-call(s32[24]{0:T(128)S(1)} %compare_select_fusion.2.ends_ref, bf16[512,2048]{1,0:T(8,128)(2,1)S(1)} %copy-done, bf16[2048,1280]{1,0:T(8,128)(2,1)} %all-gather.4.cloned.1.call-done.refs_5_.refs_1_.w_ref, bf16[512,768]{1,0:T(8,128)(2,1)S(1)} %copy-done.8, ...), custom_call_target="tpu_custom_call" | custom-call | flops 2415919104 | bytes 9699424 | tf_op jit(solution)/shard_map/attention_backward/pallas_call | solution.py:162
  367.6 6.7 %collective-permute-done.22 = bf16[512,3072]{1,0:T(8,128)(2,1)} collective-permute-done((bf16[512,3072]{1,0:T(8,128)(2,1)}, bf16[512,3072]{1,0:T(8,128)(2,1)}, u32[]{:S(2)}, u32[]{:S(2)}) %collective-permute-start.22) | collective-permute-done | bytes 3145760 | tf_op jit(solution)/shard_map/ppermute | solution.py:100
  383.8 4.8 %attention_rows_grad.1 = bf16[512,2048]{1,0:T(8,128)(2,1)} custom-call(s32[1]{0:T(128)} %constant.46.clone.1.owners_ref, bf16[1,512,768]{2,1,0:T(8,128)(2,1)S(1)} %bitcast.26, bf16[2048,1280]{1,0:T(8,128)(2,1)} %all-gather.4.cloned.1.call-done.refs_5_.refs_1_.w_ref), custom_call_target="tpu_custom_call" | custom-call | flops 1610612736 | bytes 8126468 | tf_op jit(solution)/shard_map/attention_rows_grad/pallas_call | solution.py:162
  389.7 9.8 %attention_grad.1 = (bf16[512,768]{1,0:T(8,128)(2,1)S(1)}, bf16[512,768]{1,0:T(8,128)(2,1)}, bf16[512,512]{1,0:T(8,128)(2,1)S(1)}, bf16[512,512]{1,0:T(8,128)(2,1)}) custom-call(s32[4]{0:T(128)S(1)} %multiply_xor_fusion.places_ref, bf16[512,2048]{1,0:T(8,128)(2,1)} %all-gather.8.cloned.1.call-done.grad_ref.refs_0_.refs_1_.refs_2_.refs_3_, ...), custom_call_target="tpu_custom_call" | custom-call | flops 2684354560 | bytes 38797328 | tf_op jit(solution)/shard_map/attention_grad/pallas_call | solution.py:162
  405.1 19.8 %collective-permute-done.25 = bf16[512,512]{1,0:T(8,128)(2,1)S(1)} collective-permute-done((bf16[512,512]{1,0:T(8,128)(2,1)}, bf16[512,512]{1,0:T(8,128)(2,1)S(1)}, u32[]{:S(2)}, u32[]{:S(2)}) %collective-permute-start.25) | collective-permute-done | bytes 524320 | tf_op jit(solution)/shard_map/ppermute | solution.py:100
  424.9 10.0 %collective-permute-done.24 = bf16[512,768]{1,0:T(8,128)(2,1)S(1)} collective-permute-done((bf16[512,768]{1,0:T(8,128)(2,1)}, bf16[512,768]{1,0:T(8,128)(2,1)S(1)}, u32[]{:S(2)}, u32[]{:S(2)}) %collective-permute-start.24) | collective-permute-done | bytes 786464 | tf_op jit(solution)/shard_map/ppermute | solution.py:100
  436.3 5.0 %convert_add_fusion = (f32[256,3072]{1,0:T(8,128)S(1)}, f32[256,3072]{1,0:T(8,128)S(1)}) fusion(bf16[256,3072]{1,0:T(8,128)(2,1)} %collective-permute-done.29, bf16[512,3072]{1,0:T(8,128)(2,1)} %collective-permute-done.23, bf16[512,3072]{1,0:T(8,128)(2,1)} %get-tuple-element.214, bf16[256,3072]{1,0:T(8,128)(2,1)} %collective-permute-done.28, ...), kind=kLoop, calls=%fused_computation.1 | loop fusion | flops 7864320 | bytes 15728640 | tf_op jit(solution)/shard_map/add | solution.py:150
  441.4 3.6 multiply_reduce_fusion
  (199 shorter events, 98.3 us)
Async XLA Ops:
  7.2 61.5 %all-gather.4.cloned.1.call-start = ((), (), s32[]{:S(2)}) async-start(), calls=%async_computation.3 | async-start | bytes 5898240 | tf_op jit(solution)/shard_map/all_gather | solution.py:569
  10.4 171.3 %all-gather.6.cloned.1.call-start = ((), (), s32[]{:S(2)}) async-start(), calls=%async_computation.4 | async-start | bytes 28311552 | tf_op jit(solution)/shard_map/all_gather | solution.py:570
  15.6 284.0 %reduce-scatter.4.cloned.1.call-start = ((), (), s32[]{:S(2)}) async-start(), calls=%async_computation.5 | async-start | bytes 2621440 | tf_op jit(solution)/shard_map/reduce_scatter | solution.py:607
  19.6 36.6 %collective-permute-start.1 = (bf16[128,2048]{1,0:T(8,128)(2,1)S(1)}, bf16[128,2048]{1,0:T(8,128)(2,1)S(1)}, u32[]{:S(2)}, u32[]{:S(2)}) collective-permute-start(bf16[128,2048]{1,0:T(8,128)(2,1)S(1)} %copy-done.3), channel_id=1, source_target_pairs={{0,2},{1,3},{2,0},{3,1},{4,6},{5,7},{6,4},{7,5},{8,10},{9,11},{10,... | collective-permute-start | bytes 1572872 | tf_op jit(solution)/shard_map/ppermute | solution.py:81
  22.2 34.8 %collective-permute-start.2 = (bf16[128,2048]{1,0:T(8,128)(2,1)S(1)}, bf16[128,2048]{1,0:T(8,128)(2,1)S(1)}, u32[]{:S(2)}, u32[]{:S(2)}) collective-permute-start(bf16[128,2048]{1,0:T(8,128)(2,1)S(1)} %copy-done.3), channel_id=1, source_target_pairs={{0,3},{1,0},{2,1},{3,2},{4,7},{5,4},{6,5},{7,6},{8,11},{9,8},{10,9... | collective-permute-start | bytes 1572872 | tf_op jit(solution)/shard_map/ppermute | solution.py:81
  57.7 29.7 %collective-permute-start.6 = (bf16[128,2048]{1,0:T(8,128)(2,1)S(1)}, bf16[128,2048]{1,0:T(8,128)(2,1)S(1)}, u32[]{:S(2)}, u32[]{:S(2)}) collective-permute-start(bf16[128,2048]{1,0:T(8,128)(2,1)S(1)} %copy-done.4), channel_id=1, source_target_pairs={{0,1},{1,2},{2,3},{3,0},{4,5},{5,6},{6,7},{7,4},{8,9},{9,10},{10,1... | collective-permute-start | bytes 1572872 | tf_op jit(solution)/shard_map/ppermute | solution.py:81
  87.4 79.6 %collective-permute-start.15 = (bf16[512,2048]{1,0:T(8,128)(2,1)}, bf16[512,2048]{1,0:T(8,128)(2,1)}, u32[]{:S(2)}, u32[]{:S(2)}) collective-permute-start(bf16[512,2048]{1,0:T(8,128)(2,1)} %get-tuple-element.185.refs_8_.refs_9_.refs_10_.refs_11_), channel_id=1, source_target_pairs={{0,4},{4,0},{8,12},{12,8},{16,20},{20,16},{24,28},{28,24},{1,5},{5... | collective-permute-start | bytes 6291464 | tf_op jit(solution)/shard_map/ppermute | solution.py:100
  92.9 58.2 %collective-permute-start.8 = (bf16[128,2048]{1,0:T(8,128)(2,1)S(1)}, bf16[128,2048]{1,0:T(8,128)(2,1)S(1)}, u32[]{:S(2)}, u32[]{:S(2)}) collective-permute-start(bf16[128,2048]{1,0:T(8,128)(2,1)S(1)} %get-tuple-element.130), channel_id=1, source_target_pairs={{0,2},{1,3},{2,0},{3,1},{4,6},{5,7},{6,4},{7,5},{8,10},{9,11},{10,... | collective-permute-start | bytes 1572872 | tf_op jit(solution)/shard_map/ppermute | solution.py:81
  93.5 57.7 %collective-permute-start.9 = (bf16[128,2048]{1,0:T(8,128)(2,1)S(1)}, bf16[128,2048]{1,0:T(8,128)(2,1)S(1)}, u32[]{:S(2)}, u32[]{:S(2)}) collective-permute-start(bf16[128,2048]{1,0:T(8,128)(2,1)S(1)} %get-tuple-element.131), channel_id=1, source_target_pairs={{0,1},{1,2},{2,3},{3,0},{4,5},{5,6},{6,7},{7,4},{8,9},{9,10},{10,1... | collective-permute-start | bytes 1572872 | tf_op jit(solution)/shard_map/ppermute | solution.py:81
  95.5 89.3 %collective-permute-start.13 = (bf16[128,2048]{1,0:T(8,128)(2,1)S(1)}, bf16[128,2048]{1,0:T(8,128)(2,1)S(1)}, u32[]{:S(2)}, u32[]{:S(2)}) collective-permute-start(bf16[128,2048]{1,0:T(8,128)(2,1)S(1)} %copy-done.4), channel_id=1, source_target_pairs={{0,2},{1,3},{2,0},{3,1},{4,6},{5,7},{6,4},{7,5},{8,10},{9,11},{10,... | collective-permute-start | bytes 1572872 | tf_op jit(solution)/shard_map/ppermute | solution.py:81
  105.3 79.6 %collective-permute-start.14 = (bf16[128,2048]{1,0:T(8,128)(2,1)S(1)}, bf16[128,2048]{1,0:T(8,128)(2,1)}, u32[]{:S(2)}, u32[]{:S(2)}) collective-permute-start(bf16[128,2048]{1,0:T(8,128)(2,1)S(1)} %copy-done.4), channel_id=1, source_target_pairs={{0,3},{1,0},{2,1},{3,2},{4,7},{5,4},{6,5},{7,6},{8,11},{9,8},{10,9... | collective-permute-start | bytes 1572872 | tf_op jit(solution)/shard_map/ppermute | solution.py:81
  153.0 31.9 %collective-permute-start.10 = (bf16[128,2048]{1,0:T(8,128)(2,1)S(1)}, bf16[128,2048]{1,0:T(8,128)(2,1)}, u32[]{:S(2)}, u32[]{:S(2)}) collective-permute-start(bf16[128,2048]{1,0:T(8,128)(2,1)S(1)} %get-tuple-element.138.refs_0_), channel_id=1, source_target_pairs={{0,1},{1,2},{2,3},{3,0},{4,5},{5,6},{6,7},{7,4},{8,9},{9,10},{10,1... | collective-permute-start | bytes 1572872 | tf_op jit(solution)/shard_map/ppermute | solution.py:81
  165.1 42.3 %collective-permute-start.11 = (bf16[128,2048]{1,0:T(8,128)(2,1)S(1)}, bf16[128,2048]{1,0:T(8,128)(2,1)}, u32[]{:S(2)}, u32[]{:S(2)}) collective-permute-start(bf16[128,2048]{1,0:T(8,128)(2,1)S(1)} %get-tuple-element.138.refs_0_), channel_id=1, source_target_pairs={{0,2},{1,3},{2,0},{3,1},{4,6},{5,7},{6,4},{7,5},{8,10},{9,11},{10,... | collective-permute-start | bytes 1572872 | tf_op jit(solution)/shard_map/ppermute | solution.py:81
  167.0 40.4 %collective-permute-start.12 = (bf16[128,2048]{1,0:T(8,128)(2,1)S(1)}, bf16[128,2048]{1,0:T(8,128)(2,1)}, u32[]{:S(2)}, u32[]{:S(2)}) collective-permute-start(bf16[128,2048]{1,0:T(8,128)(2,1)S(1)} %get-tuple-element.138.refs_0_), channel_id=1, source_target_pairs={{0,3},{1,0},{2,1},{3,2},{4,7},{5,4},{6,5},{7,6},{8,11},{9,8},{10,9... | collective-permute-start | bytes 1572872 | tf_op jit(solution)/shard_map/ppermute | solution.py:81
  243.7 106.0 %all-gather.8.cloned.1.call-start = ((), (), s32[]{:S(2)}) async-start(), calls=%async_computation.6 | async-start | bytes 2621440 | tf_op jit(solution)/shard_map/all_gather | solution.py:622
  304.2 98.4 %reduce-scatter.6.cloned.1.call-start = ((), (), s32[]{:S(2)}) async-start(), calls=%async_computation.7 | async-start | bytes 2621440 | tf_op jit(solution)/shard_map/reduce_scatter | solution.py:625
  304.3 70.1 %collective-permute-start.22 = (bf16[512,3072]{1,0:T(8,128)(2,1)}, bf16[512,3072]{1,0:T(8,128)(2,1)}, u32[]{:S(2)}, u32[]{:S(2)}) collective-permute-start(bf16[512,3072]{1,0:T(8,128)(2,1)} %get-tuple-element.176), channel_id=1, source_target_pairs={{0,16},{4,20},{8,24},{12,28},{16,0},{20,4},{24,8},{28,12},{1,17},{... | collective-permute-start | bytes 9437192 | tf_op jit(solution)/shard_map/ppermute | solution.py:100
  305.8 69.7 %collective-permute-start.23 = (bf16[512,3072]{1,0:T(8,128)(2,1)}, bf16[512,3072]{1,0:T(8,128)(2,1)}, u32[]{:S(2)}, u32[]{:S(2)}) collective-permute-start(bf16[512,3072]{1,0:T(8,128)(2,1)} %get-tuple-element.178), channel_id=1, source_target_pairs={{0,8},{4,12},{8,0},{12,4},{16,24},{20,28},{24,16},{28,20},{1,9},{5... | collective-permute-start | bytes 9437192 | tf_op jit(solution)/shard_map/ppermute | solution.py:100
  349.7 107.1 %reduce-scatter.8.cloned.1.call-start = ((), (), s32[]{:S(2)}) async-start(), calls=%async_computation.8 | async-start | bytes 2621440 | tf_op jit(solution)/shard_map/reduce_scatter | solution.py:635
  349.9 38.7 %collective-permute-start.20 = (bf16[512,2048]{1,0:T(8,128)(2,1)}, bf16[512,2048]{1,0:T(8,128)(2,1)}, u32[]{:S(2)}, u32[]{:S(2)}) collective-permute-start(bf16[512,2048]{1,0:T(8,128)(2,1)} %all-gather.8.cloned.1.call-done.grad_ref.refs_0_.refs_1_.refs_2_.refs_3_), channel_id=1, source_target_pairs={{0,4},{4,0},{8,12},{12,8},{16,20},{20,16},{24,28},{28,24},{1,5},{5... | collective-permute-start | bytes 6291464 | tf_op jit(solution)/shard_map/ppermute | solution.py:100
  378.7 56.9 %collective-permute-start.28 = (bf16[256,3072]{1,0:T(8,128)(2,1)}, bf16[256,3072]{1,0:T(8,128)(2,1)}, u32[]{:S(2)}, u32[]{:S(2)}) collective-permute-start(bf16[256,3072]{1,0:T(8,128)(2,1)} %add_convert_fusion.1), channel_id=1, source_target_pairs={{0,8},{4,12},{8,0},{12,4},{16,24},{20,28},{24,16},{28,20},{1,9},{5... | collective-permute-start | bytes 4718600 | tf_op jit(solution)/shard_map/ppermute | solution.py:100
  383.3 52.3 %collective-permute-start.29 = (bf16[256,3072]{1,0:T(8,128)(2,1)}, bf16[256,3072]{1,0:T(8,128)(2,1)}, u32[]{:S(2)}, u32[]{:S(2)}) collective-permute-start(bf16[256,3072]{1,0:T(8,128)(2,1)} %add_convert_fusion), channel_id=1, source_target_pairs={{0,16},{4,20},{8,24},{12,28},{16,0},{20,4},{24,8},{28,12},{1,17},{... | collective-permute-start | bytes 4718600 | tf_op jit(solution)/shard_map/ppermute | solution.py:100
  400.3 34.6 %collective-permute-start.24 = (bf16[512,768]{1,0:T(8,128)(2,1)}, bf16[512,768]{1,0:T(8,128)(2,1)S(1)}, u32[]{:S(2)}, u32[]{:S(2)}) collective-permute-start(bf16[512,768]{1,0:T(8,128)(2,1)} %get-tuple-element.200), channel_id=1, source_target_pairs={{0,16},{4,20},{8,24},{12,28},{16,0},{20,4},{24,8},{28,12},{1,17},{... | collective-permute-start | bytes 2359304 | tf_op jit(solution)/shard_map/ppermute | solution.py:100
  402.0 22.9 %collective-permute-start.25 = (bf16[512,512]{1,0:T(8,128)(2,1)}, bf16[512,512]{1,0:T(8,128)(2,1)S(1)}, u32[]{:S(2)}, u32[]{:S(2)}) collective-permute-start(bf16[512,512]{1,0:T(8,128)(2,1)} %get-tuple-element.202), channel_id=1, source_target_pairs={{0,8},{4,12},{8,0},{12,4},{16,24},{20,28},{24,16},{28,20},{1,9},{5... | collective-permute-start | bytes 1572872 | tf_op jit(solution)/shard_map/ppermute | solution.py:100
  (52 other events, 571.2 us)
Sparse Core Ops, SparseCore 0:
  10.5 43.8 all-gather.3
  56.4 125.3 all-gather.5
  243.8 55.7 reduce-scatter.3
  304.3 45.2 all-gather.7
  352.4 42.9 reduce-scatter.5
  402.8 42.4 reduce-scatter.7

commit v6 on v5

--- a/solution.py
+++ b/solution.py
@@ -171,6 +171,31 @@
 
 def whole(shape):
     return pl.BlockSpec(shape, lambda *_: (0,) * len(shape))
+
+
+def norm_backward(base, gain, x, grad, keep):
+    rows, features = x.shape
+    block = tile_of(rows, 64)
+
+    def body(base_ref, gain_ref, x_ref, grad_ref, low_ref, *wide_ref):
+        normed, factor = norm_parts(x_ref[...].astype(F32))
+        total = base_ref[...].astype(F32) + norm_back(grad_ref[...].astype(F32), gain_ref[...], normed, factor)
+        low_ref[...] = total.astype(BF16)
+        if keep:
+            wide_ref[0][...] = total
+
+    spec = pl.BlockSpec((block, features), lambda j: (j, 0))
+    kinds = (BF16, F32) if keep else (BF16,)
+    return kernel_call(
+        body,
+        "norm_backward",
+        20 * rows * features,
+        (base, gain, x, grad),
+        [jax.ShapeDtypeStruct((rows, features), kind) for kind in kinds],
+        grid=(rows // block,),
+        in_specs=[spec, whole((1, features)), spec, spec],
+        out_specs=[spec] * len(kinds),
+    )
 
 
 def feed_forward(h_blocks, c_blocks, w, owners):
@@ -585,7 +610,7 @@
     )
     attn_input_other = cube.swap(attn_input, 1)
     tokens_f = tokens.astype(F32)
-    normed_one, factor_one = norm_parts(tokens_f)
+
     out_parts = order(
         lambda a, w: rows_product(a, [0], w, 0, "attention_out", line.owners),
         after(attended, incoming_blocks[1])[None],
@@ -593,7 +618,7 @@
     )
     attended_other = cube.swap(attended, 1)
     residual = order(lambda x, *terms: x + total32(terms), tokens_f, *line.scatter(out_parts))
-    normed_two, factor_two = norm_parts(residual)
+    normed_two, _ = norm_parts(residual)
     mlp_blocks = line.gather((normed_two * gain_two).astype(BF16))
 
     mlp_input, incoming, unit_grads = order(
@@ -611,15 +636,10 @@
         return weight_grad([[h, h_other], [c, c_other]], parts, cube, 512, "feed_forward_grad")
 
     mlp_pairs = cube.first_hop(order(mlp_grad, mlp_input, incoming, unit_grads, *mlp_others))
-    grad_residual = order(
-        lambda c, g, n, f, t: c.astype(F32) + norm_back(t.astype(F32), g, n, f),
-        cotangent,
-        gain_two,
-        normed_two,
-        factor_two,
-        two_sum,
-    )
-    grad_attn_rows = lax.all_gather(grad_residual.astype(BF16), "tensor", axis=0, tiled=True)
+    grad_low, grad_residual = order(
+        lambda *a: norm_backward(*a, True), cotangent, gain_two, residual, two_sum
+    )
+    grad_attn_rows = lax.all_gather(grad_low, "tensor", axis=0, tiled=True)
     block_parts = order(lambda a, w: rows_product(a, [2], w, 2 * units, "block_out"), unit_grads, w_mlp)
     block_parts, grad_attn_rows = lax.optimization_barrier((block_parts, grad_attn_rows))
     block_sum = lax.psum_scatter(block_parts, "tensor", scatter_dimension=0, tiled=True)
@@ -664,14 +684,7 @@
         return gain_terms((gate, gate_grad), (up, up_grad)), gate_grad, up_grad, down_grad
 
     mlp_gain_terms, gate_grad, up_grad, down_grad = order(mlp_finals, mlp_terms, w_gate, w_up)
-    grad_tokens = order(
-        lambda c, g, n, f, t: (c + norm_back(t.astype(F32), g, n, f)).astype(BF16),
-        grad_residual,
-        gain_one,
-        normed_one,
-        factor_one,
-        one_sum,
-    )
+    (grad_tokens,) = order(lambda *a: norm_backward(*a, False), grad_residual, gain_one, tokens, one_sum)
     attn_sum = block_sum32(attn_terms)
     out_grad, qkv_grad = attn_sum[:, :width_out].T, attn_sum[:, width_out:]
     query_grad = qkv_grad[:, :width_q]

time: 476 us -> 476 us (level)
  starting transfers between devices: 61.1 us -> 80.4 us
  waiting for transfers between devices: 215 us -> 196 us
  other arithmetic: 37.7 us -> 30.8 us
    ppermute x15, starting transfers between devices: 47.8 us -> 67.3 us  [shift(): lax.ppermute(v, 'tensor', [(i, (i + r) % self.size) for i in range(self.s...]
    reduce_scatter x1, waiting for transfers between devices: 23 us -> 10.3 us  [per_device(): lax.psum_scatter(two_parts, 'tensor', scatter_dimension=0, tiled=True)]
    all_gather x1, waiting for transfers between devices: 11.6 us -> 4.86 us  [per_device(): lax.all_gather(jnp.concatenate([w_gate, w_up, w_down.T], axis=1), 'dp', a...]
    convert_element_type x2 -> x0, other arithmetic: 5.1 us -> none  [the longest x1 2.98 us: per_device(): grad_residual.astype(BF16)]
    pallas_call x9 -> x11, Pallas kernels: 117 us -> 120 us  [kernel_call(): pl.pallas_call(body, out_shape=out_shape, name=name, cost_estimate=pl.Cos...]
    unnamed x78 -> x84, local copies, waits for them, and re-layouts: 20.2 us -> 22.7 us
  transfers between devices with their start and end apart: 39 -> 39, of which waited for: 18 -> 19; matrix products, arithmetic and copies ran while one was open for 8% -> 8% of each run, Pallas kernels for 20% -> 20%
where the time goes in v6:
time: 476 us; the launch traced here: 466 us
  waiting for transfers between devices  196 us (41%)
  Pallas kernels  120 us (25%)
  starting transfers between devices  80.4 us (17%)
  other arithmetic  30.8 us (6%)
  local copies, waits for them, and re-layouts  24.6 us (5%)
  between operations  15.1 us (3%)
    pallas_call x11, Pallas kernels, kernel_call(): pl.pallas_call(body, out_shape=out_shape, name=name, cost_estimate=pl.Cos...  120 us
    ppermute x15, waiting for transfers between devices, shift(): lax.ppermute(v, 'tensor', [(i, (i + r) % self.size) for i in range(self.s...  102 us
    ppermute x15, starting transfers between devices, shift(): lax.ppermute(v, 'tensor', [(i, (i + r) % self.size) for i in range(self.s...  67.3 us
    ppermute x18, waiting for transfers between devices, swap(): return lax.ppermute(v, 'dp', [(i, i ^ m) for i in range(self.size)])  44.7 us
    all_gather x1, waiting for transfers between devices, per_device(): grad_attn_rows = lax.all_gather(grad_low, 'tensor', axis=0, tiled=True)  33.6 us
    unnamed x84, local copies, waits for them, and re-layouts  22.7 us
    ppermute x18, starting transfers between devices, swap(): return lax.ppermute(v, 'dp', [(i, i ^ m) for i in range(self.size)])  12.7 us
    reduce_scatter x1, waiting for transfers between devices, per_device(): lax.psum_scatter(two_parts, 'tensor', scatter_dimension=0, tiled=True)  10.3 us
  transfers between devices with their start and end apart: 39, of which 19 were waited for; matrix products, arithmetic and copies ran while one was open for 8% of the time, Pallas kernels for 20%

profile of v6, /device:TPU:0, one launch (start us, length us, event | category | flops | bytes accessed | tf_op | source)
XLA Modules:
  0.0 466.5 jit_solution(8350808083371332549)
XLA Ops:
  14.8 5.0 %collective-permute-start.2 = (bf16[128,2048]{1,0:T(8,128)(2,1)S(1)}, bf16[128,2048]{1,0:T(8,128)(2,1)S(1)}, u32[]{:S(2)}, u32[]{:S(2)}) collective-permute-start(bf16[128,2048]{1,0:T(8,128)(2,1)S(1)} %copy-done.7), channel_id=1, source_target_pairs={{0,3},{1,0},{2,1},{3,2},{4,7},{5,4},{6,5},{7,6},{8,11},{9,8},{10,9... | collective-permute-start | bytes 1572872 | tf_op jit(solution)/shard_map/ppermute | solution.py:81
  32.2 32.4 %collective-permute-done.1.refs_2_ = bf16[128,2048]{1,0:T(8,128)(2,1)S(1)} collective-permute-done((bf16[128,2048]{1,0:T(8,128)(2,1)S(1)}, bf16[128,2048]{1,0:T(8,128)(2,1)S(1)}, u32[]{:S(2)}, u32[]{:S(2)}) %collective-permute-start.1) | collective-permute-done | bytes 524320 | tf_op jit(solution)/shard_map/ppermute | solution.py:81
  67.5 15.9 %attention_forward.1 = (bf16[512,2048]{1,0:T(8,128)(2,1)}, bf16[512,768]{1,0:T(8,128)(2,1)S(1)}, bf16[512,512]{1,0:T(8,128)(2,1)S(1)}, f32[512,128]{1,0:T(8,128)S(1)}) custom-call(s32[24]{0:T(128)S(1)} %compare_select_fusion.2.ends_ref, s32[4]{0:T(128)S(1)} %compare_select_fusion.owners_ref, bf16[128,2048]{1,0:T(8,128)(2,1)S(1)} %copy-done.7, ...), custom_call_target="tpu_custom_call" | custom-call | flops 2147483648 | bytes 11542640 | tf_op jit(solution)/shard_map/attention_forward/pallas_call | solution.py:162
  91.7 3.9 collective-permute-start.14
  95.6 7.3 %collective-permute-done.7 = bf16[128,2048]{1,0:T(8,128)(2,1)S(1)} collective-permute-done((bf16[128,2048]{1,0:T(8,128)(2,1)S(1)}, bf16[128,2048]{1,0:T(8,128)(2,1)S(1)}, u32[]{:S(2)}, u32[]{:S(2)}) %collective-permute-start.7) | collective-permute-done | bytes 524320 | tf_op jit(solution)/shard_map/ppermute | solution.py:81
  102.9 23.3 %collective-permute-start.13 = (bf16[128,2048]{1,0:T(8,128)(2,1)S(1)}, bf16[128,2048]{1,0:T(8,128)(2,1)}, u32[]{:S(2)}, u32[]{:S(2)}) collective-permute-start(bf16[128,2048]{1,0:T(8,128)(2,1)S(1)} %copy-done.5), channel_id=1, source_target_pairs={{0,2},{1,3},{2,0},{3,1},{4,6},{5,7},{6,4},{7,5},{8,10},{9,11},{10,... | collective-permute-start | bytes 1572872 | tf_op jit(solution)/shard_map/ppermute | solution.py:81
  126.2 23.1 %collective-permute-done.8 = bf16[128,2048]{1,0:T(8,128)(2,1)S(1)} collective-permute-done((bf16[128,2048]{1,0:T(8,128)(2,1)S(1)}, bf16[128,2048]{1,0:T(8,128)(2,1)S(1)}, u32[]{:S(2)}, u32[]{:S(2)}) %collective-permute-start.8) | collective-permute-done | bytes 524320 | tf_op jit(solution)/shard_map/ppermute | solution.py:81
  151.9 22.8 %collective-permute-start.11 = (bf16[128,2048]{1,0:T(8,128)(2,1)S(1)}, bf16[128,2048]{1,0:T(8,128)(2,1)}, u32[]{:S(2)}, u32[]{:S(2)}) collective-permute-start(bf16[128,2048]{1,0:T(8,128)(2,1)S(1)} %multiply_convert_fusion.refs_0_), channel_id=1, source_target_pairs={{0,2},{1,3},{2,0},{3,1},{4,6},{5,7},{6,4},{7,5},{8,10},{9,11},{10,... | collective-permute-start | bytes 1572872 | tf_op jit(solution)/shard_map/ppermute | solution.py:81
  176.9 4.9 %all-gather.6.cloned.1.call-done.refs_8_.refs_9_.refs_10_.refs_2_.refs_1_ = bf16[2048,6144]{1,0:T(8,128)(2,1)} async-done(((bf16[256,6144]{1,0:T(8,128)(2,1)}), bf16[2048,6144]{1,0:T(8,128)(2,1)}) %all-gather.6.cloned.1.call-update) | async-done | bytes 25165840 | tf_op jit(solution)/shard_map/all_gather | solution.py:595
  182.9 35.7 %collective-permute-done.11.refs_2_ = bf16[128,2048]{1,0:T(8,128)(2,1)} collective-permute-done((bf16[128,2048]{1,0:T(8,128)(2,1)S(1)}, bf16[128,2048]{1,0:T(8,128)(2,1)}, u32[]{:S(2)}, u32[]{:S(2)}) %collective-permute-start.11) | collective-permute-done | bytes 524320 | tf_op jit(solution)/shard_map/ppermute | solution.py:81
  218.6 21.6 %feed_forward.1 = (bf16[512,2048]{1,0:T(8,128)(2,1)}, bf16[512,2048]{1,0:T(8,128)(2,1)}, bf16[3,512,2048]{2,1,0:T(8,128)(2,1)}) custom-call(s32[4]{0:T(128)S(1)} %compare_select_fusion.owners_ref, bf16[128,2048]{1,0:T(8,128)(2,1)S(1)} %multiply_convert_fusion.refs_0_, bf16[128,2048]{1,0:T(8,128)(2,1)} %collective-permute-done.10.refs_1_, ...), custom_call_target="tpu_custom_call" | custom-call | flops 12884901888 | bytes 90177552 | tf_op jit(solution)/shard_map/feed_forward/pallas_call | solution.py:162
  240.3 13.2 %feed_forward_rows_grad.1 = bf16[512,2048]{1,0:T(8,128)(2,1)S(1)} custom-call(s32[1]{0:T(128)} %constant.43.clone.1.owners_ref, bf16[3,512,2048]{2,1,0:T(8,128)(2,1)} %get-tuple-element.164.refs_0_.refs_1_.refs_16_.refs_18_.refs_20_, bf16[3,512,2048]{2,1,0:T(8,128)(2,1)} %get-tuple-element.164.refs_0_.refs_1_.refs_16_.refs_18_.refs_20_, ...), custom_call_target="tpu_custom_call" | custom-call | flops 8589934592 | bytes 39845892 | tf_op jit(solution)/shard_map/feed_forward_rows_grad/pallas_call | solution.py:162
  255.6 6.0 %collective-permute-done.18.refs_12_.refs_13_.refs_14_.refs_15_ = bf16[512,2048]{1,0:T(8,128)(2,1)S(1)} collective-permute-done((bf16[512,2048]{1,0:T(8,128)(2,1)}, bf16[512,2048]{1,0:T(8,128)(2,1)S(1)}, u32[]{:S(2)}, u32[]{:S(2)}) %collective-permute-start.18) | collective-permute-done | bytes 2097184 | tf_op jit(solution)/shard_map/ppermute | solution.py:100
  262.9 24.0 %feed_forward_grad.1 = (bf16[512,3072]{1,0:T(8,128)(2,1)}, bf16[512,3072]{1,0:T(8,128)(2,1)}, bf16[512,3072]{1,0:T(8,128)(2,1)}, bf16[512,3072]{1,0:T(8,128)(2,1)}) custom-call(s32[4]{0:T(128)S(1)} %multiply_xor_fusion.places_ref, bf16[512,2048]{1,0:T(8,128)(2,1)S(1)} %copy-done.1, bf16[512,2048]{1,0:T(8,128)(2,1)S(1)} %copy-done.1, ...), custom_call_target="tpu_custom_call" | custom-call | flops 12884901888 | bytes 83886096 | tf_op jit(solution)/shard_map/feed_forward_grad/pallas_call | solution.py:162
  286.9 10.3 %reduce-scatter.4.cloned.1.call-done.grad_ref = bf16[128,2048]{1,0:T(8,128)(2,1)} async-done(((bf16[512,2048]{1,0:T(8,128)(2,1)}), bf16[128,2048]{1,0:T(8,128)(2,1)}) %reduce-scatter.4.cloned.1.call-update) | async-done | bytes 524304 | tf_op jit(solution)/shard_map/reduce_scatter | solution.py:632
  303.8 8.8 %block_out.1 = bf16[512,2048]{1,0:T(8,128)(2,1)} custom-call(s32[1]{0:T(128)} %constant.43.clone.1.owners_ref, bf16[3,512,2048]{2,1,0:T(8,128)(2,1)} %get-tuple-element.164.refs_0_.refs_1_.refs_16_.refs_18_.refs_20_, bf16[2048,6144]{1,0:T(8,128)(2,1)} %all-gather.6.cloned.1.call-done.refs_8_.refs_9_.refs_10_.refs_2_.refs_1_), custom_call_target="tpu_custom_call" | custom-call | flops 4294967296 | bytes 33554436 | tf_op jit(solution)/shard_map/block_out/pallas_call | solution.py:162
  312.6 33.6 %all-gather.8.cloned.1.call-done.grad_ref.refs_0_.refs_1_.refs_2_.refs_3_ = bf16[512,2048]{1,0:T(8,128)(2,1)} async-done(((bf16[128,2048]{1,0:T(8,128)(2,1)}), bf16[512,2048]{1,0:T(8,128)(2,1)}) %all-gather.8.cloned.1.call-update) | async-done | bytes 2097168 | tf_op jit(solution)/shard_map/all_gather | solution.py:642
  350.2 15.5 %attention_backward.1 = bf16[512,768]{1,0:T(8,128)(2,1)S(1)} custom-call(s32[24]{0:T(128)S(1)} %compare_select_fusion.2.ends_ref, bf16[512,2048]{1,0:T(8,128)(2,1)S(1)} %copy-done, bf16[2048,1280]{1,0:T(8,128)(2,1)} %all-gather.4.cloned.1.call-done.refs_5_.refs_1_.w_ref, bf16[512,768]{1,0:T(8,128)(2,1)S(1)} %copy-done.12, f32[512,128]{1,0:T(8,128)S(1)} %copy-done.22, ...), custom_call_target="tpu_custom_call" | custom-call | flops 2415919104 | bytes 9699424 | tf_op jit(solution)/shard_map/attention_backward/pallas_call | solution.py:162
  366.2 4.6 collective-permute-done.22
  380.3 4.8 %attention_rows_grad.1 = bf16[512,2048]{1,0:T(8,128)(2,1)} custom-call(s32[1]{0:T(128)} %constant.43.clone.1.owners_ref, bf16[1,512,768]{2,1,0:T(8,128)(2,1)S(1)} %bitcast.18, bf16[2048,1280]{1,0:T(8,128)(2,1)} %all-gather.4.cloned.1.call-done.refs_5_.refs_1_.w_ref), custom_call_target="tpu_custom_call" | custom-call | flops 1610612736 | bytes 8126468 | tf_op jit(solution)/shard_map/attention_rows_grad/pallas_call | solution.py:162
  386.1 9.8 %attention_grad.1 = (bf16[512,768]{1,0:T(8,128)(2,1)S(1)}, bf16[512,768]{1,0:T(8,128)(2,1)}, bf16[512,512]{1,0:T(8,128)(2,1)S(1)}, bf16[512,512]{1,0:T(8,128)(2,1)}) custom-call(s32[4]{0:T(128)S(1)} %multiply_xor_fusion.places_ref, bf16[512,2048]{1,0:T(8,128)(2,1)} %all-gather.8.cloned.1.call-done.grad_ref.refs_0_.refs_1_.refs_2_.refs_3_, ...), custom_call_target="tpu_custom_call" | custom-call | flops 2684354560 | bytes 38797328 | tf_op jit(solution)/shard_map/attention_grad/pallas_call | solution.py:162
  401.8 19.7 %collective-permute-done.25 = bf16[512,512]{1,0:T(8,128)(2,1)} collective-permute-done((bf16[512,512]{1,0:T(8,128)(2,1)}, bf16[512,512]{1,0:T(8,128)(2,1)}, u32[]{:S(2)}, u32[]{:S(2)}) %collective-permute-start.25) | collective-permute-done | bytes 524320 | tf_op jit(solution)/shard_map/ppermute | solution.py:100
  421.5 10.0 %collective-permute-done.24 = bf16[512,768]{1,0:T(8,128)(2,1)} collective-permute-done((bf16[512,768]{1,0:T(8,128)(2,1)}, bf16[512,768]{1,0:T(8,128)(2,1)}, u32[]{:S(2)}, u32[]{:S(2)}) %collective-permute-start.24) | collective-permute-done | bytes 786464 | tf_op jit(solution)/shard_map/ppermute | solution.py:100
  434.9 5.0 %convert_add_fusion = (f32[256,3072]{1,0:T(8,128)S(1)}, f32[256,3072]{1,0:T(8,128)S(1)}) fusion(bf16[256,3072]{1,0:T(8,128)(2,1)} %collective-permute-done.29, bf16[512,3072]{1,0:T(8,128)(2,1)} %collective-permute-done.23, bf16[512,3072]{1,0:T(8,128)(2,1)} %get-tuple-element.214, bf16[256,3072]{1,0:T(8,128)(2,1)} %collective-permute-done.28, ...), kind=kLoop, calls=%fused_computation.1 | loop fusion | flops 7864320 | bytes 15728640 | tf_op jit(solution)/shard_map/add | solution.py:150
  (198 shorter events, 90.3 us)
Async XLA Ops:
  7.2 59.1 %all-gather.4.cloned.1.call-start = ((), (), s32[]{:S(2)}) async-start(), calls=%async_computation.3 | async-start | bytes 5898240 | tf_op jit(solution)/shard_map/all_gather | solution.py:594
  10.4 171.3 %all-gather.6.cloned.1.call-start = ((), (), s32[]{:S(2)}) async-start(), calls=%async_computation.4 | async-start | bytes 28311552 | tf_op jit(solution)/shard_map/all_gather | solution.py:595
  13.8 283.4 %reduce-scatter.4.cloned.1.call-start = ((), (), s32[]{:S(2)}) async-start(), calls=%async_computation.5 | async-start | bytes 2621440 | tf_op jit(solution)/shard_map/reduce_scatter | solution.py:632
  19.9 44.8 %collective-permute-start.1 = (bf16[128,2048]{1,0:T(8,128)(2,1)S(1)}, bf16[128,2048]{1,0:T(8,128)(2,1)S(1)}, u32[]{:S(2)}, u32[]{:S(2)}) collective-permute-start(bf16[128,2048]{1,0:T(8,128)(2,1)S(1)} %copy-done.7), channel_id=1, source_target_pairs={{0,2},{1,3},{2,0},{3,1},{4,6},{5,7},{6,4},{7,5},{8,10},{9,11},{10,... | collective-permute-start | bytes 1572872 | tf_op jit(solution)/shard_map/ppermute | solution.py:81
  19.9 44.8 %collective-permute-start = (bf16[128,2048]{1,0:T(8,128)(2,1)S(1)}, bf16[128,2048]{1,0:T(8,128)(2,1)S(1)}, u32[]{:S(2)}, u32[]{:S(2)}) collective-permute-start(bf16[128,2048]{1,0:T(8,128)(2,1)S(1)} %copy-done.7), channel_id=1, source_target_pairs={{0,1},{1,2},{2,3},{3,0},{4,5},{5,6},{6,7},{7,4},{8,9},{9,10},{10,1... | collective-permute-start | bytes 1572872 | tf_op jit(solution)/shard_map/ppermute | solution.py:81
  84.2 90.5 %collective-permute-start.15 = (bf16[512,2048]{1,0:T(8,128)(2,1)}, bf16[512,2048]{1,0:T(8,128)(2,1)}, u32[]{:S(2)}, u32[]{:S(2)}) collective-permute-start(bf16[512,2048]{1,0:T(8,128)(2,1)} %get-tuple-element.185.refs_8_.refs_9_.refs_10_.refs_11_), channel_id=1, source_target_pairs={{0,4},{4,0},{8,12},{12,8},{16,20},{20,16},{24,28},{28,24},{1,5},{5... | collective-permute-start | bytes 6291464 | tf_op jit(solution)/shard_map/ppermute | solution.py:100
  90.5 58.7 %collective-permute-start.8 = (bf16[128,2048]{1,0:T(8,128)(2,1)S(1)}, bf16[128,2048]{1,0:T(8,128)(2,1)S(1)}, u32[]{:S(2)}, u32[]{:S(2)}) collective-permute-start(bf16[128,2048]{1,0:T(8,128)(2,1)S(1)} %get-tuple-element.130), channel_id=1, source_target_pairs={{0,2},{1,3},{2,0},{3,1},{4,6},{5,7},{6,4},{7,5},{8,10},{9,11},{10,... | collective-permute-start | bytes 1572872 | tf_op jit(solution)/shard_map/ppermute | solution.py:81
  91.6 57.6 %collective-permute-start.9 = (bf16[128,2048]{1,0:T(8,128)(2,1)S(1)}, bf16[128,2048]{1,0:T(8,128)(2,1)S(1)}, u32[]{:S(2)}, u32[]{:S(2)}) collective-permute-start(bf16[128,2048]{1,0:T(8,128)(2,1)S(1)} %get-tuple-element.131), channel_id=1, source_target_pairs={{0,1},{1,2},{2,3},{3,0},{4,5},{5,6},{6,7},{7,4},{8,9},{9,10},{10,1... | collective-permute-start | bytes 1572872 | tf_op jit(solution)/shard_map/ppermute | solution.py:81
  91.7 90.0 %collective-permute-start.14 = (bf16[128,2048]{1,0:T(8,128)(2,1)S(1)}, bf16[128,2048]{1,0:T(8,128)(2,1)S(1)}, u32[]{:S(2)}, u32[]{:S(2)}) collective-permute-start(bf16[128,2048]{1,0:T(8,128)(2,1)S(1)} %copy-done.5), channel_id=1, source_target_pairs={{0,3},{1,0},{2,1},{3,2},{4,7},{5,4},{6,5},{7,6},{8,11},{9,8},{10,9... | collective-permute-start | bytes 1572872 | tf_op jit(solution)/shard_map/ppermute | solution.py:81
  102.9 78.8 %collective-permute-start.13 = (bf16[128,2048]{1,0:T(8,128)(2,1)S(1)}, bf16[128,2048]{1,0:T(8,128)(2,1)}, u32[]{:S(2)}, u32[]{:S(2)}) collective-permute-start(bf16[128,2048]{1,0:T(8,128)(2,1)S(1)} %copy-done.5), channel_id=1, source_target_pairs={{0,2},{1,3},{2,0},{3,1},{4,6},{5,7},{6,4},{7,5},{8,10},{9,11},{10,... | collective-permute-start | bytes 1572872 | tf_op jit(solution)/shard_map/ppermute | solution.py:81
  149.9 33.0 %collective-permute-start.12 = (bf16[128,2048]{1,0:T(8,128)(2,1)S(1)}, bf16[128,2048]{1,0:T(8,128)(2,1)}, u32[]{:S(2)}, u32[]{:S(2)}) collective-permute-start(bf16[128,2048]{1,0:T(8,128)(2,1)S(1)} %multiply_convert_fusion.refs_0_), channel_id=1, source_target_pairs={{0,3},{1,0},{2,1},{3,2},{4,7},{5,4},{6,5},{7,6},{8,11},{9,8},{10,9... | collective-permute-start | bytes 1572872 | tf_op jit(solution)/shard_map/ppermute | solution.py:81
  151.9 66.7 %collective-permute-start.11 = (bf16[128,2048]{1,0:T(8,128)(2,1)S(1)}, bf16[128,2048]{1,0:T(8,128)(2,1)}, u32[]{:S(2)}, u32[]{:S(2)}) collective-permute-start(bf16[128,2048]{1,0:T(8,128)(2,1)S(1)} %multiply_convert_fusion.refs_0_), channel_id=1, source_target_pairs={{0,2},{1,3},{2,0},{3,1},{4,6},{5,7},{6,4},{7,5},{8,10},{9,11},{10,... | collective-permute-start | bytes 1572872 | tf_op jit(solution)/shard_map/ppermute | solution.py:81
  174.7 43.9 %collective-permute-start.10 = (bf16[128,2048]{1,0:T(8,128)(2,1)S(1)}, bf16[128,2048]{1,0:T(8,128)(2,1)}, u32[]{:S(2)}, u32[]{:S(2)}) collective-permute-start(bf16[128,2048]{1,0:T(8,128)(2,1)S(1)} %multiply_convert_fusion.refs_0_), channel_id=1, source_target_pairs={{0,1},{1,2},{2,3},{3,0},{4,5},{5,6},{6,7},{7,4},{8,9},{9,10},{10,1... | collective-permute-start | bytes 1572872 | tf_op jit(solution)/shard_map/ppermute | solution.py:81
  240.3 22.0 %collective-permute-start.19 = (bf16[3,512,2048]{2,1,0:T(8,128)(2,1)}, bf16[3,512,2048]{2,1,0:T(8,128)(2,1)}, u32[]{:S(2)}, u32[]{:S(2)}) collective-permute-start(bf16[3,512,2048]{2,1,0:T(8,128)(2,1)} %get-tuple-element.164.refs_0_.refs_1_.refs_16_.refs_18_.refs_20_), channel_id=1, source_target_pairs={{0,4},{4,0},{8,12},{12,8},{16,20},{20,16},{24,28},{28,24},{1,5},{5... | collective-permute-start | bytes 18874376 | tf_op jit(solution)/shard_map/ppermute | solution.py:100
  254.9 91.3 %all-gather.8.cloned.1.call-start = ((), (), s32[]{:S(2)}) async-start(), calls=%async_computation.6 | async-start | bytes 2621440 | tf_op jit(solution)/shard_map/all_gather | solution.py:642
  300.7 99.0 %reduce-scatter.6.cloned.1.call-start = ((), (), s32[]{:S(2)}) async-start(), calls=%async_computation.7 | async-start | bytes 2621440 | tf_op jit(solution)/shard_map/reduce_scatter | solution.py:645
  300.7 70.1 %collective-permute-start.22 = (bf16[512,3072]{1,0:T(8,128)(2,1)}, bf16[512,3072]{1,0:T(8,128)(2,1)}, u32[]{:S(2)}, u32[]{:S(2)}) collective-permute-start(bf16[512,3072]{1,0:T(8,128)(2,1)} %get-tuple-element.176), channel_id=1, source_target_pairs={{0,16},{4,20},{8,24},{12,28},{16,0},{20,4},{24,8},{28,12},{1,17},{... | collective-permute-start | bytes 9437192 | tf_op jit(solution)/shard_map/ppermute | solution.py:100
  302.3 69.7 %collective-permute-start.23 = (bf16[512,3072]{1,0:T(8,128)(2,1)}, bf16[512,3072]{1,0:T(8,128)(2,1)}, u32[]{:S(2)}, u32[]{:S(2)}) collective-permute-start(bf16[512,3072]{1,0:T(8,128)(2,1)} %get-tuple-element.178), channel_id=1, source_target_pairs={{0,8},{4,12},{8,0},{12,4},{16,24},{20,28},{24,16},{28,20},{1,9},{5... | collective-permute-start | bytes 9437192 | tf_op jit(solution)/shard_map/ppermute | solution.py:100
  346.2 110.6 %reduce-scatter.8.cloned.1.call-start = ((), (), s32[]{:S(2)}) async-start(), calls=%async_computation.8 | async-start | bytes 2621440 | tf_op jit(solution)/shard_map/reduce_scatter | solution.py:655
  346.5 38.6 %collective-permute-start.20 = (bf16[512,2048]{1,0:T(8,128)(2,1)}, bf16[512,2048]{1,0:T(8,128)(2,1)}, u32[]{:S(2)}, u32[]{:S(2)}) collective-permute-start(bf16[512,2048]{1,0:T(8,128)(2,1)} %all-gather.8.cloned.1.call-done.grad_ref.refs_0_.refs_1_.refs_2_.refs_3_), channel_id=1, source_target_pairs={{0,4},{4,0},{8,12},{12,8},{16,20},{20,16},{24,28},{28,24},{1,5},{5... | collective-permute-start | bytes 6291464 | tf_op jit(solution)/shard_map/ppermute | solution.py:100
  375.2 59.7 %collective-permute-start.28 = (bf16[256,3072]{1,0:T(8,128)(2,1)}, bf16[256,3072]{1,0:T(8,128)(2,1)}, u32[]{:S(2)}, u32[]{:S(2)}) collective-permute-start(bf16[256,3072]{1,0:T(8,128)(2,1)} %add_convert_fusion.1), channel_id=1, source_target_pairs={{0,8},{4,12},{8,0},{12,4},{16,24},{20,28},{24,16},{28,20},{1,9},{5... | collective-permute-start | bytes 4718600 | tf_op jit(solution)/shard_map/ppermute | solution.py:100
  379.8 55.0 %collective-permute-start.29 = (bf16[256,3072]{1,0:T(8,128)(2,1)}, bf16[256,3072]{1,0:T(8,128)(2,1)}, u32[]{:S(2)}, u32[]{:S(2)}) collective-permute-start(bf16[256,3072]{1,0:T(8,128)(2,1)} %add_convert_fusion), channel_id=1, source_target_pairs={{0,16},{4,20},{8,24},{12,28},{16,0},{20,4},{24,8},{28,12},{1,17},{... | collective-permute-start | bytes 4718600 | tf_op jit(solution)/shard_map/ppermute | solution.py:100
  397.6 33.8 %collective-permute-start.24 = (bf16[512,768]{1,0:T(8,128)(2,1)}, bf16[512,768]{1,0:T(8,128)(2,1)}, u32[]{:S(2)}, u32[]{:S(2)}) collective-permute-start(bf16[512,768]{1,0:T(8,128)(2,1)} %get-tuple-element.200), channel_id=1, source_target_pairs={{0,16},{4,20},{8,24},{12,28},{16,0},{20,4},{24,8},{28,12},{1,17},{... | collective-permute-start | bytes 2359304 | tf_op jit(solution)/shard_map/ppermute | solution.py:100
  399.2 22.3 %collective-permute-start.25 = (bf16[512,512]{1,0:T(8,128)(2,1)}, bf16[512,512]{1,0:T(8,128)(2,1)}, u32[]{:S(2)}, u32[]{:S(2)}) collective-permute-start(bf16[512,512]{1,0:T(8,128)(2,1)} %get-tuple-element.202), channel_id=1, source_target_pairs={{0,8},{4,12},{8,0},{12,4},{16,24},{20,28},{24,16},{28,20},{1,9},{5... | collective-permute-start | bytes 1572872 | tf_op jit(solution)/shard_map/ppermute | solution.py:100
  (55 other events, 605.3 us)
Sparse Core Ops, SparseCore 0:
  10.5 43.8 all-gather.3
  56.4 125.3 all-gather.5
  255.0 42.1 reduce-scatter.3
  300.8 45.3 all-gather.7
  349.0 42.4 reduce-scatter.5
  399.9 42.5 reduce-scatter.7

commit v7 on v6

--- a/solution.py
+++ b/solution.py
@@ -372,6 +372,58 @@
         ),
     )
     return (keep_a, send_a), (keep_b, send_b)
+
+
+def feed_forward_finals(halves, w_gate, w_up):
+    rows, units = w_gate.shape
+    widths = [terms[0].shape[1] for terms in halves]
+    tile = functools.reduce(math.gcd, widths, units)
+    steps, first = units // tile, widths[0] // tile
+    flat = [t for terms in halves for t in terms]
+    count = len(halves[0])
+
+    def body(*refs):
+        terms, (gate_w, up_w, gate_ref, up_ref, down_ref, gain_ref) = refs[: len(flat)], refs[len(flat) :]
+        j = pl.program_id(0)
+
+        @pl.when(j == 0)
+        def _():
+            gain_ref[...] = jnp.zeros_like(gain_ref)
+
+        for k in range(3 * steps):
+
+            @pl.when(j == k)
+            def _(k=k):
+                total = total32([t[...] for t in (terms[:count] if k < first else terms[count:])])
+                if k >= 2 * steps:
+                    down_ref[...] = total.T
+                else:
+                    w_ref, out_ref = (gate_w, gate_ref) if k < steps else (up_w, up_ref)
+                    out_ref[...] = total
+                    gain_ref[...] += jnp.sum(total * w_ref[...].astype(F32), axis=1, keepdims=True)
+
+    def columns(lo, n):
+        return pl.BlockSpec((rows, tile), lambda j: (0, jnp.clip(j - lo, 0, n - 1)))
+
+    wide = jax.ShapeDtypeStruct((rows, units), F32)
+    gate_grad, up_grad, down_grad, gain = kernel_call(
+        body,
+        "feed_forward_finals",
+        4 * rows * units * 3,
+        (*flat, w_gate, w_up),
+        (wide, wide, jax.ShapeDtypeStruct((units, rows), F32), jax.ShapeDtypeStruct((rows, 128), F32)),
+        grid=(3 * steps,),
+        in_specs=[columns(0, first)] * count
+        + [columns(first, widths[1] // tile)] * count
+        + [columns(0, steps), columns(steps, steps)],
+        out_specs=[
+            columns(0, steps),
+            columns(steps, steps),
+            pl.BlockSpec((tile, rows), lambda j: (jnp.clip(j - 2 * steps, 0, steps - 1), 0)),
+            whole((rows, 128)),
+        ],
+    )
+    return gain[:, 0], gate_grad, up_grad, down_grad
 
 
 def head_columns(heads, kv):
@@ -678,12 +730,7 @@
     def gain_terms(*pairs):
         return functools.reduce(lambda a, b: a + b, [jnp.sum(w.astype(F32) * g, axis=1) for w, g in pairs])
 
-    def mlp_finals(terms, gate, up):
-        sums = block_sum32(terms)
-        gate_grad, up_grad, down_grad = sums[:, :units], sums[:, units : 2 * units], sums[:, 2 * units :].T
-        return gain_terms((gate, gate_grad), (up, up_grad)), gate_grad, up_grad, down_grad
-
-    mlp_gain_terms, gate_grad, up_grad, down_grad = order(mlp_finals, mlp_terms, w_gate, w_up)
+    mlp_gain_terms, gate_grad, up_grad, down_grad = order(feed_forward_finals, mlp_terms, w_gate, w_up)
     (grad_tokens,) = order(lambda *a: norm_backward(*a, False), grad_residual, gain_one, tokens, one_sum)
     attn_sum = block_sum32(attn_terms)
     out_grad, qkv_grad = attn_sum[:, :width_out].T, attn_sum[:, width_out:]

time: 476 us -> 521 us (1.095)
  waiting for transfers between devices: 196 us -> 251 us
  other arithmetic: 30.8 us -> 15.1 us
  Pallas kernels: 120 us -> 127 us
    ppermute x18, waiting for transfers between devices: 44.7 us -> 94.3 us  [swap(): return lax.ppermute(v, 'dp', [(i, i ^ m) for i in range(self.size)])]
    pallas_call x11 -> x12, Pallas kernels: 120 us -> 127 us  [kernel_call(): pl.pallas_call(body, out_shape=out_shape, name=name, cost_estimate=pl.Cos...]
    add x3 -> x2, other arithmetic: 7.29 us -> 0.22 us  [total32(): return functools.reduce(lambda a, b: a + b, [t.astype(F32) for t in terms])]
    unnamed x84 -> x83, local copies, waits for them, and re-layouts: 22.7 us -> 19.6 us
  transfers between devices with their start and end apart: 39 -> 39, of which waited for: 19 -> 22; matrix products, arithmetic and copies ran while one was open for 8% -> 3% of each run, Pallas kernels for 20% -> 20%
where the time goes in v7:
time: 521 us; the launch traced here: 512 us
  waiting for transfers between devices  251 us (48%)
  Pallas kernels  127 us (24%)
  starting transfers between devices  81.8 us (16%)
  local copies, waits for them, and re-layouts  21.6 us (4%)
  other arithmetic  15.1 us (3%)
  between operations  15.1 us (3%)
    pallas_call x12, Pallas kernels, kernel_call(): pl.pallas_call(body, out_shape=out_shape, name=name, cost_estimate=pl.Cos...  127 us
    ppermute x15, waiting for transfers between devices, shift(): lax.ppermute(v, 'tensor', [(i, (i + r) % self.size) for i in range(self.s...  105 us
    ppermute x18, waiting for transfers between devices, swap(): return lax.ppermute(v, 'dp', [(i, i ^ m) for i in range(self.size)])  94.3 us
    ppermute x15, starting transfers between devices, shift(): lax.ppermute(v, 'tensor', [(i, (i + r) % self.size) for i in range(self.s...  66.1 us
    all_gather x1, waiting for transfers between devices, per_device(): grad_attn_rows = lax.all_gather(grad_low, 'tensor', axis=0, tiled=True)  36.1 us
    unnamed x83, local copies, waits for them, and re-layouts  19.6 us
    ppermute x18, starting transfers between devices, swap(): return lax.ppermute(v, 'dp', [(i, i ^ m) for i in range(self.size)])  15.2 us
    reduce_scatter x1, waiting for transfers between devices, per_device(): lax.psum_scatter(two_parts, 'tensor', scatter_dimension=0, tiled=True)  10.8 us
  transfers between devices with their start and end apart: 39, of which 22 were waited for; matrix products, arithmetic and copies ran while one was open for 3% of the time, Pallas kernels for 20%

profile of v7, /device:TPU:0, one launch (start us, length us, event | category | flops | bytes accessed | tf_op | source)
XLA Modules:
  0.0 512.0 jit_solution(14854181275068312213)
XLA Ops:
  14.8 5.0 collective-permute-start.2
  32.2 32.4 %collective-permute-done.1.refs_2_ = bf16[128,2048]{1,0:T(8,128)(2,1)S(1)} collective-permute-done((bf16[128,2048]{1,0:T(8,128)(2,1)S(1)}, bf16[128,2048]{1,0:T(8,128)(2,1)S(1)}, u32[]{:S(2)}, u32[]{:S(2)}) %collective-permute-start.1) | collective-permute-done | bytes 524320 | tf_op jit(solution)/shard_map/ppermute | solution.py:81
  67.5 15.9 %attention_forward.1 = (bf16[512,2048]{1,0:T(8,128)(2,1)}, bf16[512,768]{1,0:T(8,128)(2,1)S(1)}, bf16[512,512]{1,0:T(8,128)(2,1)S(1)}, f32[512,128]{1,0:T(8,128)S(1)}) custom-call(s32[24]{0:T(128)S(1)} %compare_select_fusion.2.ends_ref, s32[4]{0:T(128)S(1)} %compare_select_fusion.owners_ref, bf16[128,2048]{1,0:T(8,128)(2,1)S(1)} %copy-done.13, ...), custom_call_target="tpu_custom_call" | custom-call | flops 2147483648 | bytes 11542640 | tf_op jit(solution)/shard_map/attention_forward/pallas_call | solution.py:162
  84.2 3.4 attention_out.1
  91.7 3.9 collective-permute-start.14
  95.6 7.3 %collective-permute-done.7 = bf16[128,2048]{1,0:T(8,128)(2,1)S(1)} collective-permute-done((bf16[128,2048]{1,0:T(8,128)(2,1)S(1)}, bf16[128,2048]{1,0:T(8,128)(2,1)S(1)}, u32[]{:S(2)}, u32[]{:S(2)}) %collective-permute-start.7) | collective-permute-done | bytes 524320 | tf_op jit(solution)/shard_map/ppermute | solution.py:81
  102.9 23.3 %collective-permute-start.13 = (bf16[128,2048]{1,0:T(8,128)(2,1)S(1)}, bf16[128,2048]{1,0:T(8,128)(2,1)}, u32[]{:S(2)}, u32[]{:S(2)}) collective-permute-start(bf16[128,2048]{1,0:T(8,128)(2,1)S(1)} %copy-done.11), channel_id=1, source_target_pairs={{0,2},{1,3},{2,0},{3,1},{4,6},{5,7},{6,4},{7,5},{8,10},{9,11},{10,... | collective-permute-start | bytes 1572872 | tf_op jit(solution)/shard_map/ppermute | solution.py:81
  126.2 23.1 %collective-permute-done.8 = bf16[128,2048]{1,0:T(8,128)(2,1)S(1)} collective-permute-done((bf16[128,2048]{1,0:T(8,128)(2,1)S(1)}, bf16[128,2048]{1,0:T(8,128)(2,1)S(1)}, u32[]{:S(2)}, u32[]{:S(2)}) %collective-permute-start.8) | collective-permute-done | bytes 524320 | tf_op jit(solution)/shard_map/ppermute | solution.py:81
  151.9 22.8 %collective-permute-start.11 = (bf16[128,2048]{1,0:T(8,128)(2,1)S(1)}, bf16[128,2048]{1,0:T(8,128)(2,1)}, u32[]{:S(2)}, u32[]{:S(2)}) collective-permute-start(bf16[128,2048]{1,0:T(8,128)(2,1)S(1)} %multiply_convert_fusion.refs_0_), channel_id=1, source_target_pairs={{0,2},{1,3},{2,0},{3,1},{4,6},{5,7},{6,4},{7,5},{8,10},{9,11},{10,... | collective-permute-start | bytes 1572872 | tf_op jit(solution)/shard_map/ppermute | solution.py:81
  176.9 4.9 all-gather.6.cloned.1.call-done.refs_8_.refs_9_.refs_10_.refs_2_.refs_1_
  182.9 35.7 %collective-permute-done.11.refs_2_ = bf16[128,2048]{1,0:T(8,128)(2,1)} collective-permute-done((bf16[128,2048]{1,0:T(8,128)(2,1)S(1)}, bf16[128,2048]{1,0:T(8,128)(2,1)}, u32[]{:S(2)}, u32[]{:S(2)}) %collective-permute-start.11) | collective-permute-done | bytes 524320 | tf_op jit(solution)/shard_map/ppermute | solution.py:81
  218.6 21.6 %feed_forward.1 = (bf16[512,2048]{1,0:T(8,128)(2,1)}, bf16[512,2048]{1,0:T(8,128)(2,1)}, bf16[3,512,2048]{2,1,0:T(8,128)(2,1)}) custom-call(s32[4]{0:T(128)S(1)} %compare_select_fusion.owners_ref, bf16[128,2048]{1,0:T(8,128)(2,1)S(1)} %multiply_convert_fusion.refs_0_, bf16[128,2048]{1,0:T(8,128)(2,1)} %collective-permute-done.10.refs_1_, ...), custom_call_target="tpu_custom_call" | custom-call | flops 12884901888 | bytes 90177552 | tf_op jit(solution)/shard_map/feed_forward/pallas_call | solution.py:162
  240.2 13.1 %feed_forward_rows_grad.1 = bf16[512,2048]{1,0:T(8,128)(2,1)S(1)} custom-call(s32[1]{0:T(128)} %constant.43.clone.1.owners_ref, bf16[3,512,2048]{2,1,0:T(8,128)(2,1)} %get-tuple-element.168.refs_0_.refs_1_.refs_16_.refs_18_.refs_20_, bf16[3,512,2048]{2,1,0:T(8,128)(2,1)} %get-tuple-element.168.refs_0_.refs_1_.refs_16_.refs_18_.refs_20_, ...), custom_call_target="tpu_custom_call" | custom-call | flops 8589934592 | bytes 39845892 | tf_op jit(solution)/shard_map/feed_forward_rows_grad/pallas_call | solution.py:162
  262.1 24.1 %feed_forward_grad.1 = (bf16[512,3072]{1,0:T(8,128)(2,1)}, bf16[512,3072]{1,0:T(8,128)(2,1)}, bf16[512,3072]{1,0:T(8,128)(2,1)}, bf16[512,3072]{1,0:T(8,128)(2,1)}) custom-call(s32[4]{0:T(128)S(1)} %multiply_xor_fusion.places_ref, bf16[512,2048]{1,0:T(8,128)(2,1)S(1)} %copy-done.1, bf16[512,2048]{1,0:T(8,128)(2,1)S(1)} %copy-done.1, ...), custom_call_target="tpu_custom_call" | custom-call | flops 12884901888 | bytes 83886096 | tf_op jit(solution)/shard_map/feed_forward_grad/pallas_call | solution.py:162
  286.2 10.8 %reduce-scatter.4.cloned.1.call-done.grad_ref = bf16[128,2048]{1,0:T(8,128)(2,1)} async-done(((bf16[512,2048]{1,0:T(8,128)(2,1)}), bf16[128,2048]{1,0:T(8,128)(2,1)}) %reduce-scatter.4.cloned.1.call-update) | async-done | bytes 524304 | tf_op jit(solution)/shard_map/reduce_scatter | solution.py:684
  301.7 8.0 %block_out.1 = bf16[512,2048]{1,0:T(8,128)(2,1)S(1)} custom-call(s32[1]{0:T(128)} %constant.43.clone.1.owners_ref, bf16[3,512,2048]{2,1,0:T(8,128)(2,1)} %get-tuple-element.168.refs_0_.refs_1_.refs_16_.refs_18_.refs_20_, bf16[2048,6144]{1,0:T(8,128)(2,1)} %all-gather.6.cloned.1.call-done.refs_8_.refs_9_.refs_10_.refs_2_.refs_1_), custom_call_target="tpu_custom_call" | custom-call | flops 4294967296 | bytes 33554436 | tf_op jit(solution)/shard_map/block_out/pallas_call | solution.py:162
  311.0 36.1 %all-gather.8.cloned.1.call-done.grad_ref.refs_0_.refs_1_.refs_2_.refs_3_ = bf16[512,2048]{1,0:T(8,128)(2,1)} async-done(((bf16[128,2048]{1,0:T(8,128)(2,1)}), bf16[512,2048]{1,0:T(8,128)(2,1)}) %all-gather.8.cloned.1.call-update) | async-done | bytes 2097168 | tf_op jit(solution)/shard_map/all_gather | solution.py:694
  352.5 16.6 %attention_backward.1 = bf16[512,768]{1,0:T(8,128)(2,1)} custom-call(s32[24]{0:T(128)S(1)} %compare_select_fusion.2.ends_ref, bf16[512,2048]{1,0:T(8,128)(2,1)S(1)} %copy-done, bf16[2048,1280]{1,0:T(8,128)(2,1)} %all-gather.4.cloned.1.call-done.refs_5_.refs_1_.w_ref, bf16[512,768]{1,0:T(8,128)(2,1)S(1)} %copy-done.20, ...), custom_call_target="tpu_custom_call" | custom-call | flops 2415919104 | bytes 9699424 | tf_op jit(solution)/shard_map/attention_backward/pallas_call | solution.py:162
  369.7 47.8 %collective-permute-done.22.refs_1_ = bf16[512,3072]{1,0:T(8,128)(2,1)S(1)} collective-permute-done((bf16[512,3072]{1,0:T(8,128)(2,1)}, bf16[512,3072]{1,0:T(8,128)(2,1)S(1)}, u32[]{:S(2)}, u32[]{:S(2)}) %collective-permute-start.22) | collective-permute-done | bytes 3145760 | tf_op jit(solution)/shard_map/ppermute | solution.py:100
  420.9 4.1 attention_rows_grad.1
  431.8 9.1 %attention_grad.1 = (bf16[512,768]{1,0:T(8,128)(2,1)S(1)}, bf16[512,768]{1,0:T(8,128)(2,1)S(1)}, bf16[512,512]{1,0:T(8,128)(2,1)S(1)}, bf16[512,512]{1,0:T(8,128)(2,1)S(1)}) custom-call(s32[4]{0:T(128)S(1)} %multiply_xor_fusion.places_ref, bf16[512,2048]{1,0:T(8,128)(2,1)} %all-gather.8.cloned.1.call-done.grad_ref.refs_0_.refs_1_.refs_2_.refs_3_, ...), custom_call_target="tpu_custom_call" | custom-call | flops 2684354560 | bytes 38797328 | tf_op jit(solution)/shard_map/attention_grad/pallas_call | solution.py:162
  443.5 32.9 %collective-permute-done.25 = bf16[512,512]{1,0:T(8,128)(2,1)S(1)} collective-permute-done((bf16[512,512]{1,0:T(8,128)(2,1)S(1)}, bf16[512,512]{1,0:T(8,128)(2,1)S(1)}, u32[]{:S(2)}, u32[]{:S(2)}) %collective-permute-start.25) | collective-permute-done | bytes 524320 | tf_op jit(solution)/shard_map/ppermute | solution.py:100
  476.4 4.5 collective-permute-done.24
  484.1 8.4 %feed_forward_finals.1 = (f32[256,2048]{1,0:T(8,128)}, f32[256,2048]{1,0:T(8,128)}, f32[2048,256]{1,0:T(8,128)}, f32[256,128]{1,0:T(8,128)S(1)}) custom-call(bf16[512,3072]{1,0:T(8,128)(2,1)} %get-tuple-element.213.refs_0_, bf16[512,3072]{1,0:T(8,128)(2,1)} %copy-done.29, bf16[256,3072]{1,0:T(8,128)(2,1)S(1)} %collective-permute-done.28.refs_2_, ...), custom_call_target="tpu_custom_call" | custom-call | flops 6291456 | bytes 24248320 | tf_op jit(solution)/shard_map/feed_forward_finals/pallas_call | solution.py:162
  (195 shorter events, 82.1 us)
Async XLA Ops:
  7.2 59.1 %all-gather.4.cloned.1.call-start = ((), (), s32[]{:S(2)}) async-start(), calls=%async_computation.3 | async-start | bytes 5898240 | tf_op jit(solution)/shard_map/all_gather | solution.py:646
  10.4 171.3 %all-gather.6.cloned.1.call-start = ((), (), s32[]{:S(2)}) async-start(), calls=%async_computation.4 | async-start | bytes 28311552 | tf_op jit(solution)/shard_map/all_gather | solution.py:647
  13.8 283.3 %reduce-scatter.4.cloned.1.call-start = ((), (), s32[]{:S(2)}) async-start(), calls=%async_computation.5 | async-start | bytes 2621440 | tf_op jit(solution)/shard_map/reduce_scatter | solution.py:684
  19.9 44.8 %collective-permute-start.1 = (bf16[128,2048]{1,0:T(8,128)(2,1)S(1)}, bf16[128,2048]{1,0:T(8,128)(2,1)S(1)}, u32[]{:S(2)}, u32[]{:S(2)}) collective-permute-start(bf16[128,2048]{1,0:T(8,128)(2,1)S(1)} %copy-done.13), channel_id=1, source_target_pairs={{0,2},{1,3},{2,0},{3,1},{4,6},{5,7},{6,4},{7,5},{8,10},{9,11},{10,... | collective-permute-start | bytes 1572872 | tf_op jit(solution)/shard_map/ppermute | solution.py:81
  19.9 44.8 %collective-permute-start = (bf16[128,2048]{1,0:T(8,128)(2,1)S(1)}, bf16[128,2048]{1,0:T(8,128)(2,1)S(1)}, u32[]{:S(2)}, u32[]{:S(2)}) collective-permute-start(bf16[128,2048]{1,0:T(8,128)(2,1)S(1)} %copy-done.13), channel_id=1, source_target_pairs={{0,1},{1,2},{2,3},{3,0},{4,5},{5,6},{6,7},{7,4},{8,9},{9,10},{10,1... | collective-permute-start | bytes 1572872 | tf_op jit(solution)/shard_map/ppermute | solution.py:81
  84.2 90.5 %collective-permute-start.15 = (bf16[512,2048]{1,0:T(8,128)(2,1)}, bf16[512,2048]{1,0:T(8,128)(2,1)}, u32[]{:S(2)}, u32[]{:S(2)}) collective-permute-start(bf16[512,2048]{1,0:T(8,128)(2,1)} %get-tuple-element.189.refs_8_.refs_9_.refs_10_.refs_11_), channel_id=1, source_target_pairs={{0,4},{4,0},{8,12},{12,8},{16,20},{20,16},{24,28},{28,24},{1,5},{5... | collective-permute-start | bytes 6291464 | tf_op jit(solution)/shard_map/ppermute | solution.py:100
  90.5 58.8 %collective-permute-start.8 = (bf16[128,2048]{1,0:T(8,128)(2,1)S(1)}, bf16[128,2048]{1,0:T(8,128)(2,1)S(1)}, u32[]{:S(2)}, u32[]{:S(2)}) collective-permute-start(bf16[128,2048]{1,0:T(8,128)(2,1)S(1)} %get-tuple-element.134), channel_id=1, source_target_pairs={{0,2},{1,3},{2,0},{3,1},{4,6},{5,7},{6,4},{7,5},{8,10},{9,11},{10,... | collective-permute-start | bytes 1572872 | tf_op jit(solution)/shard_map/ppermute | solution.py:81
  91.6 57.6 %collective-permute-start.9 = (bf16[128,2048]{1,0:T(8,128)(2,1)S(1)}, bf16[128,2048]{1,0:T(8,128)(2,1)S(1)}, u32[]{:S(2)}, u32[]{:S(2)}) collective-permute-start(bf16[128,2048]{1,0:T(8,128)(2,1)S(1)} %get-tuple-element.135), channel_id=1, source_target_pairs={{0,1},{1,2},{2,3},{3,0},{4,5},{5,6},{6,7},{7,4},{8,9},{9,10},{10,1... | collective-permute-start | bytes 1572872 | tf_op jit(solution)/shard_map/ppermute | solution.py:81
  91.7 90.0 %collective-permute-start.14 = (bf16[128,2048]{1,0:T(8,128)(2,1)S(1)}, bf16[128,2048]{1,0:T(8,128)(2,1)S(1)}, u32[]{:S(2)}, u32[]{:S(2)}) collective-permute-start(bf16[128,2048]{1,0:T(8,128)(2,1)S(1)} %copy-done.11), channel_id=1, source_target_pairs={{0,3},{1,0},{2,1},{3,2},{4,7},{5,4},{6,5},{7,6},{8,11},{9,8},{10,9... | collective-permute-start | bytes 1572872 | tf_op jit(solution)/shard_map/ppermute | solution.py:81
  102.9 78.8 %collective-permute-start.13 = (bf16[128,2048]{1,0:T(8,128)(2,1)S(1)}, bf16[128,2048]{1,0:T(8,128)(2,1)}, u32[]{:S(2)}, u32[]{:S(2)}) collective-permute-start(bf16[128,2048]{1,0:T(8,128)(2,1)S(1)} %copy-done.11), channel_id=1, source_target_pairs={{0,2},{1,3},{2,0},{3,1},{4,6},{5,7},{6,4},{7,5},{8,10},{9,11},{10,... | collective-permute-start | bytes 1572872 | tf_op jit(solution)/shard_map/ppermute | solution.py:81
  149.9 33.0 %collective-permute-start.12 = (bf16[128,2048]{1,0:T(8,128)(2,1)S(1)}, bf16[128,2048]{1,0:T(8,128)(2,1)}, u32[]{:S(2)}, u32[]{:S(2)}) collective-permute-start(bf16[128,2048]{1,0:T(8,128)(2,1)S(1)} %multiply_convert_fusion.refs_0_), channel_id=1, source_target_pairs={{0,3},{1,0},{2,1},{3,2},{4,7},{5,4},{6,5},{7,6},{8,11},{9,8},{10,9... | collective-permute-start | bytes 1572872 | tf_op jit(solution)/shard_map/ppermute | solution.py:81
  151.9 66.7 %collective-permute-start.11 = (bf16[128,2048]{1,0:T(8,128)(2,1)S(1)}, bf16[128,2048]{1,0:T(8,128)(2,1)}, u32[]{:S(2)}, u32[]{:S(2)}) collective-permute-start(bf16[128,2048]{1,0:T(8,128)(2,1)S(1)} %multiply_convert_fusion.refs_0_), channel_id=1, source_target_pairs={{0,2},{1,3},{2,0},{3,1},{4,6},{5,7},{6,4},{7,5},{8,10},{9,11},{10,... | collective-permute-start | bytes 1572872 | tf_op jit(solution)/shard_map/ppermute | solution.py:81
  174.7 43.9 %collective-permute-start.10 = (bf16[128,2048]{1,0:T(8,128)(2,1)S(1)}, bf16[128,2048]{1,0:T(8,128)(2,1)}, u32[]{:S(2)}, u32[]{:S(2)}) collective-permute-start(bf16[128,2048]{1,0:T(8,128)(2,1)S(1)} %multiply_convert_fusion.refs_0_), channel_id=1, source_target_pairs={{0,1},{1,2},{2,3},{3,0},{4,5},{5,6},{6,7},{7,4},{8,9},{9,10},{10,1... | collective-permute-start | bytes 1572872 | tf_op jit(solution)/shard_map/ppermute | solution.py:81
  254.7 92.3 %all-gather.8.cloned.1.call-start = ((), (), s32[]{:S(2)}) async-start(), calls=%async_computation.6 | async-start | bytes 2621440 | tf_op jit(solution)/shard_map/all_gather | solution.py:694
  301.6 124.7 %reduce-scatter.6.cloned.1.call-start = ((), (), s32[]{:S(2)}) async-start(), calls=%async_computation.7 | async-start | bytes 2621440 | tf_op jit(solution)/shard_map/reduce_scatter | solution.py:697
  347.1 155.3 %reduce-scatter.8.cloned.1.call-start = ((), (), s32[]{:S(2)}) async-start(), calls=%async_computation.8 | async-start | bytes 2621440 | tf_op jit(solution)/shard_map/reduce_scatter | solution.py:707
  347.3 70.1 %collective-permute-start.22 = (bf16[512,3072]{1,0:T(8,128)(2,1)}, bf16[512,3072]{1,0:T(8,128)(2,1)S(1)}, u32[]{:S(2)}, u32[]{:S(2)}) collective-permute-start(bf16[512,3072]{1,0:T(8,128)(2,1)} %get-tuple-element.180), channel_id=1, source_target_pairs={{0,16},{4,20},{8,24},{12,28},{16,0},{20,4},{24,8},{28,12},{1,17},{... | collective-permute-start | bytes 9437192 | tf_op jit(solution)/shard_map/ppermute | solution.py:100
  348.9 69.8 %collective-permute-start.23 = (bf16[512,3072]{1,0:T(8,128)(2,1)}, bf16[512,3072]{1,0:T(8,128)(2,1)S(1)}, u32[]{:S(2)}, u32[]{:S(2)}) collective-permute-start(bf16[512,3072]{1,0:T(8,128)(2,1)} %get-tuple-element.182), channel_id=1, source_target_pairs={{0,8},{4,12},{8,0},{12,4},{16,24},{20,28},{24,16},{28,20},{1,9},{5... | collective-permute-start | bytes 9437192 | tf_op jit(solution)/shard_map/ppermute | solution.py:100
  350.3 81.4 %collective-permute-start.20 = (bf16[512,2048]{1,0:T(8,128)(2,1)S(1)}, bf16[512,2048]{1,0:T(8,128)(2,1)}, u32[]{:S(2)}, u32[]{:S(2)}) collective-permute-start(bf16[512,2048]{1,0:T(8,128)(2,1)S(1)} %copy-done), channel_id=1, source_target_pairs={{0,4},{4,0},{8,12},{12,8},{16,20},{20,16},{24,28},{28,24},{1,5},{5... | collective-permute-start | bytes 6291464 | tf_op jit(solution)/shard_map/ppermute | solution.py:100
  369.1 62.7 %collective-permute-start.21 = (bf16[512,768]{1,0:T(8,128)(2,1)}, bf16[512,768]{1,0:T(8,128)(2,1)}, u32[]{:S(2)}, u32[]{:S(2)}) collective-permute-start(bf16[512,768]{1,0:T(8,128)(2,1)} %attention_backward.1), channel_id=1, source_target_pairs={{0,4},{4,0},{8,12},{12,8},{16,20},{20,16},{24,28},{28,24},{1,5},{5... | collective-permute-start | bytes 2359304 | tf_op jit(solution)/shard_map/ppermute | solution.py:100
  429.0 55.1 %collective-permute-start.29 = (bf16[256,3072]{1,0:T(8,128)(2,1)S(1)}, bf16[256,3072]{1,0:T(8,128)(2,1)S(1)}, u32[]{:S(2)}, u32[]{:S(2)}) collective-permute-start(bf16[256,3072]{1,0:T(8,128)(2,1)S(1)} %add_convert_fusion), channel_id=1, source_target_pairs={{0,16},{4,20},{8,24},{12,28},{16,0},{20,4},{24,8},{28,12},{1,17},{... | collective-permute-start | bytes 4718600 | tf_op jit(solution)/shard_map/ppermute | solution.py:100
  430.3 53.8 %collective-permute-start.28 = (bf16[256,3072]{1,0:T(8,128)(2,1)S(1)}, bf16[256,3072]{1,0:T(8,128)(2,1)S(1)}, u32[]{:S(2)}, u32[]{:S(2)}) collective-permute-start(bf16[256,3072]{1,0:T(8,128)(2,1)S(1)} %copy-done.31), channel_id=1, source_target_pairs={{0,8},{4,12},{8,0},{12,4},{16,24},{20,28},{24,16},{28,20},{1,9},{5... | collective-permute-start | bytes 4718600 | tf_op jit(solution)/shard_map/ppermute | solution.py:100
  440.9 40.0 %collective-permute-start.24 = (bf16[512,768]{1,0:T(8,128)(2,1)S(1)}, bf16[512,768]{1,0:T(8,128)(2,1)S(1)}, u32[]{:S(2)}, u32[]{:S(2)}) collective-permute-start(bf16[512,768]{1,0:T(8,128)(2,1)S(1)} %get-tuple-element.204), channel_id=1, source_target_pairs={{0,16},{4,20},{8,24},{12,28},{16,0},{20,4},{24,8},{28,12},{1,17},{... | collective-permute-start | bytes 2359304 | tf_op jit(solution)/shard_map/ppermute | solution.py:100
  441.8 34.6 %collective-permute-start.25 = (bf16[512,512]{1,0:T(8,128)(2,1)S(1)}, bf16[512,512]{1,0:T(8,128)(2,1)S(1)}, u32[]{:S(2)}, u32[]{:S(2)}) collective-permute-start(bf16[512,512]{1,0:T(8,128)(2,1)S(1)} %get-tuple-element.206), channel_id=1, source_target_pairs={{0,8},{4,12},{8,0},{12,4},{16,24},{20,28},{24,16},{28,20},{1,9},{5... | collective-permute-start | bytes 1572872 | tf_op jit(solution)/shard_map/ppermute | solution.py:100
  (55 other events, 582.3 us)
Sparse Core Ops, SparseCore 0:
  10.5 43.8 all-gather.3
  56.4 125.3 all-gather.5
  254.9 42.1 reduce-scatter.3
  301.7 45.2 all-gather.7
  349.9 42.5 reduce-scatter.5
  426.5 42.5 reduce-scatter.7
